TPU v7x, 128 devices: a whole 4x4x4 slice. The times are simulated.
128 devices in a mesh: section: 16 (over z, x), tensor: 8 (over y, core).
Axes of the slice: x: 4, y: 4, z: 4, core: 2. Of those that a mesh axis runs over, the one named last changes fastest.
Arguments:
- prompt_rows: bfloat16 [32768, 8192], P('section'), may hold values from -10 to 10
- page_slot: int32 [16, 16, 8], P('section'), may hold values from -1 to 63, as said below
- context_len: int32 [128], P('section'), may hold values from 1 to 128, as said below
- new_tokens: bfloat16 [2, 128, 8192], P(None, None, 'section'), may hold values from -26 to 26
- norm_gain: float32 [8192], replicated, may hold values from 0.25 to 1.75
- q_weight: bfloat16 [8192, 8192], P('section', 'tensor'), may hold values from -1 to 1
- kv_weight: bfloat16 [8192, 2048], P('section', 'tensor'), may hold values from -1 to 1
- o_weight: bfloat16 [8192, 8192], P('tensor', 'section'), may hold values from -0.0625 to 0.0625
Outputs:
- layer_out: bfloat16 [2, 128, 8192], P(None, 'tensor', 'section')
Inputs may be any that keep to these rules, and one draw needn't show every extreme that they name: page_slot[s, g, c] = j * 8 + p says that slot c of section s holds page p of sequence j of decode group g; -1 marks an empty slot. Each of the 64 pages of every group sits in exactly one slot, and for every group some section fills all 8 of its slots. `context_len`: in every group of 8 sequences one sequence has the full 8 * 16 tokens.
All inputs are finite; a program needn't handle non-finite values.
Results may differ from a plain program's by a relative error of at most 0.0051.
Values may be sent and summed in bfloat16 or wider, within the bound.
No kernel may reach another device: no remote copies, remote signals or barrier semaphores. Data moves between devices by JAX's collectives and lax.ppermute only.
A program may use at most 128 MiB of HBM per device.

v0:
```python
import math

import jax
import jax.numpy as jnp
from jax import lax
from jax.sharding import PartitionSpec as P

D = 8192
HD = 128
GQ = 8
PAGE = 16
CAP = 8
SEQ_G = 8


EPS = 1e-05
ROPE_BASE = 500000.0


def rotate(vectors, positions):
    half_dim = vectors.shape[-1] // 2
    frequency = ROPE_BASE ** (-2.0 * jnp.arange(half_dim, dtype=jnp.float32) / vectors.shape[-1])
    angles = positions.astype(jnp.float32)[..., None, None] * frequency
    first = vectors[..., :half_dim]
    second = vectors[..., half_dim:]
    cosine = jnp.cos(angles)
    sine_term = jnp.sin(angles)
    return jnp.concatenate(
        [first * cosine - second * sine_term, second * cosine + first * sine_term], axis=-1
    )


def attend(queries, new_keys, new_values, keys, values, slot_ids, lengths, pages_seq):
    count = queries.shape[1]
    scale = 1.0 / math.sqrt(queries.shape[-1])
    offsets = jnp.arange(PAGE, dtype=jnp.int32)
    shape = slot_ids.shape + (PAGE,)
    seq_tok = jnp.broadcast_to((slot_ids // pages_seq)[..., None], shape).reshape(-1)
    pos_tok = ((slot_ids % pages_seq)[..., None] * PAGE + offsets).reshape(-1)
    valid = jnp.broadcast_to((slot_ids >= 0)[..., None], shape).reshape(-1)
    scores = (
        jnp.einsum("isjgh,ljh->isjgl", queries, keys, preferred_element_type=jnp.float32) * scale
    )
    new_scores = (
        jnp.einsum("isjgh,tsjh->isjgt", queries, new_keys, preferred_element_type=jnp.float32)
        * scale
    )
    owners = jnp.arange(count, dtype=jnp.int32)
    cache_mask = (
        valid[None, :]
        & (seq_tok[None, :] == owners[:, None])
        & (pos_tok[None, :] < lengths[:, None])
    )[None, :, None, None, :]
    steps = jnp.arange(2, dtype=jnp.int32)
    step_mask = (steps[None, :] <= steps[:, None])[:, None, None, None, :]
    highest = jnp.maximum(
        jnp.max(jnp.where(cache_mask, scores, -jnp.inf), axis=-1),
        jnp.max(jnp.where(step_mask, new_scores, -jnp.inf), axis=-1),
    )[..., None]
    cache_exp = jnp.where(cache_mask, jnp.exp(scores - highest), 0.0)
    step_exp = jnp.where(step_mask, jnp.exp(new_scores - highest), 0.0)
    denom_sum = jnp.sum(cache_exp, axis=-1, keepdims=True) + jnp.sum(
        step_exp, axis=-1, keepdims=True
    )
    cache_weight = (cache_exp / denom_sum).astype(jnp.bfloat16)
    step_weight = (step_exp / denom_sum).astype(jnp.bfloat16)
    mixed = jnp.einsum("isjgl,ljh->isjgh", cache_weight, values, preferred_element_type=jnp.float32)
    mixed = mixed + jnp.einsum(
        "isjgt,tsjh->isjgh", step_weight, new_values, preferred_element_type=jnp.float32
    )
    return mixed.reshape(2, count, -1).astype(jnp.bfloat16)


def on_device(
    prompt_rows, page_slot, context_len, new_tokens, norm_gain, q_weight, kv_weight, o_weight
):
    sections = lax.axis_size("section")
    tensors = lax.axis_size("tensor")
    section_pos = lax.axis_index("section")
    member = lax.axis_index("tensor")
    width_kv = kv_weight.shape[1]
    heads_kv = width_kv // (2 * HD)
    heads_q = q_weight.shape[1] // HD
    pages_seq = sections * CAP // (2 * SEQ_G)
    prompt_f32 = prompt_rows.astype(jnp.float32)
    normed = (
        prompt_f32
        * lax.rsqrt(jnp.mean(prompt_f32 * prompt_f32, axis=-1, keepdims=True) + EPS)
        * norm_gain
    ).astype(jnp.bfloat16)
    prompt_kv = jnp.dot(
        normed,
        lax.all_gather(kv_weight, "section", axis=0, tiled=True),
        preferred_element_type=jnp.float32,
    )
    prompt_kv = prompt_kv.reshape(sections, CAP, PAGE, heads_kv, 2, HD)
    own_ids = page_slot[0]
    positions = (jnp.maximum(own_ids, 0) % pages_seq)[..., None] * PAGE + jnp.arange(
        PAGE, dtype=jnp.int32
    )
    cache_keys = rotate(prompt_kv[..., 0, :], positions).astype(jnp.bfloat16)
    cache_values = prompt_kv[..., 1, :].astype(jnp.bfloat16)
    pages = jnp.stack([cache_keys, cache_values], axis=-2).reshape(sections, CAP * PAGE, width_kv)
    received, got_ids = (
        lax.all_to_all(pages, "section", split_axis=0, concat_axis=0, tiled=True),
        lax.all_to_all(own_ids, "section", split_axis=0, concat_axis=0, tiled=True),
    )
    received = received.reshape(sections * CAP * PAGE, heads_kv, 2, HD)
    keys_here = received[:, :, 0, :]
    values_here = received[:, :, 1, :]
    token_f32 = new_tokens.astype(jnp.float32)
    width_dev = token_f32.shape[2]
    gain_here = lax.dynamic_slice_in_dim(norm_gain, section_pos * width_dev, width_dev, 0)
    scaled = (token_f32 * gain_here).astype(jnp.bfloat16)
    squares = jnp.sum(token_f32 * token_f32, axis=-1)
    query_part = jnp.einsum("ibd,dc->ibc", scaled, q_weight, preferred_element_type=jnp.float32)
    kv_part = jnp.einsum("ibd,dc->ibc", scaled, kv_weight, preferred_element_type=jnp.float32)

    def group_rows(whole):
        return lax.dynamic_slice_in_dim(whole, section_pos * SEQ_G, SEQ_G, 1)

    query_part, kv_part, squares = lax.psum((query_part, kv_part, squares), "section")
    query_part = group_rows(query_part)
    kv_part = group_rows(kv_part)
    squares = group_rows(squares)
    rscale = lax.rsqrt(squares / D + EPS)[..., None]
    new_positions = context_len[None, :] + jnp.arange(2, dtype=jnp.int32)[:, None]
    queries = rotate((query_part * rscale).reshape(2, SEQ_G, heads_q, HD), new_positions).astype(
        jnp.bfloat16
    )
    queries = queries.reshape(2, SEQ_G, heads_kv, GQ, HD)
    kv_scaled = (kv_part * rscale).reshape(2, SEQ_G, heads_kv, 2, HD)
    new_keys = rotate(kv_scaled[..., 0, :], new_positions).astype(jnp.bfloat16)
    new_values = kv_scaled[..., 1, :].astype(jnp.bfloat16)
    attn = attend(
        queries, new_keys, new_values, keys_here, values_here, got_ids, context_len, pages_seq
    )
    partial_out = jnp.einsum(
        "isc,cd->isd",
        lax.all_gather(attn, "section", axis=1, tiled=True),
        o_weight,
        preferred_element_type=jnp.float32,
    )
    rows_dev = partial_out.shape[1] // tensors
    summed = lax.psum(partial_out, "tensor")
    summed = lax.dynamic_slice_in_dim(summed, member * rows_dev, rows_dev, 1)
    residual = lax.dynamic_slice_in_dim(token_f32, member * rows_dev, rows_dev, 1)
    return (residual + summed).astype(jnp.bfloat16)


def solution(mesh):
    placed = (
        P("section", None),
        P("section", None, None),
        P("section"),
        P(None, None, "section"),
        P(),
        P("section", "tensor"),
        P("section", "tensor"),
        P("tensor", "section"),
    )
    return jax.shard_map(
        on_device,
        mesh=mesh,
        in_specs=placed,
        out_specs=P(None, "tensor", "section"),
        check_vma=False,
    )
```

profile of v0, /device:TPU:0, one launch (start us, length us, event | category | flops | bytes accessed | tf_op | source)
XLA Modules:
  0.0 304.8 jit_solution(2507045077682214064)
XLA Ops:
  6.6 0.8 dynamic_slice.19
  7.8 2.4 fusion.21
  10.1 2.0 fusion.30
  12.9 1.4 copy.87
  14.3 8.0 %all-to-all-start.1 = ((s32[16,1,8]{2,1,0:T(1,128)}), s32[16,1,8]{2,1,0:T(1,128)S(1)}, u32[]{:S(2)}, u32[]{:S(2)}) async-start(s32[16,1,8]{2,1,0:T(1,128)} %copy.87), calls=%async_computation.1 | async-start | bytes 16384 | tf_op jit(solution)/shard_map/all_to_all | solution.py:106
  23.8 1.1 multiply_reduce_fusion
  24.9 40.7 %psum.29 = f32[2,128]{1,0:T(2,128)S(1)} all-reduce(f32[2,128]{1,0:T(2,128)S(1)} %multiply_reduce_fusion), channel_id=1, replica_groups=mesh['section'=16,'tensor'=8] {'section'}, use_global_device_ids=true, to_apply=%region_3.4 | all-reduce | flops 256 | bytes 2048 | tf_op jit(solution)/shard_map/psum | solution.py:122
  65.7 11.4 %fusion = f32[2048]{0:T(1024)S(1)} fusion(bf16[2048,8192]{1,0:T(8,128)(2,1)} %param.8), kind=kLoop, calls=%fused_computation.2 | loop fusion | flops 50329600 | bytes 33562624 | tf_op jit(solution)/shard_map/reduce_sum | solution.py:88
  78.3 24.6 %all-reduce.6.cloned.1.call-done = (f32[2,128,1024]{2,1,0:T(8,128)}, f32[2,128,256]{2,1,0:T(8,128)}) async-done(((f32[2,128,1024]{2,1,0:T(8,128)}, f32[2,128,256]{2,1,0:T(8,128)}), (f32[2,128,1024]{2,1,0:T(8,128)}, f32[2,128,256]{2,1,0:T(8,128)})) %all-reduce.6.cloned.1.call-update) | async-done | bytes 1310736 | tf_op jit(solution)/shard_map/psum | solution.py:122
  103.7 52.2 %all-gather.2.cloned.1.call-done = bf16[8192,256]{1,0:T(8,128)(2,1)} async-done(((bf16[512,256]{1,0:T(8,128)(2,1)}), bf16[8192,256]{1,0:T(8,128)(2,1)}) %all-gather.2.cloned.1.call-update) | async-done | bytes 4194320 | tf_op jit(solution)/shard_map/all_gather | solution.py:93
  155.9 17.3 %fusion.3 = f32[2048,256]{1,0:T(8,128)} fusion(bf16[8192,256]{1,0:T(8,128)(2,1)} %all-gather.2.cloned.1.call-done, bf16[2048,8192]{1,0:T(8,128)(2,1)} %param.8, f32[8192]{0:T(1024)S(1)} %copy-done.3, f32[2048]{0:T(1024)S(1)} %add_rsqrt_fusion), kind=kOutput, calls=%fused_computation.5 | convolution fusion | flops 8657043456 | bytes 39886848 | tf_op jit(solution)/shard_map/dot_general | solution.py:91
  173.2 2.3 reshape.396
  175.6 1.1 slice.53
  177.7 4.7 %fusion.28 = (bf16[16,8,16,1,1,64]{5,2,1,0,4,3:T(8,128)(2,1)S(1)}, bf16[16,8,16,1,1,64]{5,2,1,0,4,3:T(8,128)(2,1)S(1)}) fusion(f32[16,8,16,1,128]{4,2,1,0,3:T(8,128)S(1)} %bitcast.129, f32[64]{0:T(128)S(1)} %multiply_power_fusion, f32[16,8,16]{2,1,0:T(8,128)S(1)} %add_convert_fusion.2), kind=kLoop, calls=%fused_computation.45 | loop fusion | flops 1179648 | bytes 1581312 | tf_op jit(solution)/shard_map/concatenate | solution.py:28
  182.7 1.6 copy.84
  184.4 1.5 reshape.397
  185.8 5.3 %all-to-all-start = ((bf16[16,128,256]{2,1,0:T(8,128)(2,1)}), bf16[16,128,256]{2,1,0:T(8,128)(2,1)S(1)}, u32[]{:S(2)}, u32[]{:S(2)}) async-start(bf16[16,128,256]{2,1,0:T(8,128)(2,1)} %reshape.397), calls=%async_computation | async-start | bytes 2097152 | tf_op jit(solution)/shard_map/all_to_all | solution.py:105
  191.5 0.9 multiply_bitcast_fusion
  192.9 15.8 %all-to-all-done = bf16[16,128,256]{2,1,0:T(8,128)(2,1)S(1)} async-done(((bf16[16,128,256]{2,1,0:T(8,128)(2,1)}), bf16[16,128,256]{2,1,0:T(8,128)(2,1)S(1)}, u32[]{:S(2)}, u32[]{:S(2)}) %all-to-all-start) | async-done | bytes 1048608 | tf_op jit(solution)/shard_map/all_to_all | solution.py:105
  209.0 1.5 fusion.61
  212.3 21.5 %all_gather.7 = bf16[2,128,1024]{2,1,0:T(8,128)(2,1)S(1)} all-gather(bf16[2,8,1024]{2,1,0:T(8,128)(2,1)S(1)} %convert_element_type.81), channel_id=1, replica_groups=mesh['section'=16,'tensor'=8] {'section'}, dimensions={1}, use_global_device_ids=true | all-gather | bytes 557056 | tf_op jit(solution)/shard_map/all_gather | solution.py:140
  233.8 2.5 fusion.19
  236.3 60.5 %all-reduce.4.cloned.1.call-done = f32[2,128,512]{2,1,0:T(8,128)} async-done(((f32[2,128,512]{2,1,0:T(8,128)}), f32[2,128,512]{2,1,0:T(8,128)}) %all-reduce.4.cloned.1.call-update) | async-done | bytes 524304 | tf_op jit(solution)/shard_map/psum | solution.py:145
  296.8 1.5 add_convert_fusion
  (62 shorter events, 9.0 us)
Async XLA Ops:
  6.5 1.3 copy-start
  6.5 149.4 %copy-start.3 = (f32[8192]{0:T(1024)S(1)}, f32[8192]{0:T(1024)}, u32[]{:S(2)}) copy-start(f32[8192]{0:T(1024)} %param.12) | copy-start | bytes 98308
  6.5 71.7 %copy-start.2 = (s32[8]{0:T(128)S(1)}, s32[8]{0:T(128)}, u32[]{:S(2)}) copy-start(s32[8]{0:T(128)} %param.10) | copy-start | bytes 100
  6.5 96.3 %all-reduce.6.cloned.1.call-start = ((), (), s32[]{:S(2)}) async-start(), calls=%async_computation.4 | async-start | bytes 2621440 | tf_op jit(solution)/shard_map/psum | solution.py:122
  12.2 143.8 %all-gather.2.cloned.1.call-start = ((), (), s32[]{:S(2)}) async-start(), calls=%async_computation.2 | async-start | bytes 4456448 | tf_op jit(solution)/shard_map/all_gather | solution.py:93
  14.3 63.1 %all-to-all-start.1 = ((s32[16,1,8]{2,1,0:T(1,128)}), s32[16,1,8]{2,1,0:T(1,128)S(1)}, u32[]{:S(2)}, u32[]{:S(2)}) async-start(s32[16,1,8]{2,1,0:T(1,128)} %copy.87), calls=%async_computation.1 | async-start | bytes 16384 | tf_op jit(solution)/shard_map/all_to_all | solution.py:106
  173.2 63.0 %copy-start.1 = (bf16[2,128,512]{2,1,0:T(8,128)(2,1)S(1)}, bf16[2,128,512]{2,1,0:T(8,128)(2,1)}, u32[]{:S(2)}) copy-start(bf16[2,128,512]{2,1,0:T(8,128)(2,1)} %param.11) | copy-start | bytes 786436
  185.8 22.9 %all-to-all-start = ((bf16[16,128,256]{2,1,0:T(8,128)(2,1)}), bf16[16,128,256]{2,1,0:T(8,128)(2,1)S(1)}, u32[]{:S(2)}, u32[]{:S(2)}) async-start(bf16[16,128,256]{2,1,0:T(8,128)(2,1)} %reshape.397), calls=%async_computation | async-start | bytes 2097152 | tf_op jit(solution)/shard_map/all_to_all | solution.py:105
  191.1 105.7 %all-reduce.4.cloned.1.call-start = ((), (), s32[]{:S(2)}) async-start(), calls=%async_computation.3 | async-start | bytes 1048576 | tf_op jit(solution)/shard_map/psum | solution.py:145
Sparse Core Ops, SparseCore 0:
  12.3 90.5 all-reduce.5
  105.0 50.8 all-gather.1
  236.4 60.3 all-reduce.3
where the time goes:
time: 305 us
  waiting for transfers between devices  154 us (50%)
  blocking collectives  62.2 us (20%)
  matrix products  25.6 us (8%)
  other arithmetic  23.4 us (8%)
  starting transfers between devices  13.5 us (4%)
  between operations  13.4 us (4%)
  local copies, waits for them, and re-layouts  12.9 us (4%)
    psum x1, waiting for transfers between devices, on_device(): summed = lax.psum(partial_out, 'tensor')  60.5 us
    all_gather x1, waiting for transfers between devices, on_device(): lax.all_gather(kv_weight, 'section', axis=0, tiled=True)  52.2 us
    psum x1, blocking collectives, on_device(): lax.psum((query_part, kv_part, squares), 'section')  40.7 us
    psum x1, waiting for transfers between devices, on_device(): lax.psum((query_part, kv_part, squares), 'section')  24.6 us
    all_gather x1, blocking collectives, on_device(): lax.all_gather(attn, 'section', axis=1, tiled=True)  21.5 us
    dot_general x1, matrix products, on_device(): jnp.dot(normed, lax.all_gather(kv_weight, 'section', axis=0, tiled=True),...  17.3 us
    all_to_all x1, waiting for transfers between devices, on_device(): lax.all_to_all(pages, 'section', split_axis=0, concat_axis=0, tiled=True)  15.8 us
    reduce_sum x1, other arithmetic, on_device(): jnp.mean(prompt_f32 * prompt_f32, axis=-1, keepdims=True) + EPS  11.4 us
  transfers between devices with their start and end apart: 5, of which 4 were waited for; matrix products, arithmetic and copies ran while one was open for 6% of the time, Pallas kernels for 0%

commit v1 on v0

v1 whole, which is shorter than its diff:
```python
import functools
import math

import jax
import jax.numpy as jnp
from jax import lax
from jax.experimental import pallas as pl
from jax.experimental.pallas import tpu as pltpu
from jax.sharding import PartitionSpec as P

D = 8192
HD = 128
GQ = 8
PAGE = 16
CAP = 8
SEQ_G = 8
SECTIONS = 16
GROUP_TOK = CAP * PAGE
ROWS = 2 * SEQ_G
DEPTH = D // SECTIONS
WQ = GQ * HD
WKV = 2 * HD
EXTRA = 128
ID_LANE = 8
POSITIONS = 136

EPS = 1e-05
ROPE_BASE = 500000.0
BF16 = jnp.bfloat16
F32 = jnp.float32
VMEM_LIMIT = 40 * 1024 * 1024


def params(**more):
    return pltpu.CompilerParams(vmem_limit_bytes=VMEM_LIMIT, **more)


def rotation_tables():
    half = HD // 2
    frequency = ROPE_BASE ** (-2.0 * jnp.arange(half, dtype=F32) / HD)
    angles = jnp.arange(POSITIONS, dtype=jnp.int32).astype(F32)[:, None] * frequency
    cosine, sine = jnp.cos(angles), jnp.sin(angles)
    return (
        jnp.concatenate([cosine, cosine], axis=-1),
        jnp.concatenate([-sine, sine], axis=-1),
    )


def turned(rows, cosine, sine):
    return rows * cosine + pltpu.roll(rows, HD // 2, 1) * sine


def shifted(array, axis, step):
    pairs = []
    for z in range(4):
        for x in range(4):
            for member in range(8):
                along_x = (axis + member) % 2 == 0
                to_z = z if along_x else (z + step) % 4
                to_x = (x + step) % 4 if along_x else x
                pairs.append(((z * 4 + x) * 8 + member, (to_z * 4 + to_x) * 8 + member))
    return lax.ppermute(array, ("section", "tensor"), pairs)


def prompt_kernel(first, last, *refs):
    if last:
        _, ids_ref, *refs = refs
    else:
        _, *refs = refs
    x_refs, refs = refs[:4], refs[4:]
    wa_ref, wb_ref, *refs = refs
    if not first:
        acc_ref, squares_ref, *refs = refs
    if last:
        cos_ref, sin_ref, pages_ref = refs
    else:
        acc_out, squares_out = refs

    total, squares = None, None
    for k, x_ref in enumerate(x_refs):
        x = x_ref[...]
        w_ref = (wa_ref, wb_ref)[k // 2]
        w = w_ref[(k % 2) * DEPTH : (k % 2 + 1) * DEPTH, :]
        part = jnp.dot(x, w, preferred_element_type=F32)
        total = part if total is None else total + part
        wide = x.astype(F32)
        wide = wide * wide
        for c in range(DEPTH // 128):
            piece = wide[:, c * 128 : (c + 1) * 128]
            squares = piece if squares is None else squares + piece
    if not first:
        total = total + acc_ref[...]
        squares = squares + squares_ref[...]
    if not last:
        acc_out[...] = total
        squares_out[...] = squares
        return
    mean = jnp.sum(squares, axis=-1, keepdims=True) * (1.0 / D)
    total = total * lax.rsqrt(mean + EPS)
    groups = total.shape[0] // GROUP_TOK
    for g in range(groups):
        group = pl.program_id(0) * groups + g
        for c in range(CAP):
            row = g * GROUP_TOK + c * PAGE
            page = jnp.maximum(ids_ref[group, c], 0) % CAP
            at = pl.ds(pl.multiple_of(page * PAGE, PAGE), PAGE)
            key = turned(total[row : row + PAGE, :HD], cos_ref[at, :], sin_ref[at, :])
            pages_ref[g, c * PAGE : (c + 1) * PAGE, :HD] = key.astype(BF16)
        pages_ref[g, :, HD:] = total[g * GROUP_TOK : (g + 1) * GROUP_TOK, HD:].astype(BF16)


def prompt_pass(x, blocks, wa, wb, carry=None, final=None):
    first, last = carry is None, final is not None
    rows = x.shape[0]
    step = 512
    n_scalars = 2 if last else 1

    def x_at(k):
        return pl.BlockSpec((step, DEPTH), lambda r, blocks, *_: (r, blocks[k]))

    whole_w = pl.BlockSpec((2 * DEPTH, WKV), lambda r, *_: (0, 0))
    acc_spec = pl.BlockSpec((step, WKV), lambda r, *_: (r, 0))
    sq_spec = pl.BlockSpec((step, 128), lambda r, *_: (r, 0))
    in_specs = [x_at(k) for k in range(4)] + [whole_w, whole_w]
    args = [x] * 4 + [wa, wb]
    if not first:
        in_specs += [acc_spec, sq_spec]
        args += list(carry)
    scalars = [blocks]
    if last:
        ids, cosine, sine = final
        scalars.append(ids)
        table = pl.BlockSpec((POSITIONS, HD), lambda r, *_: (0, 0))
        in_specs += [table, table]
        args += [cosine, sine]
        groups = step // GROUP_TOK
        out_specs = pl.BlockSpec((groups, GROUP_TOK, WKV), lambda r, *_: (r, 0, 0))
        out_shape = jax.ShapeDtypeStruct((rows // GROUP_TOK, GROUP_TOK, WKV), BF16)
    else:
        out_specs = [acc_spec, sq_spec]
        out_shape = [
            jax.ShapeDtypeStruct((rows, WKV), F32),
            jax.ShapeDtypeStruct((rows, 128), F32),
        ]
    return pl.pallas_call(
        functools.partial(prompt_kernel, first, last),
        grid_spec=pltpu.PrefetchScalarGridSpec(
            num_scalar_prefetch=n_scalars,
            grid=(rows // step,),
            in_specs=in_specs,
            out_specs=out_specs,
        ),
        out_shape=out_shape,
        compiler_params=params(),
        name="prompt_last" if last else "prompt_first" if first else "prompt_middle",
    )(*scalars, *args)


def project_kernel(tok_ref, gain_ref, qw_ref, kvw_ref, ids_ref, out_ref):
    tok = tok_ref[...].astype(F32)
    scaled = (tok * gain_ref[...]).astype(BF16)
    squares = jnp.sum(tok * tok, axis=-1, keepdims=True)
    high = squares.astype(BF16).astype(F32)
    low = squares - high
    q = jnp.dot(scaled, qw_ref[...], preferred_element_type=F32)
    kv = jnp.dot(scaled, kvw_ref[...], preferred_element_type=F32)
    lane = lax.broadcasted_iota(jnp.int32, (tok.shape[0], EXTRA), 1)
    extra = jnp.where(lane == 0, high, jnp.where(lane == 1, low, 0.0))
    half = tok.shape[0] // 2
    for g in range(SECTIONS):
        ids = ids_ref[g : g + 1, :]
        for array, at, width in ((q, 0, WQ), (kv, WQ, WKV), (extra, WQ + WKV, EXTRA)):
            rows = jnp.concatenate(
                [
                    array[g * SEQ_G : (g + 1) * SEQ_G],
                    array[half + g * SEQ_G : half + (g + 1) * SEQ_G],
                ],
                axis=0,
            )
            if width == EXTRA:
                rows = rows + ids
            out_ref[g, :, at : at + width] = rows.astype(BF16)


def project(tokens, gain, q_weight, kv_weight, ids_wide):
    return pl.pallas_call(
        project_kernel,
        out_shape=jax.ShapeDtypeStruct((SECTIONS, ROWS, WQ + WKV + EXTRA), BF16),
        compiler_params=params(),
        name="project",
    )(tokens, gain, q_weight, kv_weight, ids_wide)


def ready_kernel(ctx_ref, got_ref, cos_ref, sin_ref, q_ref, key_ref, value_ref, seq_ref):
    got = got_ref[...].astype(F32)
    total = jnp.sum(got, axis=0)
    squares = (
        total[:, WQ + WKV : WQ + WKV + 1] + total[:, WQ + WKV + 1 : WQ + WKV + 2]
    )
    rscale = lax.rsqrt(squares * (1.0 / D) + EPS)
    total = total[:, : WQ + WKV] * rscale
    cosine = jnp.concatenate(
        [cos_ref[pl.ds(ctx_ref[r % SEQ_G] + r // SEQ_G, 1), :] for r in range(ROWS)], axis=0
    )
    sine = jnp.concatenate(
        [sin_ref[pl.ds(ctx_ref[r % SEQ_G] + r // SEQ_G, 1), :] for r in range(ROWS)], axis=0
    )
    for h in range(GQ):
        q_ref[h * ROWS : (h + 1) * ROWS, :] = turned(
            total[:, h * HD : (h + 1) * HD], cosine, sine
        ).astype(BF16)
    key_ref[...] = turned(total[:, WQ : WQ + HD], cosine, sine).astype(BF16)
    value_ref[...] = total[:, WQ + HD : WQ + WKV].astype(BF16)

    ids = jnp.max(got[:, :, WQ + WKV :], axis=1)
    lane_in = lax.broadcasted_iota(jnp.int32, (EXTRA, GROUP_TOK), 0)
    lane_out = lax.broadcasted_iota(jnp.int32, (EXTRA, GROUP_TOK), 1)
    spread = (lane_in == ID_LANE + lane_out // PAGE).astype(F32)
    ids = jnp.where(
        (lax.broadcasted_iota(jnp.int32, ids.shape, 1) >= ID_LANE), ids, 0.0
    )
    ids = jnp.dot(ids, spread, preferred_element_type=F32).astype(jnp.int32)
    position = (ids & (CAP - 1)) * PAGE + (
        lax.broadcasted_iota(jnp.int32, ids.shape, 1) & (PAGE - 1)
    )
    owner = jnp.full(ids.shape, -1, jnp.int32)
    for j in range(SEQ_G):
        held = (ids >= j * CAP) & (ids < (j + 1) * CAP) & (position < ctx_ref[j])
        owner = jnp.where(held, j, owner)
    seq_ref[...] = owner


def ready(context_len, got, cosine, sine):
    vmem = pl.BlockSpec(memory_space=pltpu.VMEM)
    return pl.pallas_call(
        ready_kernel,
        in_specs=[pl.BlockSpec(memory_space=pltpu.SMEM), vmem, vmem, vmem],
        out_shape=[
            jax.ShapeDtypeStruct((GQ * ROWS, HD), BF16),
            jax.ShapeDtypeStruct((ROWS, HD), BF16),
            jax.ShapeDtypeStruct((ROWS, HD), BF16),
            jax.ShapeDtypeStruct((SECTIONS, GROUP_TOK), jnp.int32),
        ],
        compiler_params=params(),
        name="ready",
    )(context_len, got, cosine, sine)


def attend_kernel(pages_ref, q_ref, key_ref, value_ref, seq_ref, out_ref):
    scale = 1.0 / math.sqrt(HD)
    q = q_ref[...]
    n = GQ * ROWS

    def against(keys):
        return (
            lax.dot_general(q, keys, (((1,), (1,)), ((), ())), preferred_element_type=F32) * scale
        )

    row = lax.broadcasted_iota(jnp.int32, (n, 1), 0)
    row_seq, row_step = row & (SEQ_G - 1), (row // SEQ_G) & 1
    col = lax.broadcasted_iota(jnp.int32, (n, ROWS), 1)
    fresh_ok = ((col & (SEQ_G - 1)) == row_seq) & (col // SEQ_G <= row_step)
    fresh = jnp.where(fresh_ok, against(key_ref[...]), -jnp.inf)
    cached = []
    peak = None
    for s in range(SECTIONS):
        ok = seq_ref[s : s + 1, :] == row_seq
        scores = jnp.where(ok, against(pages_ref[s, :, :HD]), -jnp.inf)
        cached.append(scores)
        peak = scores if peak is None else jnp.maximum(peak, scores)
    highest = jnp.maximum(
        jnp.max(peak, axis=-1, keepdims=True), jnp.max(fresh, axis=-1, keepdims=True)
    )
    fresh = jnp.exp(fresh - highest)
    cached = [jnp.exp(scores - highest) for scores in cached]
    denom = cached[0]
    for scores in cached[1:]:
        denom = denom + scores
    denom = jnp.sum(denom, axis=-1, keepdims=True) + jnp.sum(fresh, axis=-1, keepdims=True)
    inverse = 1.0 / denom
    mixed = jnp.dot(
        (fresh * inverse).astype(BF16), value_ref[...], preferred_element_type=F32
    )
    for s in range(SECTIONS):
        mixed = mixed + jnp.dot(
            (cached[s] * inverse).astype(BF16), pages_ref[s, :, HD:], preferred_element_type=F32
        )
    mixed = mixed.astype(BF16)
    for d in range(SECTIONS):
        for h in range(GQ):
            out_ref[d, :, h * HD : (h + 1) * HD] = mixed[h * ROWS : (h + 1) * ROWS]


def attend(pages, q, key, value, seq):
    return pl.pallas_call(
        attend_kernel,
        out_shape=jax.ShapeDtypeStruct((SECTIONS, ROWS, WQ), BF16),
        compiler_params=params(),
        name="attend",
    )(pages, q, key, value, seq)


def output_kernel(attn_ref, ow_ref, out_ref):
    attn = attn_ref[...].reshape(SECTIONS * ROWS, WQ)
    part = jnp.dot(attn, ow_ref[...], preferred_element_type=F32)
    out_ref[...] = part.astype(BF16).reshape(out_ref.shape)


def output_part(attn, o_weight, members):
    return pl.pallas_call(
        output_kernel,
        out_shape=jax.ShapeDtypeStruct(
            (members, SECTIONS * ROWS // members, o_weight.shape[1]), BF16
        ),
        compiler_params=params(),
        name="output_part",
    )(attn, o_weight)


def finish_kernel(_, got_ref, tok_ref, out_ref):
    total = jnp.sum(got_ref[...].astype(F32), axis=0)
    tok = tok_ref[...].astype(F32)
    for i in range(2):
        rows = jnp.concatenate(
            [total[g * ROWS + i * SEQ_G : g * ROWS + (i + 1) * SEQ_G] for g in range(2)], axis=0
        )
        out_ref[i] = (tok[i] + rows).astype(BF16)


def finish(member, got, tokens):
    members, rows, width = got.shape
    block = pl.BlockSpec((2, rows // 2, width), lambda r, member: (0, member[0], 0))
    return pl.pallas_call(
        finish_kernel,
        grid_spec=pltpu.PrefetchScalarGridSpec(
            num_scalar_prefetch=1,
            grid=(1,),
            in_specs=[pl.BlockSpec(got.shape, lambda r, member: (0, 0, 0)), block],
            out_specs=pl.BlockSpec((2, rows // 2, width), lambda r, member: (0, 0, 0)),
        ),
        out_shape=jax.ShapeDtypeStruct((2, rows // 2, width), BF16),
        compiler_params=params(),
        name="finish",
    )(member, got, tokens)


def on_device(
    prompt_rows, page_slot, context_len, new_tokens, norm_gain, q_weight, kv_weight, o_weight
):
    section = lax.axis_index("section")
    member = lax.axis_index("tensor")
    members = lax.axis_size("tensor")
    core = member % 2
    own_ids = page_slot[0]
    gain_here = lax.dynamic_slice_in_dim(norm_gain, section * DEPTH, DEPTH, 0)
    cosine, sine = rotation_tables()

    weight = (kv_weight.astype(F32) * gain_here[:, None]).astype(BF16)
    from_1 = shifted(weight, 0, 1)
    from_3 = shifted(weight, 0, -1)
    from_2 = shifted(weight, 0, 2)
    near = jnp.concatenate([weight, from_1], axis=0)
    far = jnp.concatenate([from_3, from_2], axis=0)
    near_p = shifted(near, 1, 1)
    far_m = shifted(far, 1, -1)
    near_2, far_2 = lax.optimization_barrier((near, far))
    far_p = shifted(far_2, 1, 1)
    near_m = shifted(near_2, 1, -1)
    near_o = shifted(near_p, 1, 1)
    far_o = shifted(far_m, 1, -1)

    def blocks(*steps):
        z, x = section // 4, section % 4
        ids = []
        for a, b in steps:
            at_0 = ((z + b) % 4) * 4 + (x + a) % 4
            at_1 = ((z + a) % 4) * 4 + (x + b) % 4
            ids.append(jnp.where(core == 0, at_0, at_1))
        return jnp.stack(ids).astype(jnp.int32)

    ids_wide = jnp.pad(
        own_ids.astype(F32), ((0, 0), (ID_LANE, EXTRA - ID_LANE - CAP))
    )
    payload = project(
        new_tokens.reshape(-1, DEPTH), gain_here[None, :], q_weight, kv_weight, ids_wide
    )
    got = lax.all_to_all(payload, "section", split_axis=0, concat_axis=0, tiled=True)
    queries, new_keys, new_values, owners = ready(context_len, got, cosine, sine)

    carry = prompt_pass(
        prompt_rows, blocks((0, 0), (3, 0), (1, 0), (2, 0)), near, far
    )
    carry = prompt_pass(
        prompt_rows, blocks((0, 3), (3, 3), (1, 1), (2, 1)), near_p, far_m, carry
    )
    carry = prompt_pass(
        prompt_rows, blocks((0, 1), (3, 1), (1, 3), (2, 3)), near_m, far_p, carry
    )
    pages = prompt_pass(
        prompt_rows,
        blocks((0, 2), (3, 2), (1, 2), (2, 2)),
        near_o,
        far_o,
        carry,
        (own_ids, cosine, sine),
    )
    received = lax.all_to_all(pages, "section", split_axis=0, concat_axis=0, tiled=True)
    attn = attend(received, queries, new_keys, new_values, owners)
    attn = lax.all_to_all(attn, "section", split_axis=0, concat_axis=0, tiled=True)
    part = output_part(attn, o_weight, members)
    part = lax.all_to_all(part, "tensor", split_axis=0, concat_axis=0, tiled=True)
    return finish(member[None].astype(jnp.int32), part, new_tokens)


def solution(mesh):
    placed = (
        P("section", None),
        P("section", None, None),
        P("section"),
        P(None, None, "section"),
        P(),
        P("section", "tensor"),
        P("section", "tensor"),
        P("tensor", "section"),
    )
    return jax.shard_map(
        on_device,
        mesh=mesh,
        in_specs=placed,
        out_specs=P(None, "tensor", "section"),
        check_vma=False,
    )
```

time: 305 us -> 108 us (0.35)
  waiting for transfers between devices: 154 us -> 19.3 us
  blocking collectives: 62.2 us -> 24.8 us
  Pallas kernels: 0 us -> 31.3 us
  matrix products: 25.6 us -> 0 us
  other arithmetic: 23.4 us -> 1.87 us
  starting transfers between devices: 13.5 us -> 28.5 us
  between operations: 13.4 us -> 0.39 us
  local copies, waits for them, and re-layouts: 12.9 us -> 1.16 us
    psum x2 -> x0, waiting for transfers between devices: 85 us -> none  [the longest x1 60.5 us: on_device(): summed = lax.psum(partial_out, 'tensor')]
    all_gather x1 -> x0, waiting for transfers between devices: 52.2 us -> none  [on_device(): lax.all_gather(kv_weight, 'section', axis=0, tiled=True)]
    psum x1 -> x0, blocking collectives: 40.7 us -> none  [on_device(): lax.psum((query_part, kv_part, squares), 'section')]
    pallas_call x0 -> x9, Pallas kernels: none -> 31.3 us  [the longest x4 26 us: prompt_pass(): pl.pallas_call(functools.partial(prompt_kernel, first, last), grid_spec=p...]
    dot_general x8 -> x0, matrix products: 25.6 us -> none  [the longest x1 17.3 us: on_device(): jnp.dot(normed, lax.all_gather(kv_weight, 'section', axis=0, tiled=True),...]
    all_to_all x0 -> x2, blocking collectives: none -> 24.8 us  [the longest x1 13 us: on_device(): lax.all_to_all(attn, 'section', split_axis=0, concat_axis=0, tiled=True)]
    all_gather x1 -> x0, blocking collectives: 21.5 us -> none  [on_device(): lax.all_gather(attn, 'section', axis=1, tiled=True)]
    ppermute x0 -> x9, starting transfers between devices: none -> 15.4 us  [shifted(): return lax.ppermute(array, ('section', 'tensor'), pairs)]
  transfers between devices with their start and end apart: 5 -> 11, of which waited for: 4 -> 3; matrix products, arithmetic and copies ran while one was open for 6% -> 1% of each run, Pallas kernels for 0% -> 27%
where the time goes in v1:
time: 108 us; the launch traced here: 107 us
  Pallas kernels  31.3 us (29%)
  starting transfers between devices  28.5 us (26%)
  blocking collectives  24.8 us (23%)
  waiting for transfers between devices  19.3 us (18%)
  other arithmetic  1.87 us (2%)
  local copies, waits for them, and re-layouts  1.16 us (1%)
    pallas_call x4, Pallas kernels, prompt_pass(): pl.pallas_call(functools.partial(prompt_kernel, first, last), grid_spec=p...  26 us
    ppermute x9, starting transfers between devices, shifted(): return lax.ppermute(array, ('section', 'tensor'), pairs)  15.4 us
    all_to_all x1, waiting for transfers between devices, on_device(): lax.all_to_all(pages, 'section', split_axis=0, concat_axis=0, tiled=True)  13 us
    all_to_all x1, blocking collectives, on_device(): lax.all_to_all(attn, 'section', split_axis=0, concat_axis=0, tiled=True)  13 us
    all_to_all x1, blocking collectives, on_device(): lax.all_to_all(part, 'tensor', split_axis=0, concat_axis=0, tiled=True)  11.8 us
    all_to_all x1, starting transfers between devices, on_device(): lax.all_to_all(pages, 'section', split_axis=0, concat_axis=0, tiled=True)  7.03 us
    ppermute x9, waiting for transfers between devices, shifted(): return lax.ppermute(array, ('section', 'tensor'), pairs)  6.29 us
    all_to_all x1, starting transfers between devices, on_device(): lax.all_to_all(payload, 'section', split_axis=0, concat_axis=0, tiled=True)  6.06 us
  transfers between devices with their start and end apart: 11, of which 3 were waited for; matrix products, arithmetic and copies ran while one was open for 1% of the time, Pallas kernels for 27%

profile of v1, /device:TPU:0, one launch (start us, length us, event | category | flops | bytes accessed | tf_op | source)
XLA Modules:
  0.0 107.4 jit_solution(180749144486980341)
XLA Ops:
  0.0 0.9 dynamic_slice.3
  0.9 1.1 %multiply_convert_fusion = bf16[512,256]{1,0:T(8,128)(2,1)S(1)} fusion(bf16[512,256]{1,0:T(8,128)(2,1)} %kvw_ref.1, f32[512]{0:T(512)S(1)} %dynamic_slice.3), kind=kLoop, calls=%fused_computation.1 | loop fusion | flops 393216 | bytes 526336 | tf_op jit(solution)/shard_map/convert_element_type | solution.py:358
  2.0 2.9 %collective-permute-start.3 = (bf16[512,256]{1,0:T(8,128)(2,1)S(1)}, bf16[512,256]{1,0:T(8,128)(2,1)S(1)}, u32[]{:S(2)}, u32[]{:S(2)}) collective-permute-start(bf16[512,256]{1,0:T(8,128)(2,1)S(1)} %multiply_convert_fusion), channel_id=1, source_target_pairs={{0,24},{1,97},{2,26},{3,99},{4,28},{5,101},{6,30},{7,103},{8,0},{9... | collective-permute-start | bytes 786440 | tf_op jit(solution)/shard_map/ppermute | solution.py:62
  4.9 0.8 collective-permute-start.4
  5.7 0.9 collective-permute-start
  6.6 5.0 %collective-permute-done.3 = bf16[512,256]{1,0:T(8,128)(2,1)S(1)} collective-permute-done((bf16[512,256]{1,0:T(8,128)(2,1)S(1)}, bf16[512,256]{1,0:T(8,128)(2,1)S(1)}, u32[]{:S(2)}, u32[]{:S(2)}) %collective-permute-start.3) | collective-permute-done | bytes 262176 | tf_op jit(solution)/shard_map/ppermute | solution.py:62
  11.6 1.3 %collective-permute-done.4 = bf16[512,256]{1,0:T(8,128)(2,1)S(1)} collective-permute-done((bf16[512,256]{1,0:T(8,128)(2,1)S(1)}, bf16[512,256]{1,0:T(8,128)(2,1)S(1)}, u32[]{:S(2)}, u32[]{:S(2)}) %collective-permute-start.4) | collective-permute-done | bytes 262176 | tf_op jit(solution)/shard_map/ppermute | solution.py:62
  12.9 4.1 %collective-permute-start.5 = (bf16[1024,256]{1,0:T(8,128)(2,1)S(1)}, bf16[1024,256]{1,0:T(8,128)(2,1)S(1)}, u32[]{:S(2)}, u32[]{:S(2)}) collective-permute-start(bf16[1024,256]{1,0:T(8,128)(2,1)S(1)} %constant_dynamic-update-slice_fusion.refs_6_), channel_id=1, source_target_pairs={{0,96},{1,25},{2,98},{3,27},{4,100},{5,29},{6,102},{7,31},{8,104},... | collective-permute-start | bytes 1572872 | tf_op jit(solution)/shard_map/ppermute | solution.py:62
  17.1 0.6 collective-permute-start.1
  17.8 1.4 %project.1 = bf16[16,16,1408]{2,1,0:T(8,128)(2,1)} custom-call(bf16[256,512]{1,0:T(8,128)(2,1)S(1)} %bitcast.21, f32[1,512]{1,0:T(1,128)S(1)} %bitcast.22, bf16[512,1024]{1,0:T(8,128)(2,1)S(1)} %copy-done.1, bf16[512,256]{1,0:T(8,128)(2,1)S(1)} %copy-done.3, f32[16,128]{1,0:T(8,128)S(1)} %pad.4.ids_ref), custom_call_target="tpu_custom_call" | custom-call | tf_op jit(solution)/shard_map/project/pallas_call | solution.py:186
  19.2 6.1 %all-to-all-start.1 = ((bf16[16,16,1408]{2,1,0:T(8,128)(2,1)}), bf16[16,16,1408]{2,1,0:T(8,128)(2,1)}, u32[]{:S(2)}, u32[]{:S(2)}) async-start(bf16[16,16,1408]{2,1,0:T(8,128)(2,1)} %project.1), calls=%async_computation.1 | async-start | bytes 1441792 | tf_op jit(solution)/shard_map/all_to_all | solution.py:387
  25.8 2.9 %collective-permute-start.7 = (bf16[1024,256]{1,0:T(8,128)(2,1)S(1)}, bf16[1024,256]{1,0:T(8,128)(2,1)S(1)}, u32[]{:S(2)}, u32[]{:S(2)}) collective-permute-start(bf16[1024,256]{1,0:T(8,128)(2,1)S(1)} %pad_maximum_fusion.refs_5_), channel_id=1, source_target_pairs={{0,96},{1,25},{2,98},{3,27},{4,100},{5,29},{6,102},{7,31},{8,104},... | collective-permute-start | bytes 1572872 | tf_op jit(solution)/shard_map/ppermute | solution.py:62
  28.7 3.2 %collective-permute-start.6 = (bf16[1024,256]{1,0:T(8,128)(2,1)S(1)}, bf16[1024,256]{1,0:T(8,128)(2,1)S(1)}, u32[]{:S(2)}, u32[]{:S(2)}) collective-permute-start(bf16[1024,256]{1,0:T(8,128)(2,1)S(1)} %collective-permute-done.5.refs_6_), channel_id=1, source_target_pairs={{0,96},{1,25},{2,98},{3,27},{4,100},{5,29},{6,102},{7,31},{8,104},... | collective-permute-start | bytes 1572872 | tf_op jit(solution)/shard_map/ppermute | solution.py:62
  32.5 6.0 %prompt_first.1 = (f32[2048,256]{1,0:T(8,128)S(1)}, f32[2048,128]{1,0:T(8,128)S(1)}) custom-call(s32[4]{0:T(128)S(1)} %pad_add_fusion.3.refs_0_, bf16[2048,8192]{1,0:T(8,128)(2,1)} %refs_5_.1, bf16[2048,8192]{1,0:T(8,128)(2,1)} %refs_5_.1, bf16[2048,8192]{1,0:T(8,128)(2,1)} %refs_5_.1, bf16[2048,8192]{1,0:T(8,128)(2,1)} %refs_5_.1, ...), custom_call_target="tpu_custom_call" | custom-call | tf_op jit(solution)/shard_map/prompt_first/pallas_call | solution.py:145
  38.5 6.5 %prompt_middle.2 = (f32[2048,256]{1,0:T(8,128)S(1)}, f32[2048,128]{1,0:T(8,128)S(1)}) custom-call(s32[4]{0:T(128)S(1)} %pad_add_fusion.2.refs_0_, bf16[2048,8192]{1,0:T(8,128)(2,1)} %refs_5_.1, bf16[2048,8192]{1,0:T(8,128)(2,1)} %refs_5_.1, bf16[2048,8192]{1,0:T(8,128)(2,1)} %refs_5_.1, bf16[2048,8192]{1,0:T(8,128)(2,1)} %refs_5_.1, ...), custom_call_target="tpu_custom_call" | custom-call | tf_op jit(solution)/shard_map/prompt_middle/pallas_call | solution.py:145
  45.0 6.1 %prompt_middle.3 = (f32[2048,256]{1,0:T(8,128)S(1)}, f32[2048,128]{1,0:T(8,128)S(1)}) custom-call(s32[4]{0:T(128)S(1)} %pad_add_fusion.1.refs_0_, bf16[2048,8192]{1,0:T(8,128)(2,1)} %refs_5_.1, bf16[2048,8192]{1,0:T(8,128)(2,1)} %refs_5_.1, bf16[2048,8192]{1,0:T(8,128)(2,1)} %refs_5_.1, bf16[2048,8192]{1,0:T(8,128)(2,1)} %refs_5_.1, ...), custom_call_target="tpu_custom_call" | custom-call | tf_op jit(solution)/shard_map/prompt_middle/pallas_call | solution.py:145
  51.1 7.5 %prompt_last.1 = bf16[16,128,256]{2,1,0:T(8,128)(2,1)} custom-call(s32[4]{0:T(128)S(1)} %pad_add_fusion.refs_0_, s32[16,8]{1,0:T(8,128)S(1)} %copy.11.refs_1_, bf16[2048,8192]{1,0:T(8,128)(2,1)} %refs_5_.1, bf16[2048,8192]{1,0:T(8,128)(2,1)} %refs_5_.1, bf16[2048,8192]{1,0:T(8,128)(2,1)} %refs_5_.1, bf16[2048,8192]{1,0:T(8,128)(2,1)} %refs_5_.1, ...), custom_call_target="tpu_custom_call" | custom-call | tf_op jit(solution)/shard_map/prompt_last/pallas_call | solution.py:145
  58.6 7.0 %all-to-all-start = ((bf16[16,128,256]{2,1,0:T(8,128)(2,1)}), bf16[16,128,256]{2,1,0:T(8,128)(2,1)S(1)}, u32[]{:S(2)}, u32[]{:S(2)}) async-start(bf16[16,128,256]{2,1,0:T(8,128)(2,1)} %prompt_last.1), calls=%async_computation | async-start | bytes 2097152 | tf_op jit(solution)/shard_map/all_to_all | solution.py:407
  65.6 1.5 %ready.1 = (bf16[128,128]{1,0:T(8,128)(2,1)S(1)}, bf16[16,128]{1,0:T(8,128)(2,1)S(1)}, bf16[16,128]{1,0:T(8,128)(2,1)S(1)}, s32[16,128]{1,0:T(8,128)S(1)}) custom-call(s32[8]{0:T(128)S(1)} %copy-done.4, bf16[16,16,1408]{2,1,0:T(8,128)(2,1)} %all-to-all-done.1.got_ref, f32[136,128]{1,0:T(8,128)S(1)} %get-tuple-element.32.refs_10_.cos_ref, ...), custom_call_target="tpu_custom_call" | custom-call | tf_op jit(solution)/shard_map/ready/pallas_call | solution.py:235
  67.1 13.0 %all-to-all-done.pages_ref = bf16[16,128,256]{2,1,0:T(8,128)(2,1)S(1)} async-done(((bf16[16,128,256]{2,1,0:T(8,128)(2,1)}), bf16[16,128,256]{2,1,0:T(8,128)(2,1)S(1)}, u32[]{:S(2)}, u32[]{:S(2)}) %all-to-all-start) | async-done | bytes 1048608 | tf_op jit(solution)/shard_map/all_to_all | solution.py:407
  80.1 1.4 %attend.1 = bf16[16,16,1024]{2,1,0:T(8,128)(2,1)S(1)} custom-call(bf16[16,128,256]{2,1,0:T(8,128)(2,1)S(1)} %all-to-all-done.pages_ref, bf16[128,128]{1,0:T(8,128)(2,1)S(1)} %get-tuple-element.25.q_ref, bf16[16,128]{1,0:T(8,128)(2,1)S(1)} %get-tuple-element.26.key_ref, bf16[16,128]{1,0:T(8,128)(2,1)S(1)} %get-tuple-element.27.value_ref, ...), custom_call_target="tpu_custom_call" | custom-call | tf_op jit(solution)/shard_map/attend/pallas_call | solution.py:295
  81.5 13.0 %all_to_all.20.attn_ref = bf16[16,16,1024]{2,1,0:T(8,128)(2,1)S(1)} all-to-all(bf16[16,16,1024]{2,1,0:T(8,128)(2,1)S(1)} %attend.1), channel_id=1, replica_groups=mesh['section'=16,'tensor'=8] {'section'}, dimensions={0} | all-to-all | bytes 1048576 | tf_op jit(solution)/shard_map/all_to_all | solution.py:409
  94.9 11.8 %all_to_all.21.got_ref = bf16[8,32,512]{2,1,0:T(8,128)(2,1)S(1)} all-to-all(bf16[8,32,512]{2,1,0:T(8,128)(2,1)S(1)} %output_part.1), channel_id=1, replica_groups=mesh['section'=16,'tensor'=8] {'tensor'}, dimensions={0} | all-to-all | bytes 524288 | tf_op jit(solution)/shard_map/all_to_all | solution.py:411
  106.7 0.7 finish.1
  (38 shorter events, 1.5 us)
Async XLA Ops:
  0.0 17.8 %copy-start.3 = (bf16[512,256]{1,0:T(8,128)(2,1)S(1)}, bf16[512,256]{1,0:T(8,128)(2,1)}, u32[]{:S(2)}) copy-start(bf16[512,256]{1,0:T(8,128)(2,1)} %kvw_ref.1) | copy-start | bytes 786436
  0.0 17.6 %copy-start.5 = (s32[1,16,8]{1,2,0:T(8,128)S(1)}, s32[1,16,8]{1,2,0:T(8,128)}, u32[]{:S(2)}) copy-start(s32[1,16,8]{1,2,0:T(8,128)} %param.9) | copy-start | bytes 1540
  0.0 17.8 %copy-start.2 = (bf16[2,128,512]{2,1,0:T(8,128)(2,1)S(1)}, bf16[2,128,512]{2,1,0:T(8,128)(2,1)}, u32[]{:S(2)}) copy-start(bf16[2,128,512]{2,1,0:T(8,128)(2,1)} %tok_ref.1) | copy-start | bytes 786436
  0.0 17.8 %copy-start.1 = (bf16[512,1024]{1,0:T(8,128)(2,1)S(1)}, bf16[512,1024]{1,0:T(8,128)(2,1)}, u32[]{:S(2)}) copy-start(bf16[512,1024]{1,0:T(8,128)(2,1)} %qw_ref.1) | copy-start | bytes 3145732
  2.0 9.6 %collective-permute-start.3 = (bf16[512,256]{1,0:T(8,128)(2,1)S(1)}, bf16[512,256]{1,0:T(8,128)(2,1)S(1)}, u32[]{:S(2)}, u32[]{:S(2)}) collective-permute-start(bf16[512,256]{1,0:T(8,128)(2,1)S(1)} %multiply_convert_fusion), channel_id=1, source_target_pairs={{0,24},{1,97},{2,26},{3,99},{4,28},{5,101},{6,30},{7,103},{8,0},{9... | collective-permute-start | bytes 786440 | tf_op jit(solution)/shard_map/ppermute | solution.py:62
  4.9 8.0 %collective-permute-start.4 = (bf16[512,256]{1,0:T(8,128)(2,1)S(1)}, bf16[512,256]{1,0:T(8,128)(2,1)S(1)}, u32[]{:S(2)}, u32[]{:S(2)}) collective-permute-start(bf16[512,256]{1,0:T(8,128)(2,1)S(1)} %multiply_convert_fusion), channel_id=1, source_target_pairs={{0,16},{1,65},{2,18},{3,67},{4,20},{5,69},{6,22},{7,71},{8,24},{9,... | collective-permute-start | bytes 786440 | tf_op jit(solution)/shard_map/ppermute | solution.py:62
  5.7 11.3 %collective-permute-start = (bf16[512,256]{1,0:T(8,128)(2,1)S(1)}, bf16[512,256]{1,0:T(8,128)(2,1)S(1)}, u32[]{:S(2)}, u32[]{:S(2)}) collective-permute-start(bf16[512,256]{1,0:T(8,128)(2,1)S(1)} %multiply_convert_fusion), channel_id=1, source_target_pairs={{0,8},{1,33},{2,10},{3,35},{4,12},{5,37},{6,14},{7,39},{8,16},{9,4... | collective-permute-start | bytes 786440 | tf_op jit(solution)/shard_map/ppermute | solution.py:62
  12.9 15.8 %collective-permute-start.5 = (bf16[1024,256]{1,0:T(8,128)(2,1)S(1)}, bf16[1024,256]{1,0:T(8,128)(2,1)S(1)}, u32[]{:S(2)}, u32[]{:S(2)}) collective-permute-start(bf16[1024,256]{1,0:T(8,128)(2,1)S(1)} %constant_dynamic-update-slice_fusion.refs_6_), channel_id=1, source_target_pairs={{0,96},{1,25},{2,98},{3,27},{4,100},{5,29},{6,102},{7,31},{8,104},... | collective-permute-start | bytes 1572872 | tf_op jit(solution)/shard_map/ppermute | solution.py:62
  17.1 14.9 %collective-permute-start.1 = (bf16[1024,256]{1,0:T(8,128)(2,1)S(1)}, bf16[1024,256]{1,0:T(8,128)(2,1)}, u32[]{:S(2)}, u32[]{:S(2)}) collective-permute-start(bf16[1024,256]{1,0:T(8,128)(2,1)S(1)} %pad_maximum_fusion.refs_5_), channel_id=1, source_target_pairs={{0,32},{1,9},{2,34},{3,11},{4,36},{5,13},{6,38},{7,15},{8,40},{9,1... | collective-permute-start | bytes 1572872 | tf_op jit(solution)/shard_map/ppermute | solution.py:62
  19.2 39.4 %all-to-all-start.1 = ((bf16[16,16,1408]{2,1,0:T(8,128)(2,1)}), bf16[16,16,1408]{2,1,0:T(8,128)(2,1)}, u32[]{:S(2)}, u32[]{:S(2)}) async-start(bf16[16,16,1408]{2,1,0:T(8,128)(2,1)} %project.1), calls=%async_computation.1 | async-start | bytes 1441792 | tf_op jit(solution)/shard_map/all_to_all | solution.py:387
  25.8 19.2 %collective-permute-start.7 = (bf16[1024,256]{1,0:T(8,128)(2,1)S(1)}, bf16[1024,256]{1,0:T(8,128)(2,1)S(1)}, u32[]{:S(2)}, u32[]{:S(2)}) collective-permute-start(bf16[1024,256]{1,0:T(8,128)(2,1)S(1)} %pad_maximum_fusion.refs_5_), channel_id=1, source_target_pairs={{0,96},{1,25},{2,98},{3,27},{4,100},{5,29},{6,102},{7,31},{8,104},... | collective-permute-start | bytes 1572872 | tf_op jit(solution)/shard_map/ppermute | solution.py:62
  28.7 16.3 %collective-permute-start.8 = (bf16[1024,256]{1,0:T(8,128)(2,1)S(1)}, bf16[1024,256]{1,0:T(8,128)(2,1)S(1)}, u32[]{:S(2)}, u32[]{:S(2)}) collective-permute-start(bf16[1024,256]{1,0:T(8,128)(2,1)S(1)} %constant_dynamic-update-slice_fusion.refs_6_), channel_id=1, source_target_pairs={{0,32},{1,9},{2,34},{3,11},{4,36},{5,13},{6,38},{7,15},{8,40},{9,1... | collective-permute-start | bytes 1572872 | tf_op jit(solution)/shard_map/ppermute | solution.py:62
  28.7 22.4 %collective-permute-start.6 = (bf16[1024,256]{1,0:T(8,128)(2,1)S(1)}, bf16[1024,256]{1,0:T(8,128)(2,1)S(1)}, u32[]{:S(2)}, u32[]{:S(2)}) collective-permute-start(bf16[1024,256]{1,0:T(8,128)(2,1)S(1)} %collective-permute-done.5.refs_6_), channel_id=1, source_target_pairs={{0,96},{1,25},{2,98},{3,27},{4,100},{5,29},{6,102},{7,31},{8,104},... | collective-permute-start | bytes 1572872 | tf_op jit(solution)/shard_map/ppermute | solution.py:62
  31.9 19.2 %collective-permute-start.2 = (bf16[1024,256]{1,0:T(8,128)(2,1)}, bf16[1024,256]{1,0:T(8,128)(2,1)S(1)}, u32[]{:S(2)}, u32[]{:S(2)}) collective-permute-start(bf16[1024,256]{1,0:T(8,128)(2,1)} %collective-permute-done.1.refs_5_), channel_id=1, source_target_pairs={{0,32},{1,9},{2,34},{3,11},{4,36},{5,13},{6,38},{7,15},{8,40},{9,1... | collective-permute-start | bytes 1572872 | tf_op jit(solution)/shard_map/ppermute | solution.py:62
  58.6 7.0 %copy-start.4 = (s32[8]{0:T(128)S(1)}, s32[8]{0:T(128)}, u32[]{:S(2)}) copy-start(s32[8]{0:T(128)} %ctx_ref.1) | copy-start | bytes 100
  58.6 21.6 %all-to-all-start = ((bf16[16,128,256]{2,1,0:T(8,128)(2,1)}), bf16[16,128,256]{2,1,0:T(8,128)(2,1)S(1)}, u32[]{:S(2)}, u32[]{:S(2)}) async-start(bf16[16,128,256]{2,1,0:T(8,128)(2,1)} %prompt_last.1), calls=%async_computation | async-start | bytes 2097152 | tf_op jit(solution)/shard_map/all_to_all | solution.py:407
  65.6 28.9 %copy-start = (bf16[1024,512]{1,0:T(8,128)(2,1)S(1)}, bf16[1024,512]{1,0:T(8,128)(2,1)}, u32[]{:S(2)}) copy-start(bf16[1024,512]{1,0:T(8,128)(2,1)} %ow_ref.1) | copy-start | bytes 3145732

commit v2 on v1

--- a/solution.py
+++ b/solution.py
@@ -28,11 +28,10 @@
 ROPE_BASE = 500000.0
 BF16 = jnp.bfloat16
 F32 = jnp.float32
-VMEM_LIMIT = 40 * 1024 * 1024
-
-
-def params(**more):
-    return pltpu.CompilerParams(vmem_limit_bytes=VMEM_LIMIT, **more)
+
+
+def params(mib=16):
+    return pltpu.CompilerParams(vmem_limit_bytes=mib * 1024 * 1024)
 
 
 def rotation_tables():
@@ -62,101 +61,170 @@
     return lax.ppermute(array, ("section", "tensor"), pairs)
 
 
-def prompt_kernel(first, last, *refs):
-    if last:
-        _, ids_ref, *refs = refs
-    else:
-        _, *refs = refs
-    x_refs, refs = refs[:4], refs[4:]
-    wa_ref, wb_ref, *refs = refs
-    if not first:
-        acc_ref, squares_ref, *refs = refs
-    if last:
-        cos_ref, sin_ref, pages_ref = refs
-    else:
-        acc_out, squares_out = refs
-
-    total, squares = None, None
-    for k, x_ref in enumerate(x_refs):
-        x = x_ref[...]
-        w_ref = (wa_ref, wb_ref)[k // 2]
-        w = w_ref[(k % 2) * DEPTH : (k % 2 + 1) * DEPTH, :]
-        part = jnp.dot(x, w, preferred_element_type=F32)
-        total = part if total is None else total + part
-        wide = x.astype(F32)
-        wide = wide * wide
-        for c in range(DEPTH // 128):
-            piece = wide[:, c * 128 : (c + 1) * 128]
-            squares = piece if squares is None else squares + piece
-    if not first:
-        total = total + acc_ref[...]
-        squares = squares + squares_ref[...]
-    if not last:
-        acc_out[...] = total
-        squares_out[...] = squares
-        return
-    mean = jnp.sum(squares, axis=-1, keepdims=True) * (1.0 / D)
-    total = total * lax.rsqrt(mean + EPS)
-    groups = total.shape[0] // GROUP_TOK
-    for g in range(groups):
-        group = pl.program_id(0) * groups + g
-        for c in range(CAP):
-            row = g * GROUP_TOK + c * PAGE
-            page = jnp.maximum(ids_ref[group, c], 0) % CAP
-            at = pl.ds(pl.multiple_of(page * PAGE, PAGE), PAGE)
-            key = turned(total[row : row + PAGE, :HD], cos_ref[at, :], sin_ref[at, :])
-            pages_ref[g, c * PAGE : (c + 1) * PAGE, :HD] = key.astype(BF16)
-        pages_ref[g, :, HD:] = total[g * GROUP_TOK : (g + 1) * GROUP_TOK, HD:].astype(BF16)
-
-
-def prompt_pass(x, blocks, wa, wb, carry=None, final=None):
-    first, last = carry is None, final is not None
+TILE = 256
+PAGES = TILE // PAGE
+BUFFERS = 3
+
+
+def early_kernel(n_early, blocks_ref, order_ref, count_ref, x_ref, *refs):
+    w_refs, refs = refs[: n_early // 2], refs[n_early // 2 :]
+    acc_ref, rest_ref, squares_ref, buf_ref, sems = refs
+    count = count_ref[0]
+
+    def copy(t, c):
+        slot = t % BUFFERS
+        row = pl.multiple_of(order_ref[t * PAGES + c] * PAGE, PAGE)
+        return pltpu.make_async_copy(
+            x_ref.at[pl.ds(row, PAGE), :],
+            buf_ref.at[slot, pl.ds(c * PAGE, PAGE), :],
+            sems.at[slot, c],
+        )
+
+    def begin(t):
+        for c in range(PAGES):
+
+            @pl.when(t * PAGES + c < count)
+            def _():
+                copy(t, c).start()
+
+    def end(t):
+        for c in range(PAGES):
+
+            @pl.when(t * PAGES + c < count)
+            def _():
+                copy(t, c).wait()
+
+    for t in range(BUFFERS - 1):
+        begin(t)
+
+    def tile(t, _):
+        begin(t + BUFFERS - 1)
+        end(t)
+        slot = t % BUFFERS
+        rows = pl.ds(pl.multiple_of(t * TILE, TILE), TILE)
+
+        def depth(k):
+            return pl.ds(pl.multiple_of(blocks_ref[k] * DEPTH, DEPTH), DEPTH)
+
+        total = None
+        for k in range(n_early):
+            w = w_refs[k // 2][(k % 2) * DEPTH : (k % 2 + 1) * DEPTH, :]
+            part = jnp.dot(buf_ref[slot, :, depth(k)], w, preferred_element_type=F32)
+            total = part if total is None else total + part
+        acc_ref[rows, :] = total
+        for k in range(n_early, SECTIONS):
+            at = (k - n_early) * DEPTH
+            rest_ref[rows, at : at + DEPTH] = buf_ref[slot, :, depth(k)]
+        for c in range(PAGES):
+            sums = [None] * 4
+            for j in range(D // 128):
+                piece = buf_ref[slot, c * PAGE : (c + 1) * PAGE, j * 128 : (j + 1) * 128]
+                piece = piece.astype(F32)
+                piece = piece * piece
+                sums[j % 4] = piece if sums[j % 4] is None else sums[j % 4] + piece
+            at = pl.multiple_of(t * TILE + c * PAGE, PAGE)
+            squares_ref[pl.ds(at, PAGE), :] = (sums[0] + sums[1]) + (sums[2] + sums[3])
+        return 0
+
+    lax.fori_loop(0, pl.cdiv(count, PAGES), tile, 0)
+
+
+def kept(array):
+    return pltpu.with_memory_space_constraint(array, pltpu.VMEM)
+
+
+def in_hbm(array):
+    return pltpu.with_memory_space_constraint(array, pltpu.HBM)
+
+
+SMEM_SPEC = pl.BlockSpec(memory_space=pltpu.SMEM)
+VMEM_SPEC = pl.BlockSpec(memory_space=pltpu.VMEM)
+
+
+def prompt_early(blocks, order, count, x, weights):
     rows = x.shape[0]
-    step = 512
-    n_scalars = 2 if last else 1
-
-    def x_at(k):
-        return pl.BlockSpec((step, DEPTH), lambda r, blocks, *_: (r, blocks[k]))
-
-    whole_w = pl.BlockSpec((2 * DEPTH, WKV), lambda r, *_: (0, 0))
-    acc_spec = pl.BlockSpec((step, WKV), lambda r, *_: (r, 0))
-    sq_spec = pl.BlockSpec((step, 128), lambda r, *_: (r, 0))
-    in_specs = [x_at(k) for k in range(4)] + [whole_w, whole_w]
-    args = [x] * 4 + [wa, wb]
-    if not first:
-        in_specs += [acc_spec, sq_spec]
-        args += list(carry)
-    scalars = [blocks]
-    if last:
-        ids, cosine, sine = final
-        scalars.append(ids)
-        table = pl.BlockSpec((POSITIONS, HD), lambda r, *_: (0, 0))
-        in_specs += [table, table]
-        args += [cosine, sine]
-        groups = step // GROUP_TOK
-        out_specs = pl.BlockSpec((groups, GROUP_TOK, WKV), lambda r, *_: (r, 0, 0))
-        out_shape = jax.ShapeDtypeStruct((rows // GROUP_TOK, GROUP_TOK, WKV), BF16)
-    else:
-        out_specs = [acc_spec, sq_spec]
-        out_shape = [
-            jax.ShapeDtypeStruct((rows, WKV), F32),
-            jax.ShapeDtypeStruct((rows, 128), F32),
-        ]
-    return pl.pallas_call(
-        functools.partial(prompt_kernel, first, last),
-        grid_spec=pltpu.PrefetchScalarGridSpec(
-            num_scalar_prefetch=n_scalars,
-            grid=(rows // step,),
-            in_specs=in_specs,
-            out_specs=out_specs,
-        ),
-        out_shape=out_shape,
-        compiler_params=params(),
-        name="prompt_last" if last else "prompt_first" if first else "prompt_middle",
-    )(*scalars, *args)
-
-
-def project_kernel(tok_ref, gain_ref, qw_ref, kvw_ref, ids_ref, out_ref):
+    n_early = 2 * len(weights)
+    return pl.pallas_call(
+        functools.partial(early_kernel, n_early),
+        in_specs=[SMEM_SPEC] * 3
+        + [pl.BlockSpec(memory_space=pl.ANY)]
+        + [VMEM_SPEC] * len(weights),
+        out_specs=[VMEM_SPEC] * 3,
+        out_shape=[
+            pltpu.VMEM((rows, WKV), F32),
+            pltpu.VMEM((rows, (SECTIONS - n_early) * DEPTH), BF16),
+            pltpu.VMEM((rows, 128), F32),
+        ],
+        scratch_shapes=[
+            pltpu.VMEM((BUFFERS, TILE, D), BF16),
+            pltpu.SemaphoreType.DMA((BUFFERS, PAGES)),
+        ],
+        compiler_params=params(24),
+        name="prompt_early",
+    )(blocks, order, count, x, *weights)
+
+
+def late_kernel(
+    order_ref, turn_ref, count_ref, cos_ref, sin_ref, acc_ref, rest_ref, squares_ref, *refs
+):
+    w_refs, (pages_ref, tile_ref, cos_tile, sin_tile) = refs[:-4], refs[-4:]
+    count = count_ref[0]
+    pages_ref[...] = jnp.zeros_like(pages_ref)
+
+    def tile(t, _):
+        rows = pl.ds(pl.multiple_of(t * TILE, TILE), TILE)
+        last = count - 1 - t * PAGES
+        for c in range(PAGES):
+            page = turn_ref[t * PAGES + jnp.minimum(c, last)]
+            turn = pl.ds(pl.multiple_of(page * PAGE, PAGE), PAGE)
+            cos_tile[c * PAGE : (c + 1) * PAGE, :] = cos_ref[turn, :]
+            sin_tile[c * PAGE : (c + 1) * PAGE, :] = sin_ref[turn, :]
+        total = acc_ref[rows, :]
+        for k, w_ref in enumerate(w_refs):
+            x = rest_ref[rows, k * 2 * DEPTH : (k + 1) * 2 * DEPTH]
+            total = total + jnp.dot(x, w_ref[...], preferred_element_type=F32)
+        mean = jnp.sum(squares_ref[rows, :], axis=-1, keepdims=True) * (1.0 / D)
+        total = total * lax.rsqrt(mean + EPS)
+        tile_ref[:, :HD] = turned(total[:, :HD], cos_tile[...], sin_tile[...]).astype(BF16)
+        tile_ref[:, HD:] = total[:, HD:].astype(BF16)
+        for c in range(PAGES):
+            source = jnp.minimum(c, last)
+            slot = order_ref[t * PAGES + source]
+            to = pl.ds(pl.multiple_of((slot % CAP) * PAGE, PAGE), PAGE)
+            here = pl.ds(pl.multiple_of(source * PAGE, PAGE), PAGE)
+            pages_ref[slot // CAP, to, :] = tile_ref[here, :]
+        return 0
+
+    lax.fori_loop(0, pl.cdiv(count, PAGES), tile, 0)
+
+
+def prompt_late(order, turn, count, cosine, sine, early, weights):
+    return pl.pallas_call(
+        late_kernel,
+        in_specs=[SMEM_SPEC] * 3 + [VMEM_SPEC] * (5 + len(weights)),
+        out_specs=VMEM_SPEC,
+        out_shape=jax.ShapeDtypeStruct((SECTIONS, GROUP_TOK, WKV), BF16),
+        scratch_shapes=[
+            pltpu.VMEM((TILE, WKV), BF16),
+            pltpu.VMEM((TILE, HD), F32),
+            pltpu.VMEM((TILE, HD), F32),
+        ],
+        compiler_params=params(16),
+        name="prompt_late",
+    )(order, turn, count, cosine, sine, *[kept(array) for array in early], *weights)
+
+
+def project_kernel(
+    slot_ref, tok_ref, gain_ref, qw_ref, kvw_ref, ids_ref, out_ref, order_ref, turn_ref, count_ref
+):
+    found = jnp.int32(0)
+    for slot in range(SECTIONS * CAP):
+        held = slot_ref[slot // CAP, slot % CAP]
+        order_ref[found] = slot
+        turn_ref[found] = jnp.maximum(held, 0) & (CAP - 1)
+        found = found + jnp.where(held >= 0, 1, 0)
+    count_ref[0] = found
+
     tok = tok_ref[...].astype(F32)
     scaled = (tok * gain_ref[...]).astype(BF16)
     squares = jnp.sum(tok * tok, axis=-1, keepdims=True)
@@ -182,13 +250,21 @@
             out_ref[g, :, at : at + width] = rows.astype(BF16)
 
 
-def project(tokens, gain, q_weight, kv_weight, ids_wide):
+def project(own_ids, tokens, gain, q_weight, kv_weight, ids_wide):
+    slots = jax.ShapeDtypeStruct((SECTIONS * CAP,), jnp.int32)
     return pl.pallas_call(
         project_kernel,
-        out_shape=jax.ShapeDtypeStruct((SECTIONS, ROWS, WQ + WKV + EXTRA), BF16),
+        in_specs=[SMEM_SPEC] + [VMEM_SPEC] * 5,
+        out_specs=[VMEM_SPEC] + [SMEM_SPEC] * 3,
+        out_shape=[
+            jax.ShapeDtypeStruct((SECTIONS, ROWS, WQ + WKV + EXTRA), BF16),
+            slots,
+            slots,
+            jax.ShapeDtypeStruct((1,), jnp.int32),
+        ],
         compiler_params=params(),
         name="project",
-    )(tokens, gain, q_weight, kv_weight, ids_wide)
+    )(own_ids, in_hbm(tokens), gain, in_hbm(q_weight), kv_weight, ids_wide)
 
 
 def ready_kernel(ctx_ref, got_ref, cos_ref, sin_ref, q_ref, key_ref, value_ref, seq_ref):
@@ -246,7 +322,9 @@
     )(context_len, got, cosine, sine)
 
 
-def attend_kernel(pages_ref, q_ref, key_ref, value_ref, seq_ref, out_ref):
+def attend_kernel(pages_ref, q_ref, key_ref, value_ref, seq_ref, ow_ref, out_ref, ow_out, sem):
+    fetch = pltpu.make_async_copy(ow_ref, ow_out, sem)
+    fetch.start()
     scale = 1.0 / math.sqrt(HD)
     q = q_ref[...]
     n = GQ * ROWS
@@ -289,15 +367,22 @@
     for d in range(SECTIONS):
         for h in range(GQ):
             out_ref[d, :, h * HD : (h + 1) * HD] = mixed[h * ROWS : (h + 1) * ROWS]
-
-
-def attend(pages, q, key, value, seq):
+    fetch.wait()
+
+
+def attend(pages, q, key, value, seq, o_weight):
     return pl.pallas_call(
         attend_kernel,
-        out_shape=jax.ShapeDtypeStruct((SECTIONS, ROWS, WQ), BF16),
+        in_specs=[VMEM_SPEC] * 5 + [pl.BlockSpec(memory_space=pl.ANY)],
+        out_specs=[VMEM_SPEC] * 2,
+        out_shape=[
+            jax.ShapeDtypeStruct((SECTIONS, ROWS, WQ), BF16),
+            pltpu.VMEM(o_weight.shape, BF16),
+        ],
+        scratch_shapes=[pltpu.SemaphoreType.DMA(())],
         compiler_params=params(),
         name="attend",
-    )(pages, q, key, value, seq)
+    )(pages, q, key, value, seq, in_hbm(o_weight))
 
 
 def output_kernel(attn_ref, ow_ref, out_ref):
@@ -314,7 +399,7 @@
         ),
         compiler_params=params(),
         name="output_part",
-    )(attn, o_weight)
+    )(attn, kept(o_weight))
 
 
 def finish_kernel(_, got_ref, tok_ref, out_ref):
@@ -355,12 +440,19 @@
     gain_here = lax.dynamic_slice_in_dim(norm_gain, section * DEPTH, DEPTH, 0)
     cosine, sine = rotation_tables()
 
+    ids_wide = jnp.pad(own_ids.astype(F32), ((0, 0), (ID_LANE, EXTRA - ID_LANE - CAP)))
+    payload, order, turn, count = project(
+        own_ids, new_tokens.reshape(-1, DEPTH), gain_here[None, :], q_weight, kv_weight, ids_wide
+    )
+
     weight = (kv_weight.astype(F32) * gain_here[:, None]).astype(BF16)
     from_1 = shifted(weight, 0, 1)
     from_3 = shifted(weight, 0, -1)
     from_2 = shifted(weight, 0, 2)
     near = jnp.concatenate([weight, from_1], axis=0)
     far = jnp.concatenate([from_3, from_2], axis=0)
+    near, far, payload = lax.optimization_barrier((near, far, payload))
+    got = lax.all_to_all(payload, "section", split_axis=0, concat_axis=0, tiled=True)
     near_p = shifted(near, 1, 1)
     far_m = shifted(far, 1, -1)
     near_2, far_2 = lax.optimization_barrier((near, far))
@@ -378,34 +470,19 @@
             ids.append(jnp.where(core == 0, at_0, at_1))
         return jnp.stack(ids).astype(jnp.int32)
 
-    ids_wide = jnp.pad(
-        own_ids.astype(F32), ((0, 0), (ID_LANE, EXTRA - ID_LANE - CAP))
-    )
-    payload = project(
-        new_tokens.reshape(-1, DEPTH), gain_here[None, :], q_weight, kv_weight, ids_wide
-    )
-    got = lax.all_to_all(payload, "section", split_axis=0, concat_axis=0, tiled=True)
+    where = blocks(
+        (0, 0), (3, 0), (1, 0), (2, 0),
+        (0, 3), (3, 3), (1, 1), (2, 1),
+        (0, 1), (3, 1), (1, 3), (2, 3),
+        (0, 2), (3, 2), (1, 2), (2, 2),
+    )
+    early = prompt_early(where, order, count, prompt_rows, (near, far, near_p, far_m))
+    pages = prompt_late(
+        order, turn, count, cosine, sine, early, (near_m, far_p, near_o, far_o)
+    )
     queries, new_keys, new_values, owners = ready(context_len, got, cosine, sine)
-
-    carry = prompt_pass(
-        prompt_rows, blocks((0, 0), (3, 0), (1, 0), (2, 0)), near, far
-    )
-    carry = prompt_pass(
-        prompt_rows, blocks((0, 3), (3, 3), (1, 1), (2, 1)), near_p, far_m, carry
-    )
-    carry = prompt_pass(
-        prompt_rows, blocks((0, 1), (3, 1), (1, 3), (2, 3)), near_m, far_p, carry
-    )
-    pages = prompt_pass(
-        prompt_rows,
-        blocks((0, 2), (3, 2), (1, 2), (2, 2)),
-        near_o,
-        far_o,
-        carry,
-        (own_ids, cosine, sine),
-    )
     received = lax.all_to_all(pages, "section", split_axis=0, concat_axis=0, tiled=True)
-    attn = attend(received, queries, new_keys, new_values, owners)
+    attn, o_weight = attend(received, queries, new_keys, new_values, owners, o_weight)
     attn = lax.all_to_all(attn, "section", split_axis=0, concat_axis=0, tiled=True)
     part = output_part(attn, o_weight, members)
     part = lax.all_to_all(part, "tensor", split_axis=0, concat_axis=0, tiled=True)

time: 108 us -> 101 us (0.935)
  Pallas kernels: 31.3 us -> 25.5 us
  waiting for transfers between devices: 19.3 us -> 17.4 us
  starting transfers between devices: 28.5 us -> 26.8 us
  local copies, waits for them, and re-layouts: 1.16 us -> 2.73 us
    pallas_call x6 -> x4, Pallas kernels: 28.8 us -> 23.6 us  [the longest x1 12.8 us: prompt_early(): pl.pallas_call(functools.partial(early_kernel, n_early), in_specs=[SMEM_S...]
    ppermute x9, waiting for transfers between devices: 6.29 us -> 3.75 us  [shifted(): return lax.ppermute(array, ('section', 'tensor'), pairs)]
    all_to_all x1, starting transfers between devices: 7.03 us -> 4.78 us  [on_device(): lax.all_to_all(pages, 'section', split_axis=0, concat_axis=0, tiled=True)]
    ppermute x9, starting transfers between devices: 15.4 us -> 17 us  [shifted(): return lax.ppermute(array, ('section', 'tensor'), pairs)]
  transfers between devices with their start and end apart: 11 -> 11, of which waited for: 3 -> 3; matrix products, arithmetic and copies ran while one was open for 1% -> 2% of each run, Pallas kernels for 27% -> 23%
where the time goes in v2:
time: 101 us; the launch traced here: 99.9 us
  starting transfers between devices  26.8 us (27%)
  Pallas kernels  25.5 us (25%)
  blocking collectives  24.8 us (25%)
  waiting for transfers between devices  17.4 us (17%)
  local copies, waits for them, and re-layouts  2.73 us (3%)
  other arithmetic  2.29 us (2%)
    ppermute x9, starting transfers between devices, shifted(): return lax.ppermute(array, ('section', 'tensor'), pairs)  17 us
    all_to_all x1, waiting for transfers between devices, on_device(): lax.all_to_all(pages, 'section', split_axis=0, concat_axis=0, tiled=True)  13.7 us
    all_to_all x1, blocking collectives, on_device(): lax.all_to_all(attn, 'section', split_axis=0, concat_axis=0, tiled=True)  13 us
    pallas_call x1, Pallas kernels, prompt_early(): pl.pallas_call(functools.partial(early_kernel, n_early), in_specs=[SMEM_S...  12.8 us
    all_to_all x1, blocking collectives, on_device(): lax.all_to_all(part, 'tensor', split_axis=0, concat_axis=0, tiled=True)  11.8 us
    pallas_call x1, Pallas kernels, prompt_late(): pl.pallas_call(late_kernel, in_specs=[SMEM_SPEC] * 3 + [VMEM_SPEC] * (5 +...  6.58 us
    all_to_all x1, starting transfers between devices, on_device(): lax.all_to_all(payload, 'section', split_axis=0, concat_axis=0, tiled=True)  5.02 us
    all_to_all x1, starting transfers between devices, on_device(): lax.all_to_all(pages, 'section', split_axis=0, concat_axis=0, tiled=True)  4.78 us
  transfers between devices with their start and end apart: 11, of which 3 were waited for; matrix products, arithmetic and copies ran while one was open for 2% of the time, Pallas kernels for 23%

profile of v2, /device:TPU:0, one launch (start us, length us, event | category | flops | bytes accessed | tf_op | source)
XLA Modules:
  0.0 99.9 jit_solution(8359232222479906946)
XLA Ops:
  0.0 0.8 dynamic_slice.3
  0.8 1.1 %multiply_convert_fusion = bf16[512,256]{1,0:T(8,128)(2,1)S(1)} fusion(bf16[512,256]{1,0:T(8,128)(2,1)} %kvw_ref.1, f32[512]{0:T(512)S(1)} %dynamic_slice.3), kind=kLoop, calls=%fused_computation.2 | loop fusion | flops 393216 | bytes 526336 | tf_op jit(solution)/shard_map/convert_element_type | solution.py:448
  1.8 1.6 %collective-permute-start = (bf16[512,256]{1,0:T(8,128)(2,1)S(1)}, bf16[512,256]{1,0:T(8,128)(2,1)S(1)}, u32[]{:S(2)}, u32[]{:S(2)}) collective-permute-start(bf16[512,256]{1,0:T(8,128)(2,1)S(1)} %multiply_convert_fusion), channel_id=1, source_target_pairs={{0,8},{1,33},{2,10},{3,35},{4,12},{5,37},{6,14},{7,39},{8,16},{9,4... | collective-permute-start | bytes 786440 | tf_op jit(solution)/shard_map/ppermute | solution.py:61
  3.5 1.7 %collective-permute-start.1 = (bf16[512,256]{1,0:T(8,128)(2,1)S(1)}, bf16[512,256]{1,0:T(8,128)(2,1)S(1)}, u32[]{:S(2)}, u32[]{:S(2)}) collective-permute-start(bf16[512,256]{1,0:T(8,128)(2,1)S(1)} %multiply_convert_fusion), channel_id=1, source_target_pairs={{0,24},{1,97},{2,26},{3,99},{4,28},{5,101},{6,30},{7,103},{8,0},{9... | collective-permute-start | bytes 786440 | tf_op jit(solution)/shard_map/ppermute | solution.py:61
  5.2 1.9 %collective-permute-start.2 = (bf16[512,256]{1,0:T(8,128)(2,1)S(1)}, bf16[512,256]{1,0:T(8,128)(2,1)S(1)}, u32[]{:S(2)}, u32[]{:S(2)}) collective-permute-start(bf16[512,256]{1,0:T(8,128)(2,1)S(1)} %multiply_convert_fusion), channel_id=1, source_target_pairs={{0,16},{1,65},{2,18},{3,67},{4,20},{5,69},{6,22},{7,71},{8,24},{9,... | collective-permute-start | bytes 786440 | tf_op jit(solution)/shard_map/ppermute | solution.py:61
  7.8 0.8 copy.12.slot_ref
  8.6 0.9 copy-done.1
  9.6 2.9 %project.1 = (bf16[16,16,1408]{2,1,0:T(8,128)(2,1)}, s32[128]{0:T(128)S(1)}, s32[128]{0:T(128)S(1)}, s32[1]{0:T(128)}) custom-call(s32[16,8]{1,0:T(8,128)S(1)} %copy.12.slot_ref, bf16[256,512]{1,0:T(8,128)(2,1)} %bitcast.21, f32[1,512]{1,0:T(1,128)S(1)} %bitcast.22, bf16[512,1024]{1,0:T(8,128)(2,1)} %qw_ref.1, bf16[512,256]{1,0:T(8,128)(2,1)S(1)} %copy-done.1, ...), custom_call_target="tpu_custom_call" | custom-call | tf_op jit(solution)/shard_map/project/pallas_call | solution.py:255
  12.5 0.8 collective-permute-done.2
  13.4 2.0 %collective-permute-start.3 = (bf16[1024,256]{1,0:T(8,128)(2,1)S(1)}, bf16[1024,256]{1,0:T(8,128)(2,1)S(1)}, u32[]{:S(2)}, u32[]{:S(2)}) collective-permute-start(bf16[1024,256]{1,0:T(8,128)(2,1)S(1)} %pad_maximum_fusion.refs_0_), channel_id=1, source_target_pairs={{0,32},{1,9},{2,34},{3,11},{4,36},{5,13},{6,38},{7,15},{8,40},{9,1... | collective-permute-start | bytes 1572872 | tf_op jit(solution)/shard_map/ppermute | solution.py:61
  15.4 2.2 %collective-permute-start.4 = (bf16[1024,256]{1,0:T(8,128)(2,1)S(1)}, bf16[1024,256]{1,0:T(8,128)(2,1)}, u32[]{:S(2)}, u32[]{:S(2)}) collective-permute-start(bf16[1024,256]{1,0:T(8,128)(2,1)S(1)} %pad_maximum_fusion.1.refs_1_), channel_id=1, source_target_pairs={{0,96},{1,25},{2,98},{3,27},{4,100},{5,29},{6,102},{7,31},{8,104},... | collective-permute-start | bytes 1572872 | tf_op jit(solution)/shard_map/ppermute | solution.py:61
  17.6 5.0 %all-to-all-start.1 = ((bf16[16,16,1408]{2,1,0:T(8,128)(2,1)}), bf16[16,16,1408]{2,1,0:T(8,128)(2,1)S(1)}, u32[]{:S(2)}, u32[]{:S(2)}) async-start(bf16[16,16,1408]{2,1,0:T(8,128)(2,1)} %get-tuple-element.34), calls=%async_computation.1 | async-start | bytes 1441792 | tf_op jit(solution)/shard_map/all_to_all | solution.py:455
  22.9 3.0 %collective-permute-start.5 = (bf16[1024,256]{1,0:T(8,128)(2,1)S(1)}, bf16[1024,256]{1,0:T(8,128)(2,1)S(1)}, u32[]{:S(2)}, u32[]{:S(2)}) collective-permute-start(bf16[1024,256]{1,0:T(8,128)(2,1)S(1)} %pad_maximum_fusion.refs_0_), channel_id=1, source_target_pairs={{0,96},{1,25},{2,98},{3,27},{4,100},{5,29},{6,102},{7,31},{8,104},... | collective-permute-start | bytes 1572872 | tf_op jit(solution)/shard_map/ppermute | solution.py:61
  25.9 0.8 collective-permute-start.7
  26.8 2.9 %collective-permute-done.4.refs_3_ = bf16[1024,256]{1,0:T(8,128)(2,1)} collective-permute-done((bf16[1024,256]{1,0:T(8,128)(2,1)S(1)}, bf16[1024,256]{1,0:T(8,128)(2,1)}, u32[]{:S(2)}, u32[]{:S(2)}) %collective-permute-start.4) | collective-permute-done | bytes 524320 | tf_op jit(solution)/shard_map/ppermute | solution.py:61
  29.6 3.8 %collective-permute-start.8 = (bf16[1024,256]{1,0:T(8,128)(2,1)}, bf16[1024,256]{1,0:T(8,128)(2,1)S(1)}, u32[]{:S(2)}, u32[]{:S(2)}) collective-permute-start(bf16[1024,256]{1,0:T(8,128)(2,1)} %collective-permute-done.4.refs_3_), channel_id=1, source_target_pairs={{0,96},{1,25},{2,98},{3,27},{4,100},{5,29},{6,102},{7,31},{8,104},... | collective-permute-start | bytes 1572872 | tf_op jit(solution)/shard_map/ppermute | solution.py:61
  33.9 12.8 %prompt_early.1 = (f32[2048,256]{1,0:T(8,128)S(1)}, bf16[2048,4096]{1,0:T(8,128)(2,1)S(1)}, f32[2048,128]{1,0:T(8,128)S(1)}) custom-call(s32[16]{0:T(128)S(1)} %stack.67.blocks_ref, s32[128]{0:T(128)S(1)} %get-tuple-element.23.order_ref, s32[1]{0:T(128)} %get-tuple-element.25.count_ref, bf16[2048,8192]{1,0:T(8,128)(2,1)} %x_ref.1, ...), custom_call_target="tpu_custom_call" | custom-call | tf_op jit(solution)/shard_map/prompt_early/pallas_call | solution.py:147
  46.8 6.6 %prompt_late.1 = bf16[16,128,256]{2,1,0:T(8,128)(2,1)} custom-call(s32[128]{0:T(128)S(1)} %get-tuple-element.23.order_ref, s32[128]{0:T(128)S(1)} %get-tuple-element.24.turn_ref, s32[1]{0:T(128)} %get-tuple-element.25.count_ref, f32[136,128]{1,0:T(8,128)S(1)} %get-tuple-element.44.cos_ref, f32[136,128]{1,0:T(8,128)S(1)} %get-tuple-element.45.sin_ref, ...), custom_call_target="tpu_custom_call" | custom-call | tf_op jit(solution)/shard_map/prompt_late/pallas_call | solution.py:202
  53.3 4.8 %all-to-all-start = ((bf16[16,128,256]{2,1,0:T(8,128)(2,1)}), bf16[16,128,256]{2,1,0:T(8,128)(2,1)S(1)}, u32[]{:S(2)}, u32[]{:S(2)}) async-start(bf16[16,128,256]{2,1,0:T(8,128)(2,1)} %prompt_late.1), calls=%async_computation | async-start | bytes 2097152 | tf_op jit(solution)/shard_map/all_to_all | solution.py:484
  58.1 0.8 ready.1
  58.9 13.7 %all-to-all-done.pages_ref = bf16[16,128,256]{2,1,0:T(8,128)(2,1)S(1)} async-done(((bf16[16,128,256]{2,1,0:T(8,128)(2,1)}), bf16[16,128,256]{2,1,0:T(8,128)(2,1)S(1)}, u32[]{:S(2)}, u32[]{:S(2)}) %all-to-all-start) | async-done | bytes 1048608 | tf_op jit(solution)/shard_map/all_to_all | solution.py:484
  72.6 1.4 %attend.1 = (bf16[16,16,1024]{2,1,0:T(8,128)(2,1)S(1)}, bf16[1024,512]{1,0:T(8,128)(2,1)S(1)}) custom-call(bf16[16,128,256]{2,1,0:T(8,128)(2,1)S(1)} %all-to-all-done.pages_ref, bf16[128,128]{1,0:T(8,128)(2,1)S(1)} %get-tuple-element.35.q_ref, bf16[16,128]{1,0:T(8,128)(2,1)S(1)} %get-tuple-element.36.key_ref, ...), custom_call_target="tpu_custom_call" | custom-call | tf_op jit(solution)/shard_map/attend/pallas_call | solution.py:374
  74.0 13.0 %all_to_all.20.attn_ref = bf16[16,16,1024]{2,1,0:T(8,128)(2,1)S(1)} all-to-all(bf16[16,16,1024]{2,1,0:T(8,128)(2,1)S(1)} %get-tuple-element.39), channel_id=1, replica_groups=mesh['section'=16,'tensor'=8] {'section'}, dimensions={0} | all-to-all | bytes 1048576 | tf_op jit(solution)/shard_map/all_to_all | solution.py:486
  87.4 11.8 %all_to_all.21.got_ref = bf16[8,32,512]{2,1,0:T(8,128)(2,1)S(1)} all-to-all(bf16[8,32,512]{2,1,0:T(8,128)(2,1)S(1)} %output_part.1), channel_id=1, replica_groups=mesh['section'=16,'tensor'=8] {'tensor'}, dimensions={0} | all-to-all | bytes 524288 | tf_op jit(solution)/shard_map/all_to_all | solution.py:488
  (26 shorter events, 2.6 us)
Async XLA Ops:
  1.8 10.6 %collective-permute-start = (bf16[512,256]{1,0:T(8,128)(2,1)S(1)}, bf16[512,256]{1,0:T(8,128)(2,1)S(1)}, u32[]{:S(2)}, u32[]{:S(2)}) collective-permute-start(bf16[512,256]{1,0:T(8,128)(2,1)S(1)} %multiply_convert_fusion), channel_id=1, source_target_pairs={{0,8},{1,33},{2,10},{3,35},{4,12},{5,37},{6,14},{7,39},{8,16},{9,4... | collective-permute-start | bytes 786440 | tf_op jit(solution)/shard_map/ppermute | solution.py:61
  3.5 9.0 %collective-permute-start.1 = (bf16[512,256]{1,0:T(8,128)(2,1)S(1)}, bf16[512,256]{1,0:T(8,128)(2,1)S(1)}, u32[]{:S(2)}, u32[]{:S(2)}) collective-permute-start(bf16[512,256]{1,0:T(8,128)(2,1)S(1)} %multiply_convert_fusion), channel_id=1, source_target_pairs={{0,24},{1,97},{2,26},{3,99},{4,28},{5,101},{6,30},{7,103},{8,0},{9... | collective-permute-start | bytes 786440 | tf_op jit(solution)/shard_map/ppermute | solution.py:61
  5.2 8.2 %collective-permute-start.2 = (bf16[512,256]{1,0:T(8,128)(2,1)S(1)}, bf16[512,256]{1,0:T(8,128)(2,1)S(1)}, u32[]{:S(2)}, u32[]{:S(2)}) collective-permute-start(bf16[512,256]{1,0:T(8,128)(2,1)S(1)} %multiply_convert_fusion), channel_id=1, source_target_pairs={{0,16},{1,65},{2,18},{3,67},{4,20},{5,69},{6,22},{7,71},{8,24},{9,... | collective-permute-start | bytes 786440 | tf_op jit(solution)/shard_map/ppermute | solution.py:61
  8.6 1.0 copy-start.1
  13.4 12.5 %collective-permute-start.3 = (bf16[1024,256]{1,0:T(8,128)(2,1)S(1)}, bf16[1024,256]{1,0:T(8,128)(2,1)S(1)}, u32[]{:S(2)}, u32[]{:S(2)}) collective-permute-start(bf16[1024,256]{1,0:T(8,128)(2,1)S(1)} %pad_maximum_fusion.refs_0_), channel_id=1, source_target_pairs={{0,32},{1,9},{2,34},{3,11},{4,36},{5,13},{6,38},{7,15},{8,40},{9,1... | collective-permute-start | bytes 1572872 | tf_op jit(solution)/shard_map/ppermute | solution.py:61
  15.4 14.2 %collective-permute-start.4 = (bf16[1024,256]{1,0:T(8,128)(2,1)S(1)}, bf16[1024,256]{1,0:T(8,128)(2,1)}, u32[]{:S(2)}, u32[]{:S(2)}) collective-permute-start(bf16[1024,256]{1,0:T(8,128)(2,1)S(1)} %pad_maximum_fusion.1.refs_1_), channel_id=1, source_target_pairs={{0,96},{1,25},{2,98},{3,27},{4,100},{5,29},{6,102},{7,31},{8,104},... | collective-permute-start | bytes 1572872 | tf_op jit(solution)/shard_map/ppermute | solution.py:61
  17.6 35.7 %all-to-all-start.1 = ((bf16[16,16,1408]{2,1,0:T(8,128)(2,1)}), bf16[16,16,1408]{2,1,0:T(8,128)(2,1)S(1)}, u32[]{:S(2)}, u32[]{:S(2)}) async-start(bf16[16,16,1408]{2,1,0:T(8,128)(2,1)} %get-tuple-element.34), calls=%async_computation.1 | async-start | bytes 1441792 | tf_op jit(solution)/shard_map/all_to_all | solution.py:455
  22.9 23.8 %collective-permute-start.5 = (bf16[1024,256]{1,0:T(8,128)(2,1)S(1)}, bf16[1024,256]{1,0:T(8,128)(2,1)S(1)}, u32[]{:S(2)}, u32[]{:S(2)}) collective-permute-start(bf16[1024,256]{1,0:T(8,128)(2,1)S(1)} %pad_maximum_fusion.refs_0_), channel_id=1, source_target_pairs={{0,96},{1,25},{2,98},{3,27},{4,100},{5,29},{6,102},{7,31},{8,104},... | collective-permute-start | bytes 1572872 | tf_op jit(solution)/shard_map/ppermute | solution.py:61
  25.9 20.8 %collective-permute-start.6 = (bf16[1024,256]{1,0:T(8,128)(2,1)S(1)}, bf16[1024,256]{1,0:T(8,128)(2,1)S(1)}, u32[]{:S(2)}, u32[]{:S(2)}) collective-permute-start(bf16[1024,256]{1,0:T(8,128)(2,1)S(1)} %pad_maximum_fusion.1.refs_1_), channel_id=1, source_target_pairs={{0,32},{1,9},{2,34},{3,11},{4,36},{5,13},{6,38},{7,15},{8,40},{9,1... | collective-permute-start | bytes 1572872 | tf_op jit(solution)/shard_map/ppermute | solution.py:61
  25.9 20.8 %collective-permute-start.7 = (bf16[1024,256]{1,0:T(8,128)(2,1)S(1)}, bf16[1024,256]{1,0:T(8,128)(2,1)S(1)}, u32[]{:S(2)}, u32[]{:S(2)}) collective-permute-start(bf16[1024,256]{1,0:T(8,128)(2,1)S(1)} %collective-permute-done.3.refs_2_), channel_id=1, source_target_pairs={{0,32},{1,9},{2,34},{3,11},{4,36},{5,13},{6,38},{7,15},{8,40},{9,1... | collective-permute-start | bytes 1572872 | tf_op jit(solution)/shard_map/ppermute | solution.py:61
  29.6 17.1 %collective-permute-start.8 = (bf16[1024,256]{1,0:T(8,128)(2,1)}, bf16[1024,256]{1,0:T(8,128)(2,1)S(1)}, u32[]{:S(2)}, u32[]{:S(2)}) collective-permute-start(bf16[1024,256]{1,0:T(8,128)(2,1)} %collective-permute-done.4.refs_3_), channel_id=1, source_target_pairs={{0,96},{1,25},{2,98},{3,27},{4,100},{5,29},{6,102},{7,31},{8,104},... | collective-permute-start | bytes 1572872 | tf_op jit(solution)/shard_map/ppermute | solution.py:61
  46.7 11.4 %copy-start.2 = (s32[8]{0:T(128)S(1)}, s32[8]{0:T(128)}, u32[]{:S(2)}) copy-start(s32[8]{0:T(128)} %ctx_ref.1) | copy-start | bytes 100
  46.7 52.5 %copy-start = (bf16[2,128,512]{2,1,0:T(8,128)(2,1)S(1)}, bf16[2,128,512]{2,1,0:T(8,128)(2,1)}, u32[]{:S(2)}) copy-start(bf16[2,128,512]{2,1,0:T(8,128)(2,1)} %tok_ref.1) | copy-start | bytes 786436
  53.3 19.3 %all-to-all-start = ((bf16[16,128,256]{2,1,0:T(8,128)(2,1)}), bf16[16,128,256]{2,1,0:T(8,128)(2,1)S(1)}, u32[]{:S(2)}, u32[]{:S(2)}) async-start(bf16[16,128,256]{2,1,0:T(8,128)(2,1)} %prompt_late.1), calls=%async_computation | async-start | bytes 2097152 | tf_op jit(solution)/shard_map/all_to_all | solution.py:484

commit v3 on v2

--- a/solution.py
+++ b/solution.py
@@ -385,25 +385,56 @@
     )(pages, q, key, value, seq, in_hbm(o_weight))
 
 
-def output_kernel(attn_ref, ow_ref, out_ref):
+def output_kernel(attn_ref, ow_ref, mine_ref, other_ref, total_ref):
+    core = lax.axis_index("tensor") % 2
     attn = attn_ref[...].reshape(SECTIONS * ROWS, WQ)
     part = jnp.dot(attn, ow_ref[...], preferred_element_type=F32)
-    out_ref[...] = part.astype(BF16).reshape(out_ref.shape)
-
-
-def output_part(attn, o_weight, members):
+    total_ref[...] = part.reshape(total_ref.shape)
+    for chip in range(4):
+        mine_ref[chip] = total_ref[2 * chip + core]
+        other_ref[chip] = total_ref[2 * chip + 1 - core].astype(BF16)
+
+
+def output_part(attn, o_weight):
+    width = o_weight.shape[1]
+    half = (4, 2 * ROWS, width)
     return pl.pallas_call(
         output_kernel,
-        out_shape=jax.ShapeDtypeStruct(
-            (members, SECTIONS * ROWS // members, o_weight.shape[1]), BF16
-        ),
+        out_shape=[jax.ShapeDtypeStruct(half, F32), jax.ShapeDtypeStruct(half, BF16)],
+        scratch_shapes=[pltpu.VMEM((8, 2 * ROWS, width), F32)],
         compiler_params=params(),
         name="output_part",
     )(attn, kept(o_weight))
 
 
-def finish_kernel(_, got_ref, tok_ref, out_ref):
-    total = jnp.sum(got_ref[...].astype(F32), axis=0)
+CHIP_STEPS = (1, 3, 2)
+
+
+def pair_kernel(mine_ref, got_ref, own_ref, *out_refs):
+    chip = lax.axis_index("tensor") // 2
+
+    def pair(at):
+        return mine_ref[at] + got_ref[at].astype(F32)
+
+    own_ref[...] = pair(chip)
+    for step, out_ref in zip(CHIP_STEPS, out_refs):
+        out_ref[...] = pair((chip + step) % 4).astype(BF16)
+
+
+def pair_sums(mine, got):
+    piece = mine.shape[1:]
+    return pl.pallas_call(
+        pair_kernel,
+        out_shape=[jax.ShapeDtypeStruct(piece, F32)] + [jax.ShapeDtypeStruct(piece, BF16)] * 3,
+        compiler_params=params(),
+        name="pair_sums",
+    )(mine, got)
+
+
+def finish_kernel(_, own_ref, a_ref, b_ref, c_ref, tok_ref, out_ref):
+    total = own_ref[...]
+    for got_ref in (a_ref, b_ref, c_ref):
+        total = total + got_ref[...].astype(F32)
     tok = tok_ref[...].astype(F32)
     for i in range(2):
         rows = jnp.concatenate(
@@ -412,21 +443,22 @@
         out_ref[i] = (tok[i] + rows).astype(BF16)
 
 
-def finish(member, got, tokens):
-    members, rows, width = got.shape
+def finish(member, own, got, tokens):
+    rows, width = own.shape
     block = pl.BlockSpec((2, rows // 2, width), lambda r, member: (0, member[0], 0))
+    whole = pl.BlockSpec((rows, width), lambda r, member: (0, 0))
     return pl.pallas_call(
         finish_kernel,
         grid_spec=pltpu.PrefetchScalarGridSpec(
             num_scalar_prefetch=1,
             grid=(1,),
-            in_specs=[pl.BlockSpec(got.shape, lambda r, member: (0, 0, 0)), block],
+            in_specs=[whole] * 4 + [block],
             out_specs=pl.BlockSpec((2, rows // 2, width), lambda r, member: (0, 0, 0)),
         ),
         out_shape=jax.ShapeDtypeStruct((2, rows // 2, width), BF16),
         compiler_params=params(),
         name="finish",
-    )(member, got, tokens)
+    )(member, own, *got, tokens)
 
 
 def on_device(
@@ -434,7 +466,6 @@
 ):
     section = lax.axis_index("section")
     member = lax.axis_index("tensor")
-    members = lax.axis_size("tensor")
     core = member % 2
     own_ids = page_slot[0]
     gain_here = lax.dynamic_slice_in_dim(norm_gain, section * DEPTH, DEPTH, 0)
@@ -484,9 +515,14 @@
     received = lax.all_to_all(pages, "section", split_axis=0, concat_axis=0, tiled=True)
     attn, o_weight = attend(received, queries, new_keys, new_values, owners, o_weight)
     attn = lax.all_to_all(attn, "section", split_axis=0, concat_axis=0, tiled=True)
-    part = output_part(attn, o_weight, members)
-    part = lax.all_to_all(part, "tensor", split_axis=0, concat_axis=0, tiled=True)
-    return finish(member[None].astype(jnp.int32), part, new_tokens)
+    mine, other = output_part(attn, o_weight)
+    other = lax.ppermute(other, "tensor", [(t, t ^ 1) for t in range(8)])
+    own, *pieces = pair_sums(mine, other)
+    got = [
+        lax.ppermute(piece, "tensor", [(t, (t + 2 * step) % 8) for t in range(8)])
+        for step, piece in zip(CHIP_STEPS, pieces)
+    ]
+    return finish(member[None].astype(jnp.int32), own, got, new_tokens)
 
 
 def solution(mesh):

time: 101 us -> 99.3 us (0.983)
  blocking collectives: 24.8 us -> 13 us
  starting transfers between devices: 26.8 us -> 34.7 us
  waiting for transfers between devices: 17.4 us -> 22.8 us
  Pallas kernels: 25.5 us -> 23 us
    all_to_all x1 -> x0, blocking collectives: 11.8 us -> none  [on_device(): lax.all_to_all(part, 'tensor', split_axis=0, concat_axis=0, tiled=True)]
    ppermute x0 -> x4, starting transfers between devices: none -> 5.37 us  [the longest x3 5.28 us: on_device(): lax.ppermute(piece, 'tensor', [(t, (t + 2 * step) % 8) for t in range(8)])]
    ppermute x0 -> x4, waiting for transfers between devices: none -> 4.77 us  [the longest x3 3.44 us: on_device(): lax.ppermute(piece, 'tensor', [(t, (t + 2 * step) % 8) for t in range(8)])]
    all_to_all x1, starting transfers between devices: 4.78 us -> 7.36 us  [on_device(): lax.all_to_all(pages, 'section', split_axis=0, concat_axis=0, tiled=True)]
    pallas_call x1, Pallas kernels: 12.8 us -> 11.1 us  [prompt_early(): pl.pallas_call(functools.partial(early_kernel, n_early), in_specs=[SMEM_S...]
  transfers between devices with their start and end apart: 11 -> 15, of which waited for: 3 -> 6; matrix products, arithmetic and copies ran while one was open for 2% -> 2% of each run, Pallas kernels for 23% -> 21%
where the time goes in v3:
time: 99.3 us; the launch traced here: 98.8 us
  starting transfers between devices  34.7 us (35%)
  Pallas kernels  23 us (23%)
  waiting for transfers between devices  22.8 us (23%)
  blocking collectives  13 us (13%)
  local copies, waits for them, and re-layouts  2.73 us (3%)
  other arithmetic  2.29 us (2%)
    ppermute x9, starting transfers between devices, shifted(): return lax.ppermute(array, ('section', 'tensor'), pairs)  17 us
    all_to_all x1, waiting for transfers between devices, on_device(): lax.all_to_all(pages, 'section', split_axis=0, concat_axis=0, tiled=True)  14.2 us
    all_to_all x1, blocking collectives, on_device(): lax.all_to_all(attn, 'section', split_axis=0, concat_axis=0, tiled=True)  13 us
    pallas_call x1, Pallas kernels, prompt_early(): pl.pallas_call(functools.partial(early_kernel, n_early), in_specs=[SMEM_S...  11.1 us
    all_to_all x1, starting transfers between devices, on_device(): lax.all_to_all(pages, 'section', split_axis=0, concat_axis=0, tiled=True)  7.36 us
    pallas_call x1, Pallas kernels, prompt_late(): pl.pallas_call(late_kernel, in_specs=[SMEM_SPEC] * 3 + [VMEM_SPEC] * (5 +...  5.74 us
    ppermute x3, starting transfers between devices, on_device(): lax.ppermute(piece, 'tensor', [(t, (t + 2 * step) % 8) for t in range(8)])  5.28 us
    all_to_all x1, starting transfers between devices, on_device(): lax.all_to_all(payload, 'section', split_axis=0, concat_axis=0, tiled=True)  5.02 us
  transfers between devices with their start and end apart: 15, of which 6 were waited for; matrix products, arithmetic and copies ran while one was open for 2% of the time, Pallas kernels for 21%

profile of v3, /device:TPU:0, one launch (start us, length us, event | category | flops | bytes accessed | tf_op | source)
XLA Modules:
  0.0 98.8 jit_solution(18196304260508798668)
XLA Ops:
  0.8 1.1 %multiply_convert_fusion = bf16[512,256]{1,0:T(8,128)(2,1)S(1)} fusion(bf16[512,256]{1,0:T(8,128)(2,1)} %kvw_ref.1, f32[512]{0:T(512)S(1)} %dynamic_slice.3), kind=kLoop, calls=%fused_computation.2 | loop fusion | flops 393216 | bytes 526336 | tf_op jit(solution)/shard_map/convert_element_type | solution.py:479
  1.8 1.6 %collective-permute-start = (bf16[512,256]{1,0:T(8,128)(2,1)S(1)}, bf16[512,256]{1,0:T(8,128)(2,1)S(1)}, u32[]{:S(2)}, u32[]{:S(2)}) collective-permute-start(bf16[512,256]{1,0:T(8,128)(2,1)S(1)} %multiply_convert_fusion), channel_id=1, source_target_pairs={{0,8},{1,33},{2,10},{3,35},{4,12},{5,37},{6,14},{7,39},{8,16},{9,4... | collective-permute-start | bytes 786440 | tf_op jit(solution)/shard_map/ppermute | solution.py:61
  3.5 1.7 %collective-permute-start.1 = (bf16[512,256]{1,0:T(8,128)(2,1)S(1)}, bf16[512,256]{1,0:T(8,128)(2,1)S(1)}, u32[]{:S(2)}, u32[]{:S(2)}) collective-permute-start(bf16[512,256]{1,0:T(8,128)(2,1)S(1)} %multiply_convert_fusion), channel_id=1, source_target_pairs={{0,24},{1,97},{2,26},{3,99},{4,28},{5,101},{6,30},{7,103},{8,0},{9... | collective-permute-start | bytes 786440 | tf_op jit(solution)/shard_map/ppermute | solution.py:61
  5.2 1.9 %collective-permute-start.2 = (bf16[512,256]{1,0:T(8,128)(2,1)S(1)}, bf16[512,256]{1,0:T(8,128)(2,1)S(1)}, u32[]{:S(2)}, u32[]{:S(2)}) collective-permute-start(bf16[512,256]{1,0:T(8,128)(2,1)S(1)} %multiply_convert_fusion), channel_id=1, source_target_pairs={{0,16},{1,65},{2,18},{3,67},{4,20},{5,69},{6,22},{7,71},{8,24},{9,... | collective-permute-start | bytes 786440 | tf_op jit(solution)/shard_map/ppermute | solution.py:61
  8.6 0.9 copy-done
  9.6 2.9 %project.1 = (bf16[16,16,1408]{2,1,0:T(8,128)(2,1)}, s32[128]{0:T(128)S(1)}, s32[128]{0:T(128)S(1)}, s32[1]{0:T(128)}) custom-call(s32[16,8]{1,0:T(8,128)S(1)} %copy.12.slot_ref, bf16[256,512]{1,0:T(8,128)(2,1)} %bitcast.21, f32[1,512]{1,0:T(1,128)S(1)} %bitcast.22, bf16[512,1024]{1,0:T(8,128)(2,1)} %qw_ref.1, bf16[512,256]{1,0:T(8,128)(2,1)S(1)} %copy-done, ...), custom_call_target="tpu_custom_call" | custom-call | tf_op jit(solution)/shard_map/project/pallas_call | solution.py:255
  12.5 0.8 collective-permute-done.2
  13.4 2.0 %collective-permute-start.3 = (bf16[1024,256]{1,0:T(8,128)(2,1)S(1)}, bf16[1024,256]{1,0:T(8,128)(2,1)S(1)}, u32[]{:S(2)}, u32[]{:S(2)}) collective-permute-start(bf16[1024,256]{1,0:T(8,128)(2,1)S(1)} %pad_maximum_fusion.refs_0_), channel_id=1, source_target_pairs={{0,32},{1,9},{2,34},{3,11},{4,36},{5,13},{6,38},{7,15},{8,40},{9,1... | collective-permute-start | bytes 1572872 | tf_op jit(solution)/shard_map/ppermute | solution.py:61
  15.4 2.2 %collective-permute-start.4 = (bf16[1024,256]{1,0:T(8,128)(2,1)S(1)}, bf16[1024,256]{1,0:T(8,128)(2,1)}, u32[]{:S(2)}, u32[]{:S(2)}) collective-permute-start(bf16[1024,256]{1,0:T(8,128)(2,1)S(1)} %pad_maximum_fusion.1.refs_1_), channel_id=1, source_target_pairs={{0,96},{1,25},{2,98},{3,27},{4,100},{5,29},{6,102},{7,31},{8,104},... | collective-permute-start | bytes 1572872 | tf_op jit(solution)/shard_map/ppermute | solution.py:61
  17.6 5.0 %all-to-all-start.1 = ((bf16[16,16,1408]{2,1,0:T(8,128)(2,1)}), bf16[16,16,1408]{2,1,0:T(8,128)(2,1)S(1)}, u32[]{:S(2)}, u32[]{:S(2)}) async-start(bf16[16,16,1408]{2,1,0:T(8,128)(2,1)} %get-tuple-element.40), calls=%async_computation.1 | async-start | bytes 1441792 | tf_op jit(solution)/shard_map/all_to_all | solution.py:486
  22.9 3.0 %collective-permute-start.5 = (bf16[1024,256]{1,0:T(8,128)(2,1)S(1)}, bf16[1024,256]{1,0:T(8,128)(2,1)S(1)}, u32[]{:S(2)}, u32[]{:S(2)}) collective-permute-start(bf16[1024,256]{1,0:T(8,128)(2,1)S(1)} %pad_maximum_fusion.refs_0_), channel_id=1, source_target_pairs={{0,96},{1,25},{2,98},{3,27},{4,100},{5,29},{6,102},{7,31},{8,104},... | collective-permute-start | bytes 1572872 | tf_op jit(solution)/shard_map/ppermute | solution.py:61
  26.8 2.9 %collective-permute-done.4.refs_3_ = bf16[1024,256]{1,0:T(8,128)(2,1)} collective-permute-done((bf16[1024,256]{1,0:T(8,128)(2,1)S(1)}, bf16[1024,256]{1,0:T(8,128)(2,1)}, u32[]{:S(2)}, u32[]{:S(2)}) %collective-permute-start.4) | collective-permute-done | bytes 524320 | tf_op jit(solution)/shard_map/ppermute | solution.py:61
  29.6 3.8 %collective-permute-start.8 = (bf16[1024,256]{1,0:T(8,128)(2,1)}, bf16[1024,256]{1,0:T(8,128)(2,1)S(1)}, u32[]{:S(2)}, u32[]{:S(2)}) collective-permute-start(bf16[1024,256]{1,0:T(8,128)(2,1)} %collective-permute-done.4.refs_3_), channel_id=1, source_target_pairs={{0,96},{1,25},{2,98},{3,27},{4,100},{5,29},{6,102},{7,31},{8,104},... | collective-permute-start | bytes 1572872 | tf_op jit(solution)/shard_map/ppermute | solution.py:61
  33.9 11.1 %prompt_early.1 = (f32[2048,256]{1,0:T(8,128)S(1)}, bf16[2048,4096]{1,0:T(8,128)(2,1)S(1)}, f32[2048,128]{1,0:T(8,128)S(1)}) custom-call(s32[16]{0:T(128)S(1)} %stack.67.blocks_ref, s32[128]{0:T(128)S(1)} %get-tuple-element.29.order_ref, s32[1]{0:T(128)} %get-tuple-element.31.count_ref, bf16[2048,8192]{1,0:T(8,128)(2,1)} %x_ref.1, ...), custom_call_target="tpu_custom_call" | custom-call | tf_op jit(solution)/shard_map/prompt_early/pallas_call | solution.py:147
  45.0 5.7 %prompt_late.1 = bf16[16,128,256]{2,1,0:T(8,128)(2,1)} custom-call(s32[128]{0:T(128)S(1)} %get-tuple-element.29.order_ref, s32[128]{0:T(128)S(1)} %get-tuple-element.30.turn_ref, s32[1]{0:T(128)} %get-tuple-element.31.count_ref, f32[136,128]{1,0:T(8,128)S(1)} %get-tuple-element.56.cos_ref, f32[136,128]{1,0:T(8,128)S(1)} %get-tuple-element.57.sin_ref, ...), custom_call_target="tpu_custom_call" | custom-call | tf_op jit(solution)/shard_map/prompt_late/pallas_call | solution.py:202
  50.8 7.4 %all-to-all-start = ((bf16[16,128,256]{2,1,0:T(8,128)(2,1)}), bf16[16,128,256]{2,1,0:T(8,128)(2,1)S(1)}, u32[]{:S(2)}, u32[]{:S(2)}) async-start(bf16[16,128,256]{2,1,0:T(8,128)(2,1)} %prompt_late.1), calls=%async_computation | async-start | bytes 2097152 | tf_op jit(solution)/shard_map/all_to_all | solution.py:515
  59.0 14.2 %all-to-all-done.pages_ref = bf16[16,128,256]{2,1,0:T(8,128)(2,1)S(1)} async-done(((bf16[16,128,256]{2,1,0:T(8,128)(2,1)}), bf16[16,128,256]{2,1,0:T(8,128)(2,1)S(1)}, u32[]{:S(2)}, u32[]{:S(2)}) %all-to-all-start) | async-done | bytes 1048608 | tf_op jit(solution)/shard_map/all_to_all | solution.py:515
  73.2 1.4 %attend.1 = (bf16[16,16,1024]{2,1,0:T(8,128)(2,1)S(1)}, bf16[1024,512]{1,0:T(8,128)(2,1)S(1)}) custom-call(bf16[16,128,256]{2,1,0:T(8,128)(2,1)S(1)} %all-to-all-done.pages_ref, bf16[128,128]{1,0:T(8,128)(2,1)S(1)} %get-tuple-element.41.q_ref, bf16[16,128]{1,0:T(8,128)(2,1)S(1)} %get-tuple-element.42.key_ref, ...), custom_call_target="tpu_custom_call" | custom-call | tf_op jit(solution)/shard_map/attend/pallas_call | solution.py:374
  74.6 13.0 %all_to_all.15.attn_ref = bf16[16,16,1024]{2,1,0:T(8,128)(2,1)S(1)} all-to-all(bf16[16,16,1024]{2,1,0:T(8,128)(2,1)S(1)} %get-tuple-element.45), channel_id=1, replica_groups=mesh['section'=16,'tensor'=8] {'section'}, dimensions={0} | all-to-all | bytes 1048576 | tf_op jit(solution)/shard_map/all_to_all | solution.py:517
  88.1 1.3 %collective-permute-done.9.got_ref = bf16[4,32,512]{2,1,0:T(8,128)(2,1)S(1)} collective-permute-done((bf16[4,32,512]{2,1,0:T(8,128)(2,1)S(1)}, bf16[4,32,512]{2,1,0:T(8,128)(2,1)S(1)}, u32[]{:S(2)}, u32[]{:S(2)}) %collective-permute-start.9) | collective-permute-done | bytes 131104 | tf_op jit(solution)/shard_map/ppermute | solution.py:519
  89.5 1.6 %collective-permute-start.10 = (bf16[32,512]{1,0:T(8,128)(2,1)S(1)}, bf16[32,512]{1,0:T(8,128)(2,1)S(1)}, u32[]{:S(2)}, u32[]{:S(2)}) collective-permute-start(bf16[32,512]{1,0:T(8,128)(2,1)S(1)} %get-tuple-element.50), channel_id=1, source_target_pairs={{0,2},{1,3},{2,4},{3,5},{4,6},{5,7},{6,0},{7,1},{8,10},{9,11},{10,... | collective-permute-start | bytes 98312 | tf_op jit(solution)/shard_map/ppermute | solution.py:522
  91.1 1.7 %collective-permute-start.11 = (bf16[32,512]{1,0:T(8,128)(2,1)S(1)}, bf16[32,512]{1,0:T(8,128)(2,1)S(1)}, u32[]{:S(2)}, u32[]{:S(2)}) collective-permute-start(bf16[32,512]{1,0:T(8,128)(2,1)S(1)} %get-tuple-element.51), channel_id=1, source_target_pairs={{0,6},{1,7},{2,0},{3,1},{4,2},{5,3},{6,4},{7,5},{8,14},{9,15},{10,... | collective-permute-start | bytes 98312 | tf_op jit(solution)/shard_map/ppermute | solution.py:522
  92.8 2.0 %collective-permute-start.12 = (bf16[32,512]{1,0:T(8,128)(2,1)S(1)}, bf16[32,512]{1,0:T(8,128)(2,1)S(1)}, u32[]{:S(2)}, u32[]{:S(2)}) collective-permute-start(bf16[32,512]{1,0:T(8,128)(2,1)S(1)} %get-tuple-element.52), channel_id=1, source_target_pairs={{0,4},{1,5},{2,6},{3,7},{4,0},{5,1},{6,2},{7,3},{8,12},{9,13},{10,... | collective-permute-start | bytes 98312 | tf_op jit(solution)/shard_map/ppermute | solution.py:522
  95.0 3.2 %collective-permute-done.12.c_ref = bf16[32,512]{1,0:T(8,128)(2,1)S(1)} collective-permute-done((bf16[32,512]{1,0:T(8,128)(2,1)S(1)}, bf16[32,512]{1,0:T(8,128)(2,1)S(1)}, u32[]{:S(2)}, u32[]{:S(2)}) %collective-permute-start.12) | collective-permute-done | bytes 32800 | tf_op jit(solution)/shard_map/ppermute | solution.py:522
  (34 shorter events, 6.1 us)
Async XLA Ops:
  1.8 10.6 %collective-permute-start = (bf16[512,256]{1,0:T(8,128)(2,1)S(1)}, bf16[512,256]{1,0:T(8,128)(2,1)S(1)}, u32[]{:S(2)}, u32[]{:S(2)}) collective-permute-start(bf16[512,256]{1,0:T(8,128)(2,1)S(1)} %multiply_convert_fusion), channel_id=1, source_target_pairs={{0,8},{1,33},{2,10},{3,35},{4,12},{5,37},{6,14},{7,39},{8,16},{9,4... | collective-permute-start | bytes 786440 | tf_op jit(solution)/shard_map/ppermute | solution.py:61
  3.5 9.0 %collective-permute-start.1 = (bf16[512,256]{1,0:T(8,128)(2,1)S(1)}, bf16[512,256]{1,0:T(8,128)(2,1)S(1)}, u32[]{:S(2)}, u32[]{:S(2)}) collective-permute-start(bf16[512,256]{1,0:T(8,128)(2,1)S(1)} %multiply_convert_fusion), channel_id=1, source_target_pairs={{0,24},{1,97},{2,26},{3,99},{4,28},{5,101},{6,30},{7,103},{8,0},{9... | collective-permute-start | bytes 786440 | tf_op jit(solution)/shard_map/ppermute | solution.py:61
  5.2 8.2 %collective-permute-start.2 = (bf16[512,256]{1,0:T(8,128)(2,1)S(1)}, bf16[512,256]{1,0:T(8,128)(2,1)S(1)}, u32[]{:S(2)}, u32[]{:S(2)}) collective-permute-start(bf16[512,256]{1,0:T(8,128)(2,1)S(1)} %multiply_convert_fusion), channel_id=1, source_target_pairs={{0,16},{1,65},{2,18},{3,67},{4,20},{5,69},{6,22},{7,71},{8,24},{9,... | collective-permute-start | bytes 786440 | tf_op jit(solution)/shard_map/ppermute | solution.py:61
  8.6 1.0 copy-start
  13.4 12.5 %collective-permute-start.3 = (bf16[1024,256]{1,0:T(8,128)(2,1)S(1)}, bf16[1024,256]{1,0:T(8,128)(2,1)S(1)}, u32[]{:S(2)}, u32[]{:S(2)}) collective-permute-start(bf16[1024,256]{1,0:T(8,128)(2,1)S(1)} %pad_maximum_fusion.refs_0_), channel_id=1, source_target_pairs={{0,32},{1,9},{2,34},{3,11},{4,36},{5,13},{6,38},{7,15},{8,40},{9,1... | collective-permute-start | bytes 1572872 | tf_op jit(solution)/shard_map/ppermute | solution.py:61
  15.4 14.2 %collective-permute-start.4 = (bf16[1024,256]{1,0:T(8,128)(2,1)S(1)}, bf16[1024,256]{1,0:T(8,128)(2,1)}, u32[]{:S(2)}, u32[]{:S(2)}) collective-permute-start(bf16[1024,256]{1,0:T(8,128)(2,1)S(1)} %pad_maximum_fusion.1.refs_1_), channel_id=1, source_target_pairs={{0,96},{1,25},{2,98},{3,27},{4,100},{5,29},{6,102},{7,31},{8,104},... | collective-permute-start | bytes 1572872 | tf_op jit(solution)/shard_map/ppermute | solution.py:61
  17.6 33.2 %all-to-all-start.1 = ((bf16[16,16,1408]{2,1,0:T(8,128)(2,1)}), bf16[16,16,1408]{2,1,0:T(8,128)(2,1)S(1)}, u32[]{:S(2)}, u32[]{:S(2)}) async-start(bf16[16,16,1408]{2,1,0:T(8,128)(2,1)} %get-tuple-element.40), calls=%async_computation.1 | async-start | bytes 1441792 | tf_op jit(solution)/shard_map/all_to_all | solution.py:486
  22.9 22.1 %collective-permute-start.5 = (bf16[1024,256]{1,0:T(8,128)(2,1)S(1)}, bf16[1024,256]{1,0:T(8,128)(2,1)S(1)}, u32[]{:S(2)}, u32[]{:S(2)}) collective-permute-start(bf16[1024,256]{1,0:T(8,128)(2,1)S(1)} %pad_maximum_fusion.refs_0_), channel_id=1, source_target_pairs={{0,96},{1,25},{2,98},{3,27},{4,100},{5,29},{6,102},{7,31},{8,104},... | collective-permute-start | bytes 1572872 | tf_op jit(solution)/shard_map/ppermute | solution.py:61
  25.9 19.1 %collective-permute-start.6 = (bf16[1024,256]{1,0:T(8,128)(2,1)S(1)}, bf16[1024,256]{1,0:T(8,128)(2,1)S(1)}, u32[]{:S(2)}, u32[]{:S(2)}) collective-permute-start(bf16[1024,256]{1,0:T(8,128)(2,1)S(1)} %pad_maximum_fusion.1.refs_1_), channel_id=1, source_target_pairs={{0,32},{1,9},{2,34},{3,11},{4,36},{5,13},{6,38},{7,15},{8,40},{9,1... | collective-permute-start | bytes 1572872 | tf_op jit(solution)/shard_map/ppermute | solution.py:61
  25.9 19.1 %collective-permute-start.7 = (bf16[1024,256]{1,0:T(8,128)(2,1)S(1)}, bf16[1024,256]{1,0:T(8,128)(2,1)S(1)}, u32[]{:S(2)}, u32[]{:S(2)}) collective-permute-start(bf16[1024,256]{1,0:T(8,128)(2,1)S(1)} %collective-permute-done.3.refs_2_), channel_id=1, source_target_pairs={{0,32},{1,9},{2,34},{3,11},{4,36},{5,13},{6,38},{7,15},{8,40},{9,1... | collective-permute-start | bytes 1572872 | tf_op jit(solution)/shard_map/ppermute | solution.py:61
  29.6 15.4 %collective-permute-start.8 = (bf16[1024,256]{1,0:T(8,128)(2,1)}, bf16[1024,256]{1,0:T(8,128)(2,1)S(1)}, u32[]{:S(2)}, u32[]{:S(2)}) collective-permute-start(bf16[1024,256]{1,0:T(8,128)(2,1)} %collective-permute-done.4.refs_3_), channel_id=1, source_target_pairs={{0,96},{1,25},{2,98},{3,27},{4,100},{5,29},{6,102},{7,31},{8,104},... | collective-permute-start | bytes 1572872 | tf_op jit(solution)/shard_map/ppermute | solution.py:61
  45.0 13.2 %copy-start.2 = (s32[8]{0:T(128)S(1)}, s32[8]{0:T(128)}, u32[]{:S(2)}) copy-start(s32[8]{0:T(128)} %ctx_ref.1) | copy-start | bytes 100
  45.0 53.2 %copy-start.1 = (bf16[2,128,512]{2,1,0:T(8,128)(2,1)S(1)}, bf16[2,128,512]{2,1,0:T(8,128)(2,1)}, u32[]{:S(2)}) copy-start(bf16[2,128,512]{2,1,0:T(8,128)(2,1)} %tok_ref.1) | copy-start | bytes 786436
  50.8 22.4 %all-to-all-start = ((bf16[16,128,256]{2,1,0:T(8,128)(2,1)}), bf16[16,128,256]{2,1,0:T(8,128)(2,1)S(1)}, u32[]{:S(2)}, u32[]{:S(2)}) async-start(bf16[16,128,256]{2,1,0:T(8,128)(2,1)} %prompt_late.1), calls=%async_computation | async-start | bytes 2097152 | tf_op jit(solution)/shard_map/all_to_all | solution.py:515
  88.0 1.4 %collective-permute-start.9 = (bf16[4,32,512]{2,1,0:T(8,128)(2,1)S(1)}, bf16[4,32,512]{2,1,0:T(8,128)(2,1)S(1)}, u32[]{:S(2)}, u32[]{:S(2)}) collective-permute-start(bf16[4,32,512]{2,1,0:T(8,128)(2,1)S(1)} %get-tuple-element.48), channel_id=1, source_target_pairs={{0,1},{1,0},{2,3},{3,2},{4,5},{5,4},{6,7},{7,6},{8,9},{9,8},{10,11... | collective-permute-start | bytes 393224 | tf_op jit(solution)/shard_map/ppermute | solution.py:519
  89.5 5.3 %collective-permute-start.10 = (bf16[32,512]{1,0:T(8,128)(2,1)S(1)}, bf16[32,512]{1,0:T(8,128)(2,1)S(1)}, u32[]{:S(2)}, u32[]{:S(2)}) collective-permute-start(bf16[32,512]{1,0:T(8,128)(2,1)S(1)} %get-tuple-element.50), channel_id=1, source_target_pairs={{0,2},{1,3},{2,4},{3,5},{4,6},{5,7},{6,0},{7,1},{8,10},{9,11},{10,... | collective-permute-start | bytes 98312 | tf_op jit(solution)/shard_map/ppermute | solution.py:522
  91.1 3.9 %collective-permute-start.11 = (bf16[32,512]{1,0:T(8,128)(2,1)S(1)}, bf16[32,512]{1,0:T(8,128)(2,1)S(1)}, u32[]{:S(2)}, u32[]{:S(2)}) collective-permute-start(bf16[32,512]{1,0:T(8,128)(2,1)S(1)} %get-tuple-element.51), channel_id=1, source_target_pairs={{0,6},{1,7},{2,0},{3,1},{4,2},{5,3},{6,4},{7,5},{8,14},{9,15},{10,... | collective-permute-start | bytes 98312 | tf_op jit(solution)/shard_map/ppermute | solution.py:522
  92.8 5.4 %collective-permute-start.12 = (bf16[32,512]{1,0:T(8,128)(2,1)S(1)}, bf16[32,512]{1,0:T(8,128)(2,1)S(1)}, u32[]{:S(2)}, u32[]{:S(2)}) collective-permute-start(bf16[32,512]{1,0:T(8,128)(2,1)S(1)} %get-tuple-element.52), channel_id=1, source_target_pairs={{0,4},{1,5},{2,6},{3,7},{4,0},{5,1},{6,2},{7,3},{8,12},{9,13},{10,... | collective-permute-start | bytes 98312 | tf_op jit(solution)/shard_map/ppermute | solution.py:522

commit v4 on v3

--- a/solution.py
+++ b/solution.py
@@ -68,7 +68,7 @@
 
 def early_kernel(n_early, blocks_ref, order_ref, count_ref, x_ref, *refs):
     w_refs, refs = refs[: n_early // 2], refs[n_early // 2 :]
-    acc_ref, rest_ref, squares_ref, buf_ref, sems = refs
+    acc_ref, middle_ref, late_ref, squares_ref, buf_ref, sems = refs
     count = count_ref[0]
 
     def copy(t, c):
@@ -113,7 +113,8 @@
             total = part if total is None else total + part
         acc_ref[rows, :] = total
         for k in range(n_early, SECTIONS):
-            at = (k - n_early) * DEPTH
+            rest_ref = middle_ref if k < n_early + 4 else late_ref
+            at = (k - n_early) % 4 * DEPTH
             rest_ref[rows, at : at + DEPTH] = buf_ref[slot, :, depth(k)]
         for c in range(PAGES):
             sums = [None] * 4
@@ -149,10 +150,11 @@
         in_specs=[SMEM_SPEC] * 3
         + [pl.BlockSpec(memory_space=pl.ANY)]
         + [VMEM_SPEC] * len(weights),
-        out_specs=[VMEM_SPEC] * 3,
+        out_specs=[VMEM_SPEC] * 4,
         out_shape=[
             pltpu.VMEM((rows, WKV), F32),
-            pltpu.VMEM((rows, (SECTIONS - n_early) * DEPTH), BF16),
+            pltpu.VMEM((rows, 4 * DEPTH), BF16),
+            pltpu.VMEM((rows, 4 * DEPTH), BF16),
             pltpu.VMEM((rows, 128), F32),
         ],
         scratch_shapes=[
@@ -162,6 +164,32 @@
         compiler_params=params(24),
         name="prompt_early",
     )(blocks, order, count, x, *weights)
+
+
+def middle_kernel(count_ref, acc_ref, x_ref, *refs):
+    w_refs, out_ref = refs[:-1], refs[-1]
+
+    def tile(t, _):
+        rows = pl.ds(pl.multiple_of(t * TILE, TILE), TILE)
+        total = acc_ref[rows, :]
+        for k, w_ref in enumerate(w_refs):
+            x = x_ref[rows, k * 2 * DEPTH : (k + 1) * 2 * DEPTH]
+            total = total + jnp.dot(x, w_ref[...], preferred_element_type=F32)
+        out_ref[rows, :] = total
+        return 0
+
+    lax.fori_loop(0, pl.cdiv(count_ref[0], PAGES), tile, 0)
+
+
+def prompt_middle(count, acc, x, weights):
+    return pl.pallas_call(
+        middle_kernel,
+        in_specs=[SMEM_SPEC] + [VMEM_SPEC] * (2 + len(weights)),
+        out_specs=VMEM_SPEC,
+        out_shape=pltpu.VMEM(acc.shape, F32),
+        compiler_params=params(8),
+        name="prompt_middle",
+    )(count, kept(acc), kept(x), *weights)
 
 
 def late_kernel(
@@ -214,6 +242,25 @@
     )(order, turn, count, cosine, sine, *[kept(array) for array in early], *weights)
 
 
+def own_gain(gain_ref):
+    section = lax.axis_index("section")
+    return gain_ref[:, pl.ds(pl.multiple_of(section * DEPTH, DEPTH), DEPTH)]
+
+
+def weight_kernel(gain_ref, kvw_ref, out_ref):
+    column = jnp.broadcast_to(own_gain(gain_ref), (WKV, DEPTH)).T
+    out_ref[...] = (kvw_ref[...].astype(F32) * column).astype(BF16)
+
+
+def with_gain(gain, kv_weight):
+    return pl.pallas_call(
+        weight_kernel,
+        out_shape=jax.ShapeDtypeStruct(kv_weight.shape, BF16),
+        compiler_params=params(),
+        name="with_gain",
+    )(in_hbm(gain), in_hbm(kv_weight))
+
+
 def project_kernel(
     slot_ref, tok_ref, gain_ref, qw_ref, kvw_ref, ids_ref, out_ref, order_ref, turn_ref, count_ref
 ):
@@ -226,7 +273,7 @@
     count_ref[0] = found
 
     tok = tok_ref[...].astype(F32)
-    scaled = (tok * gain_ref[...]).astype(BF16)
+    scaled = (tok * own_gain(gain_ref)).astype(BF16)
     squares = jnp.sum(tok * tok, axis=-1, keepdims=True)
     high = squares.astype(BF16).astype(F32)
     low = squares - high
@@ -468,15 +515,14 @@
     member = lax.axis_index("tensor")
     core = member % 2
     own_ids = page_slot[0]
-    gain_here = lax.dynamic_slice_in_dim(norm_gain, section * DEPTH, DEPTH, 0)
     cosine, sine = rotation_tables()
 
     ids_wide = jnp.pad(own_ids.astype(F32), ((0, 0), (ID_LANE, EXTRA - ID_LANE - CAP)))
     payload, order, turn, count = project(
-        own_ids, new_tokens.reshape(-1, DEPTH), gain_here[None, :], q_weight, kv_weight, ids_wide
-    )
-
-    weight = (kv_weight.astype(F32) * gain_here[:, None]).astype(BF16)
+        own_ids, new_tokens.reshape(-1, DEPTH), norm_gain[None, :], q_weight, kv_weight, ids_wide
+    )
+
+    weight = with_gain(norm_gain[None, :], kv_weight)
     from_1 = shifted(weight, 0, 1)
     from_3 = shifted(weight, 0, -1)
     from_2 = shifted(weight, 0, 2)
@@ -507,9 +553,12 @@
         (0, 1), (3, 1), (1, 3), (2, 3),
         (0, 2), (3, 2), (1, 2), (2, 2),
     )
-    early = prompt_early(where, order, count, prompt_rows, (near, far, near_p, far_m))
+    acc, x_middle, x_late, squares = prompt_early(
+        where, order, count, prompt_rows, (near, far, near_p, far_m)
+    )
+    acc = prompt_middle(count, acc, x_middle, (near_m, far_p))
     pages = prompt_late(
-        order, turn, count, cosine, sine, early, (near_m, far_p, near_o, far_o)
+        order, turn, count, cosine, sine, (acc, x_late, squares), (near_o, far_o)
     )
     queries, new_keys, new_values, owners = ready(context_len, got, cosine, sine)
     received = lax.all_to_all(pages, "section", split_axis=0, concat_axis=0, tiled=True)

time: 99.3 us -> 97.9 us (0.986)
  waiting for transfers between devices: 22.8 us -> 20.1 us
  Pallas kernels: 23 us -> 24.7 us
  other arithmetic: 2.29 us -> 1.21 us
    pallas_call x0 -> x2, Pallas kernels: none -> 3.52 us  [the longest x1 2.41 us: prompt_middle(): pl.pallas_call(middle_kernel, in_specs=[SMEM_SPEC] + [VMEM_SPEC] * (2 + l...]
    all_to_all x1, waiting for transfers between devices: 14.2 us -> 12.5 us  [on_device(): lax.all_to_all(pages, 'section', split_axis=0, concat_axis=0, tiled=True)]
    pallas_call x1, Pallas kernels: 5.74 us -> 4.51 us  [prompt_late(): pl.pallas_call(late_kernel, in_specs=[SMEM_SPEC] * 3 + [VMEM_SPEC] * (5 +...]
    convert_element_type x1 -> x0, other arithmetic: 1.08 us -> none  [on_device(): weight = (kv_weight.astype(F32) * gain_here[:, None]).astype(BF16)]
    ppermute x9, waiting for transfers between devices: 3.77 us -> 2.77 us  [shifted(): return lax.ppermute(array, ('section', 'tensor'), pairs)]
  transfers between devices with their start and end apart: 15 -> 15, of which waited for: 6 -> 5; matrix products, arithmetic and copies ran while one was open for 2% -> 2% of each run, Pallas kernels for 21% -> 22%
where the time goes in v4:
time: 97.9 us; the launch traced here: 97.6 us
  starting transfers between devices  35.5 us (36%)
  Pallas kernels  24.7 us (25%)
  waiting for transfers between devices  20.1 us (21%)
  blocking collectives  13 us (13%)
  local copies, waits for them, and re-layouts  2.73 us (3%)
  other arithmetic  1.21 us (1%)
    ppermute x9, starting transfers between devices, shifted(): return lax.ppermute(array, ('section', 'tensor'), pairs)  17.5 us
    all_to_all x1, blocking collectives, on_device(): lax.all_to_all(attn, 'section', split_axis=0, concat_axis=0, tiled=True)  13 us
    all_to_all x1, waiting for transfers between devices, on_device(): lax.all_to_all(pages, 'section', split_axis=0, concat_axis=0, tiled=True)  12.5 us
    pallas_call x1, Pallas kernels, prompt_early(): pl.pallas_call(functools.partial(early_kernel, n_early), in_specs=[SMEM_S...  10.5 us
    all_to_all x1, starting transfers between devices, on_device(): lax.all_to_all(pages, 'section', split_axis=0, concat_axis=0, tiled=True)  7.47 us
    ppermute x3, starting transfers between devices, on_device(): lax.ppermute(piece, 'tensor', [(t, (t + 2 * step) % 8) for t in range(8)])  5.28 us
    all_to_all x1, starting transfers between devices, on_device(): lax.all_to_all(payload, 'section', split_axis=0, concat_axis=0, tiled=True)  5.17 us
    pallas_call x1, Pallas kernels, prompt_late(): pl.pallas_call(late_kernel, in_specs=[SMEM_SPEC] * 3 + [VMEM_SPEC] * (5 +...  4.51 us
  transfers between devices with their start and end apart: 15, of which 5 were waited for; matrix products, arithmetic and copies ran while one was open for 2% of the time, Pallas kernels for 22%

profile of v4, /device:TPU:0, one launch (start us, length us, event | category | flops | bytes accessed | tf_op | source)
XLA Modules:
  0.0 97.6 jit_solution(6386279378198568061)
XLA Ops:
  0.0 1.1 %with_gain.1 = bf16[512,256]{1,0:T(8,128)(2,1)S(1)} custom-call(f32[1,8192]{1,0:T(1,128)} %bitcast.22, bf16[512,256]{1,0:T(8,128)(2,1)} %kvw_ref.3), custom_call_target="tpu_custom_call" | custom-call | tf_op jit(solution)/shard_map/with_gain/pallas_call | solution.py:256
  1.1 1.6 %collective-permute-start = (bf16[512,256]{1,0:T(8,128)(2,1)S(1)}, bf16[512,256]{1,0:T(8,128)(2,1)S(1)}, u32[]{:S(2)}, u32[]{:S(2)}) collective-permute-start(bf16[512,256]{1,0:T(8,128)(2,1)S(1)} %with_gain.1), channel_id=1, source_target_pairs={{0,8},{1,33},{2,10},{3,35},{4,12},{5,37},{6,14},{7,39},{8,16},{9,4... | collective-permute-start | bytes 786440 | tf_op jit(solution)/shard_map/ppermute | solution.py:61
  2.8 2.7 %collective-permute-start.2 = (bf16[512,256]{1,0:T(8,128)(2,1)S(1)}, bf16[512,256]{1,0:T(8,128)(2,1)S(1)}, u32[]{:S(2)}, u32[]{:S(2)}) collective-permute-start(bf16[512,256]{1,0:T(8,128)(2,1)S(1)} %with_gain.1), channel_id=1, source_target_pairs={{0,16},{1,65},{2,18},{3,67},{4,20},{5,69},{6,22},{7,71},{8,24},{9,... | collective-permute-start | bytes 786440 | tf_op jit(solution)/shard_map/ppermute | solution.py:61
  5.5 1.4 %collective-permute-start.1 = (bf16[512,256]{1,0:T(8,128)(2,1)S(1)}, bf16[512,256]{1,0:T(8,128)(2,1)S(1)}, u32[]{:S(2)}, u32[]{:S(2)}) collective-permute-start(bf16[512,256]{1,0:T(8,128)(2,1)S(1)} %with_gain.1), channel_id=1, source_target_pairs={{0,24},{1,97},{2,26},{3,99},{4,28},{5,101},{6,30},{7,103},{8,0},{9... | collective-permute-start | bytes 786440 | tf_op jit(solution)/shard_map/ppermute | solution.py:61
  8.5 0.9 copy-done
  10.2 2.9 %project.1 = (bf16[16,16,1408]{2,1,0:T(8,128)(2,1)}, s32[128]{0:T(128)S(1)}, s32[128]{0:T(128)S(1)}, s32[1]{0:T(128)}) custom-call(s32[16,8]{1,0:T(8,128)S(1)} %copy.12.slot_ref, bf16[256,512]{1,0:T(8,128)(2,1)} %bitcast.21, f32[1,8192]{1,0:T(1,128)S(1)} %bitcast.23, bf16[512,1024]{1,0:T(8,128)(2,1)} %qw_ref.1, bf16[512,256]{1,0:T(8,128)(2,1)S(1)} %copy-done, ...), custom_call_target="tpu_custom_call" | custom-call | tf_op jit(solution)/shard_map/project/pallas_call | solution.py:302
  13.2 2.0 %collective-permute-start.3 = (bf16[1024,256]{1,0:T(8,128)(2,1)S(1)}, bf16[1024,256]{1,0:T(8,128)(2,1)S(1)}, u32[]{:S(2)}, u32[]{:S(2)}) collective-permute-start(bf16[1024,256]{1,0:T(8,128)(2,1)S(1)} %pad_maximum_fusion.refs_0_), channel_id=1, source_target_pairs={{0,32},{1,9},{2,34},{3,11},{4,36},{5,13},{6,38},{7,15},{8,40},{9,1... | collective-permute-start | bytes 1572872 | tf_op jit(solution)/shard_map/ppermute | solution.py:61
  15.2 2.2 %collective-permute-start.4 = (bf16[1024,256]{1,0:T(8,128)(2,1)S(1)}, bf16[1024,256]{1,0:T(8,128)(2,1)S(1)}, u32[]{:S(2)}, u32[]{:S(2)}) collective-permute-start(bf16[1024,256]{1,0:T(8,128)(2,1)S(1)} %pad_maximum_fusion.1.refs_1_), channel_id=1, source_target_pairs={{0,96},{1,25},{2,98},{3,27},{4,100},{5,29},{6,102},{7,31},{8,104},... | collective-permute-start | bytes 1572872 | tf_op jit(solution)/shard_map/ppermute | solution.py:61
  17.4 5.2 %all-to-all-start.1 = ((bf16[16,16,1408]{2,1,0:T(8,128)(2,1)}), bf16[16,16,1408]{2,1,0:T(8,128)(2,1)S(1)}, u32[]{:S(2)}, u32[]{:S(2)}) async-start(bf16[16,16,1408]{2,1,0:T(8,128)(2,1)} %get-tuple-element.42), calls=%async_computation.1 | async-start | bytes 1441792 | tf_op jit(solution)/shard_map/all_to_all | solution.py:532
  22.9 3.0 %collective-permute-start.5 = (bf16[1024,256]{1,0:T(8,128)(2,1)S(1)}, bf16[1024,256]{1,0:T(8,128)(2,1)S(1)}, u32[]{:S(2)}, u32[]{:S(2)}) collective-permute-start(bf16[1024,256]{1,0:T(8,128)(2,1)S(1)} %pad_maximum_fusion.refs_0_), channel_id=1, source_target_pairs={{0,96},{1,25},{2,98},{3,27},{4,100},{5,29},{6,102},{7,31},{8,104},... | collective-permute-start | bytes 1572872 | tf_op jit(solution)/shard_map/ppermute | solution.py:61
  26.7 2.7 %collective-permute-done.4.refs_3_ = bf16[1024,256]{1,0:T(8,128)(2,1)S(1)} collective-permute-done((bf16[1024,256]{1,0:T(8,128)(2,1)S(1)}, bf16[1024,256]{1,0:T(8,128)(2,1)S(1)}, u32[]{:S(2)}, u32[]{:S(2)}) %collective-permute-start.4) | collective-permute-done | bytes 524320 | tf_op jit(solution)/shard_map/ppermute | solution.py:61
  29.4 3.7 %collective-permute-start.8 = (bf16[1024,256]{1,0:T(8,128)(2,1)S(1)}, bf16[1024,256]{1,0:T(8,128)(2,1)S(1)}, u32[]{:S(2)}, u32[]{:S(2)}) collective-permute-start(bf16[1024,256]{1,0:T(8,128)(2,1)S(1)} %collective-permute-done.4.refs_3_), channel_id=1, source_target_pairs={{0,96},{1,25},{2,98},{3,27},{4,100},{5,29},{6,102},{7,31},{8,104},... | collective-permute-start | bytes 1572872 | tf_op jit(solution)/shard_map/ppermute | solution.py:61
  33.6 10.5 %prompt_early.1 = (f32[2048,256]{1,0:T(8,128)S(1)}, bf16[2048,2048]{1,0:T(8,128)(2,1)S(1)}, bf16[2048,2048]{1,0:T(8,128)(2,1)S(1)}, f32[2048,128]{1,0:T(8,128)S(1)}) custom-call(s32[16]{0:T(128)S(1)} %stack.67.blocks_ref, s32[128]{0:T(128)S(1)} %get-tuple-element.30.order_ref, s32[1]{0:T(128)} %get-tuple-element.32.count_ref, bf16[2048,8192]{1,0:T(8,128)(2,1)} %x_ref.1, ...), custom_call_target="tpu_custom_call" | custom-call | tf_op jit(solution)/shard_map/prompt_early/pallas_call | solution.py:148
  44.1 2.4 %prompt_middle.1.acc_ref = f32[2048,256]{1,0:T(8,128)S(1)} custom-call(s32[1]{0:T(128)} %get-tuple-element.32.count_ref, f32[2048,256]{1,0:T(8,128)S(1)} %get-tuple-element.36.acc_ref, bf16[2048,2048]{1,0:T(8,128)(2,1)S(1)} %get-tuple-element.37.x_ref, bf16[1024,256]{1,0:T(8,128)(2,1)S(1)} %collective-permute-done.5.refs_0_, ...), custom_call_target="tpu_custom_call" | custom-call | tf_op jit(solution)/shard_map/prompt_middle/pallas_call | solution.py:185
  46.6 4.5 %prompt_late.1 = bf16[16,128,256]{2,1,0:T(8,128)(2,1)} custom-call(s32[128]{0:T(128)S(1)} %get-tuple-element.30.order_ref, s32[128]{0:T(128)S(1)} %get-tuple-element.31.turn_ref, s32[1]{0:T(128)} %get-tuple-element.32.count_ref, f32[136,128]{1,0:T(8,128)S(1)} %get-tuple-element.58.cos_ref, f32[136,128]{1,0:T(8,128)S(1)} %get-tuple-element.59.sin_ref, ...), custom_call_target="tpu_custom_call" | custom-call | tf_op jit(solution)/shard_map/prompt_late/pallas_call | solution.py:230
  51.1 7.5 %all-to-all-start = ((bf16[16,128,256]{2,1,0:T(8,128)(2,1)}), bf16[16,128,256]{2,1,0:T(8,128)(2,1)S(1)}, u32[]{:S(2)}, u32[]{:S(2)}) async-start(bf16[16,128,256]{2,1,0:T(8,128)(2,1)} %prompt_late.1), calls=%async_computation | async-start | bytes 2097152 | tf_op jit(solution)/shard_map/all_to_all | solution.py:564
  59.4 12.5 %all-to-all-done.pages_ref = bf16[16,128,256]{2,1,0:T(8,128)(2,1)S(1)} async-done(((bf16[16,128,256]{2,1,0:T(8,128)(2,1)}), bf16[16,128,256]{2,1,0:T(8,128)(2,1)S(1)}, u32[]{:S(2)}, u32[]{:S(2)}) %all-to-all-start) | async-done | bytes 1048608 | tf_op jit(solution)/shard_map/all_to_all | solution.py:564
  71.9 1.4 %attend.1 = (bf16[16,16,1024]{2,1,0:T(8,128)(2,1)S(1)}, bf16[1024,512]{1,0:T(8,128)(2,1)S(1)}) custom-call(bf16[16,128,256]{2,1,0:T(8,128)(2,1)S(1)} %all-to-all-done.pages_ref, bf16[128,128]{1,0:T(8,128)(2,1)S(1)} %get-tuple-element.43.q_ref, bf16[16,128]{1,0:T(8,128)(2,1)S(1)} %get-tuple-element.44.key_ref, ...), custom_call_target="tpu_custom_call" | custom-call | tf_op jit(solution)/shard_map/attend/pallas_call | solution.py:421
  73.3 13.0 %all_to_all.15.attn_ref = bf16[16,16,1024]{2,1,0:T(8,128)(2,1)S(1)} all-to-all(bf16[16,16,1024]{2,1,0:T(8,128)(2,1)S(1)} %get-tuple-element.47), channel_id=1, replica_groups=mesh['section'=16,'tensor'=8] {'section'}, dimensions={0} | all-to-all | bytes 1048576 | tf_op jit(solution)/shard_map/all_to_all | solution.py:566
  86.9 1.3 %collective-permute-done.9.got_ref = bf16[4,32,512]{2,1,0:T(8,128)(2,1)S(1)} collective-permute-done((bf16[4,32,512]{2,1,0:T(8,128)(2,1)S(1)}, bf16[4,32,512]{2,1,0:T(8,128)(2,1)S(1)}, u32[]{:S(2)}, u32[]{:S(2)}) %collective-permute-start.9) | collective-permute-done | bytes 131104 | tf_op jit(solution)/shard_map/ppermute | solution.py:568
  88.3 1.6 %collective-permute-start.10 = (bf16[32,512]{1,0:T(8,128)(2,1)S(1)}, bf16[32,512]{1,0:T(8,128)(2,1)S(1)}, u32[]{:S(2)}, u32[]{:S(2)}) collective-permute-start(bf16[32,512]{1,0:T(8,128)(2,1)S(1)} %get-tuple-element.52), channel_id=1, source_target_pairs={{0,2},{1,3},{2,4},{3,5},{4,6},{5,7},{6,0},{7,1},{8,10},{9,11},{10,... | collective-permute-start | bytes 98312 | tf_op jit(solution)/shard_map/ppermute | solution.py:571
  89.9 1.7 %collective-permute-start.11 = (bf16[32,512]{1,0:T(8,128)(2,1)S(1)}, bf16[32,512]{1,0:T(8,128)(2,1)S(1)}, u32[]{:S(2)}, u32[]{:S(2)}) collective-permute-start(bf16[32,512]{1,0:T(8,128)(2,1)S(1)} %get-tuple-element.53), channel_id=1, source_target_pairs={{0,6},{1,7},{2,0},{3,1},{4,2},{5,3},{6,4},{7,5},{8,14},{9,15},{10,... | collective-permute-start | bytes 98312 | tf_op jit(solution)/shard_map/ppermute | solution.py:571
  91.6 2.0 %collective-permute-start.12 = (bf16[32,512]{1,0:T(8,128)(2,1)S(1)}, bf16[32,512]{1,0:T(8,128)(2,1)S(1)}, u32[]{:S(2)}, u32[]{:S(2)}) collective-permute-start(bf16[32,512]{1,0:T(8,128)(2,1)S(1)} %get-tuple-element.54), channel_id=1, source_target_pairs={{0,4},{1,5},{2,6},{3,7},{4,0},{5,1},{6,2},{7,3},{8,12},{9,13},{10,... | collective-permute-start | bytes 98312 | tf_op jit(solution)/shard_map/ppermute | solution.py:571
  93.8 3.2 %collective-permute-done.12.c_ref = bf16[32,512]{1,0:T(8,128)(2,1)S(1)} collective-permute-done((bf16[32,512]{1,0:T(8,128)(2,1)S(1)}, bf16[32,512]{1,0:T(8,128)(2,1)S(1)}, u32[]{:S(2)}, u32[]{:S(2)}) %collective-permute-start.12) | collective-permute-done | bytes 32800 | tf_op jit(solution)/shard_map/ppermute | solution.py:571
  (36 shorter events, 6.1 us)
Async XLA Ops:
  1.1 12.0 %collective-permute-start = (bf16[512,256]{1,0:T(8,128)(2,1)S(1)}, bf16[512,256]{1,0:T(8,128)(2,1)S(1)}, u32[]{:S(2)}, u32[]{:S(2)}) collective-permute-start(bf16[512,256]{1,0:T(8,128)(2,1)S(1)} %with_gain.1), channel_id=1, source_target_pairs={{0,8},{1,33},{2,10},{3,35},{4,12},{5,37},{6,14},{7,39},{8,16},{9,4... | collective-permute-start | bytes 786440 | tf_op jit(solution)/shard_map/ppermute | solution.py:61
  2.8 10.4 %collective-permute-start.2 = (bf16[512,256]{1,0:T(8,128)(2,1)S(1)}, bf16[512,256]{1,0:T(8,128)(2,1)S(1)}, u32[]{:S(2)}, u32[]{:S(2)}) collective-permute-start(bf16[512,256]{1,0:T(8,128)(2,1)S(1)} %with_gain.1), channel_id=1, source_target_pairs={{0,16},{1,65},{2,18},{3,67},{4,20},{5,69},{6,22},{7,71},{8,24},{9,... | collective-permute-start | bytes 786440 | tf_op jit(solution)/shard_map/ppermute | solution.py:61
  5.5 7.7 %collective-permute-start.1 = (bf16[512,256]{1,0:T(8,128)(2,1)S(1)}, bf16[512,256]{1,0:T(8,128)(2,1)S(1)}, u32[]{:S(2)}, u32[]{:S(2)}) collective-permute-start(bf16[512,256]{1,0:T(8,128)(2,1)S(1)} %with_gain.1), channel_id=1, source_target_pairs={{0,24},{1,97},{2,26},{3,99},{4,28},{5,101},{6,30},{7,103},{8,0},{9... | collective-permute-start | bytes 786440 | tf_op jit(solution)/shard_map/ppermute | solution.py:61
  8.5 1.0 copy-start
  9.5 0.8 copy-start.2
  13.2 12.7 %collective-permute-start.3 = (bf16[1024,256]{1,0:T(8,128)(2,1)S(1)}, bf16[1024,256]{1,0:T(8,128)(2,1)S(1)}, u32[]{:S(2)}, u32[]{:S(2)}) collective-permute-start(bf16[1024,256]{1,0:T(8,128)(2,1)S(1)} %pad_maximum_fusion.refs_0_), channel_id=1, source_target_pairs={{0,32},{1,9},{2,34},{3,11},{4,36},{5,13},{6,38},{7,15},{8,40},{9,1... | collective-permute-start | bytes 1572872 | tf_op jit(solution)/shard_map/ppermute | solution.py:61
  15.2 14.2 %collective-permute-start.4 = (bf16[1024,256]{1,0:T(8,128)(2,1)S(1)}, bf16[1024,256]{1,0:T(8,128)(2,1)S(1)}, u32[]{:S(2)}, u32[]{:S(2)}) collective-permute-start(bf16[1024,256]{1,0:T(8,128)(2,1)S(1)} %pad_maximum_fusion.1.refs_1_), channel_id=1, source_target_pairs={{0,96},{1,25},{2,98},{3,27},{4,100},{5,29},{6,102},{7,31},{8,104},... | collective-permute-start | bytes 1572872 | tf_op jit(solution)/shard_map/ppermute | solution.py:61
  17.4 33.7 %all-to-all-start.1 = ((bf16[16,16,1408]{2,1,0:T(8,128)(2,1)}), bf16[16,16,1408]{2,1,0:T(8,128)(2,1)S(1)}, u32[]{:S(2)}, u32[]{:S(2)}) async-start(bf16[16,16,1408]{2,1,0:T(8,128)(2,1)} %get-tuple-element.42), calls=%async_computation.1 | async-start | bytes 1441792 | tf_op jit(solution)/shard_map/all_to_all | solution.py:532
  22.9 21.3 %collective-permute-start.5 = (bf16[1024,256]{1,0:T(8,128)(2,1)S(1)}, bf16[1024,256]{1,0:T(8,128)(2,1)S(1)}, u32[]{:S(2)}, u32[]{:S(2)}) collective-permute-start(bf16[1024,256]{1,0:T(8,128)(2,1)S(1)} %pad_maximum_fusion.refs_0_), channel_id=1, source_target_pairs={{0,96},{1,25},{2,98},{3,27},{4,100},{5,29},{6,102},{7,31},{8,104},... | collective-permute-start | bytes 1572872 | tf_op jit(solution)/shard_map/ppermute | solution.py:61
  25.9 18.3 %collective-permute-start.6 = (bf16[1024,256]{1,0:T(8,128)(2,1)S(1)}, bf16[1024,256]{1,0:T(8,128)(2,1)S(1)}, u32[]{:S(2)}, u32[]{:S(2)}) collective-permute-start(bf16[1024,256]{1,0:T(8,128)(2,1)S(1)} %pad_maximum_fusion.1.refs_1_), channel_id=1, source_target_pairs={{0,32},{1,9},{2,34},{3,11},{4,36},{5,13},{6,38},{7,15},{8,40},{9,1... | collective-permute-start | bytes 1572872 | tf_op jit(solution)/shard_map/ppermute | solution.py:61
  25.9 20.7 %collective-permute-start.7 = (bf16[1024,256]{1,0:T(8,128)(2,1)S(1)}, bf16[1024,256]{1,0:T(8,128)(2,1)S(1)}, u32[]{:S(2)}, u32[]{:S(2)}) collective-permute-start(bf16[1024,256]{1,0:T(8,128)(2,1)S(1)} %collective-permute-done.3.refs_2_), channel_id=1, source_target_pairs={{0,32},{1,9},{2,34},{3,11},{4,36},{5,13},{6,38},{7,15},{8,40},{9,1... | collective-permute-start | bytes 1572872 | tf_op jit(solution)/shard_map/ppermute | solution.py:61
  29.4 17.1 %collective-permute-start.8 = (bf16[1024,256]{1,0:T(8,128)(2,1)S(1)}, bf16[1024,256]{1,0:T(8,128)(2,1)S(1)}, u32[]{:S(2)}, u32[]{:S(2)}) collective-permute-start(bf16[1024,256]{1,0:T(8,128)(2,1)S(1)} %collective-permute-done.4.refs_3_), channel_id=1, source_target_pairs={{0,96},{1,25},{2,98},{3,27},{4,100},{5,29},{6,102},{7,31},{8,104},... | collective-permute-start | bytes 1572872 | tf_op jit(solution)/shard_map/ppermute | solution.py:61
  46.6 12.0 %copy-start.3 = (s32[8]{0:T(128)S(1)}, s32[8]{0:T(128)}, u32[]{:S(2)}) copy-start(s32[8]{0:T(128)} %ctx_ref.1) | copy-start | bytes 100
  46.6 50.4 %copy-start.1 = (bf16[2,128,512]{2,1,0:T(8,128)(2,1)S(1)}, bf16[2,128,512]{2,1,0:T(8,128)(2,1)}, u32[]{:S(2)}) copy-start(bf16[2,128,512]{2,1,0:T(8,128)(2,1)} %tok_ref.1) | copy-start | bytes 786436
  51.1 20.8 %all-to-all-start = ((bf16[16,128,256]{2,1,0:T(8,128)(2,1)}), bf16[16,128,256]{2,1,0:T(8,128)(2,1)S(1)}, u32[]{:S(2)}, u32[]{:S(2)}) async-start(bf16[16,128,256]{2,1,0:T(8,128)(2,1)} %prompt_late.1), calls=%async_computation | async-start | bytes 2097152 | tf_op jit(solution)/shard_map/all_to_all | solution.py:564
  86.8 1.4 %collective-permute-start.9 = (bf16[4,32,512]{2,1,0:T(8,128)(2,1)S(1)}, bf16[4,32,512]{2,1,0:T(8,128)(2,1)S(1)}, u32[]{:S(2)}, u32[]{:S(2)}) collective-permute-start(bf16[4,32,512]{2,1,0:T(8,128)(2,1)S(1)} %get-tuple-element.50), channel_id=1, source_target_pairs={{0,1},{1,0},{2,3},{3,2},{4,5},{5,4},{6,7},{7,6},{8,9},{9,8},{10,11... | collective-permute-start | bytes 393224 | tf_op jit(solution)/shard_map/ppermute | solution.py:568
  88.3 5.3 %collective-permute-start.10 = (bf16[32,512]{1,0:T(8,128)(2,1)S(1)}, bf16[32,512]{1,0:T(8,128)(2,1)S(1)}, u32[]{:S(2)}, u32[]{:S(2)}) collective-permute-start(bf16[32,512]{1,0:T(8,128)(2,1)S(1)} %get-tuple-element.52), channel_id=1, source_target_pairs={{0,2},{1,3},{2,4},{3,5},{4,6},{5,7},{6,0},{7,1},{8,10},{9,11},{10,... | collective-permute-start | bytes 98312 | tf_op jit(solution)/shard_map/ppermute | solution.py:571
  89.9 3.9 %collective-permute-start.11 = (bf16[32,512]{1,0:T(8,128)(2,1)S(1)}, bf16[32,512]{1,0:T(8,128)(2,1)S(1)}, u32[]{:S(2)}, u32[]{:S(2)}) collective-permute-start(bf16[32,512]{1,0:T(8,128)(2,1)S(1)} %get-tuple-element.53), channel_id=1, source_target_pairs={{0,6},{1,7},{2,0},{3,1},{4,2},{5,3},{6,4},{7,5},{8,14},{9,15},{10,... | collective-permute-start | bytes 98312 | tf_op jit(solution)/shard_map/ppermute | solution.py:571
  91.6 5.4 %collective-permute-start.12 = (bf16[32,512]{1,0:T(8,128)(2,1)S(1)}, bf16[32,512]{1,0:T(8,128)(2,1)S(1)}, u32[]{:S(2)}, u32[]{:S(2)}) collective-permute-start(bf16[32,512]{1,0:T(8,128)(2,1)S(1)} %get-tuple-element.54), channel_id=1, source_target_pairs={{0,4},{1,5},{2,6},{3,7},{4,0},{5,1},{6,2},{7,3},{8,12},{9,13},{10,... | collective-permute-start | bytes 98312 | tf_op jit(solution)/shard_map/ppermute | solution.py:571

commit v5 on v4

--- a/solution.py
+++ b/solution.py
@@ -63,7 +63,9 @@
 
 TILE = 256
 PAGES = TILE // PAGE
-BUFFERS = 3
+EARLY_TILE = 128
+EARLY_PAGES = EARLY_TILE // PAGE
+BUFFERS = 6
 
 
 def early_kernel(n_early, blocks_ref, order_ref, count_ref, x_ref, *refs):
@@ -73,7 +75,7 @@
 
     def copy(t, c):
         slot = t % BUFFERS
-        row = pl.multiple_of(order_ref[t * PAGES + c] * PAGE, PAGE)
+        row = pl.multiple_of(order_ref[t * EARLY_PAGES + c] * PAGE, PAGE)
         return pltpu.make_async_copy(
             x_ref.at[pl.ds(row, PAGE), :],
             buf_ref.at[slot, pl.ds(c * PAGE, PAGE), :],
@@ -81,16 +83,16 @@
         )
 
     def begin(t):
-        for c in range(PAGES):
-
-            @pl.when(t * PAGES + c < count)
+        for c in range(EARLY_PAGES):
+
+            @pl.when(t * EARLY_PAGES + c < count)
             def _():
                 copy(t, c).start()
 
     def end(t):
-        for c in range(PAGES):
-
-            @pl.when(t * PAGES + c < count)
+        for c in range(EARLY_PAGES):
+
+            @pl.when(t * EARLY_PAGES + c < count)
             def _():
                 copy(t, c).wait()
 
@@ -101,7 +103,7 @@
         begin(t + BUFFERS - 1)
         end(t)
         slot = t % BUFFERS
-        rows = pl.ds(pl.multiple_of(t * TILE, TILE), TILE)
+        rows = pl.ds(pl.multiple_of(t * EARLY_TILE, EARLY_TILE), EARLY_TILE)
 
         def depth(k):
             return pl.ds(pl.multiple_of(blocks_ref[k] * DEPTH, DEPTH), DEPTH)
@@ -112,22 +114,23 @@
             part = jnp.dot(buf_ref[slot, :, depth(k)], w, preferred_element_type=F32)
             total = part if total is None else total + part
         acc_ref[rows, :] = total
-        for k in range(n_early, SECTIONS):
-            rest_ref = middle_ref if k < n_early + 4 else late_ref
-            at = (k - n_early) % 4 * DEPTH
-            rest_ref[rows, at : at + DEPTH] = buf_ref[slot, :, depth(k)]
-        for c in range(PAGES):
-            sums = [None] * 4
-            for j in range(D // 128):
-                piece = buf_ref[slot, c * PAGE : (c + 1) * PAGE, j * 128 : (j + 1) * 128]
-                piece = piece.astype(F32)
-                piece = piece * piece
-                sums[j % 4] = piece if sums[j % 4] is None else sums[j % 4] + piece
-            at = pl.multiple_of(t * TILE + c * PAGE, PAGE)
-            squares_ref[pl.ds(at, PAGE), :] = (sums[0] + sums[1]) + (sums[2] + sums[3])
+        for c in range(EARLY_PAGES):
+            at = pl.ds(pl.multiple_of(t * EARLY_TILE + c * PAGE, PAGE), PAGE)
+            sums = [None] * (DEPTH // 128)
+            for k in range(SECTIONS):
+                block = buf_ref[slot, c * PAGE : (c + 1) * PAGE, depth(k)]
+                if k >= n_early:
+                    rest_ref = middle_ref if k < n_early + 4 else late_ref
+                    to = (k - n_early) % 4 * DEPTH
+                    rest_ref[at, to : to + DEPTH] = block
+                for j in range(len(sums)):
+                    piece = block[:, j * 128 : (j + 1) * 128].astype(F32)
+                    piece = piece * piece
+                    sums[j] = piece if sums[j] is None else sums[j] + piece
+            squares_ref[at, :] = (sums[0] + sums[1]) + (sums[2] + sums[3])
         return 0
 
-    lax.fori_loop(0, pl.cdiv(count, PAGES), tile, 0)
+    lax.fori_loop(0, pl.cdiv(count, EARLY_PAGES), tile, 0)
 
 
 def kept(array):
@@ -158,8 +161,8 @@
             pltpu.VMEM((rows, 128), F32),
         ],
         scratch_shapes=[
-            pltpu.VMEM((BUFFERS, TILE, D), BF16),
-            pltpu.SemaphoreType.DMA((BUFFERS, PAGES)),
+            pltpu.VMEM((BUFFERS, EARLY_TILE, D), BF16),
+            pltpu.SemaphoreType.DMA((BUFFERS, EARLY_PAGES)),
         ],
         compiler_params=params(24),
         name="prompt_early",
@@ -195,32 +198,28 @@
 def late_kernel(
     order_ref, turn_ref, count_ref, cos_ref, sin_ref, acc_ref, rest_ref, squares_ref, *refs
 ):
-    w_refs, (pages_ref, tile_ref, cos_tile, sin_tile) = refs[:-4], refs[-4:]
+    w_refs, pages_ref = refs[:-1], refs[-1]
     count = count_ref[0]
     pages_ref[...] = jnp.zeros_like(pages_ref)
 
     def tile(t, _):
         rows = pl.ds(pl.multiple_of(t * TILE, TILE), TILE)
         last = count - 1 - t * PAGES
-        for c in range(PAGES):
-            page = turn_ref[t * PAGES + jnp.minimum(c, last)]
-            turn = pl.ds(pl.multiple_of(page * PAGE, PAGE), PAGE)
-            cos_tile[c * PAGE : (c + 1) * PAGE, :] = cos_ref[turn, :]
-            sin_tile[c * PAGE : (c + 1) * PAGE, :] = sin_ref[turn, :]
         total = acc_ref[rows, :]
         for k, w_ref in enumerate(w_refs):
             x = rest_ref[rows, k * 2 * DEPTH : (k + 1) * 2 * DEPTH]
             total = total + jnp.dot(x, w_ref[...], preferred_element_type=F32)
         mean = jnp.sum(squares_ref[rows, :], axis=-1, keepdims=True) * (1.0 / D)
         total = total * lax.rsqrt(mean + EPS)
-        tile_ref[:, :HD] = turned(total[:, :HD], cos_tile[...], sin_tile[...]).astype(BF16)
-        tile_ref[:, HD:] = total[:, HD:].astype(BF16)
-        for c in range(PAGES):
-            source = jnp.minimum(c, last)
-            slot = order_ref[t * PAGES + source]
-            to = pl.ds(pl.multiple_of((slot % CAP) * PAGE, PAGE), PAGE)
-            here = pl.ds(pl.multiple_of(source * PAGE, PAGE), PAGE)
-            pages_ref[slot // CAP, to, :] = tile_ref[here, :]
+        for c in reversed(range(PAGES)):
+            at = t * PAGES + jnp.minimum(c, last)
+            turn = pl.ds(pl.multiple_of(turn_ref[at] * PAGE, PAGE), PAGE)
+            slot = order_ref[at]
+            to = pl.ds(pl.multiple_of((slot & (CAP - 1)) * PAGE, PAGE), PAGE)
+            here = total[c * PAGE : (c + 1) * PAGE]
+            key = turned(here[:, :HD], cos_ref[turn, :], sin_ref[turn, :])
+            pages_ref[slot // CAP, to, :HD] = key.astype(BF16)
+            pages_ref[slot // CAP, to, HD:] = here[:, HD:].astype(BF16)
         return 0
 
     lax.fori_loop(0, pl.cdiv(count, PAGES), tile, 0)
@@ -232,11 +231,6 @@
         in_specs=[SMEM_SPEC] * 3 + [VMEM_SPEC] * (5 + len(weights)),
         out_specs=VMEM_SPEC,
         out_shape=jax.ShapeDtypeStruct((SECTIONS, GROUP_TOK, WKV), BF16),
-        scratch_shapes=[
-            pltpu.VMEM((TILE, WKV), BF16),
-            pltpu.VMEM((TILE, HD), F32),
-            pltpu.VMEM((TILE, HD), F32),
-        ],
         compiler_params=params(16),
         name="prompt_late",
     )(order, turn, count, cosine, sine, *[kept(array) for array in early], *weights)

time: 97.9 us -> 97.5 us (level)
  waiting for transfers between devices: 20.1 us -> 22.8 us
  starting transfers between devices: 35.5 us -> 32.9 us
  Pallas kernels: 24.7 us -> 23.7 us
    all_to_all x1, waiting for transfers between devices: 12.5 us -> 15.3 us  [on_device(): lax.all_to_all(pages, 'section', split_axis=0, concat_axis=0, tiled=True)]
    all_to_all x1, starting transfers between devices: 7.47 us -> 4.89 us  [on_device(): lax.all_to_all(pages, 'section', split_axis=0, concat_axis=0, tiled=True)]
    pallas_call x1, Pallas kernels: 10.5 us -> 8.59 us  [prompt_early(): pl.pallas_call(functools.partial(early_kernel, n_early), in_specs=[SMEM_S...]
  transfers between devices with their start and end apart: 15 -> 15, of which waited for: 5 -> 5; matrix products, arithmetic and copies ran while one was open for 2% -> 2% of each run, Pallas kernels for 22% -> 21%
where the time goes in v5:
time: 97.5 us; the launch traced here: 96.7 us
  starting transfers between devices  32.9 us (34%)
  Pallas kernels  23.7 us (24%)
  waiting for transfers between devices  22.8 us (23%)
  blocking collectives  13 us (13%)
  local copies, waits for them, and re-layouts  2.73 us (3%)
  other arithmetic  1.21 us (1%)
    ppermute x9, starting transfers between devices, shifted(): return lax.ppermute(array, ('section', 'tensor'), pairs)  17.5 us
    all_to_all x1, waiting for transfers between devices, on_device(): lax.all_to_all(pages, 'section', split_axis=0, concat_axis=0, tiled=True)  15.3 us
    all_to_all x1, blocking collectives, on_device(): lax.all_to_all(attn, 'section', split_axis=0, concat_axis=0, tiled=True)  13 us
    pallas_call x1, Pallas kernels, prompt_early(): pl.pallas_call(functools.partial(early_kernel, n_early), in_specs=[SMEM_S...  8.59 us
    ppermute x3, starting transfers between devices, on_device(): lax.ppermute(piece, 'tensor', [(t, (t + 2 * step) % 8) for t in range(8)])  5.28 us
    all_to_all x1, starting transfers between devices, on_device(): lax.all_to_all(payload, 'section', split_axis=0, concat_axis=0, tiled=True)  5.17 us
    pallas_call x1, Pallas kernels, prompt_late(): pl.pallas_call(late_kernel, in_specs=[SMEM_SPEC] * 3 + [VMEM_SPEC] * (5 +...  4.96 us
    all_to_all x1, starting transfers between devices, on_device(): lax.all_to_all(pages, 'section', split_axis=0, concat_axis=0, tiled=True)  4.89 us
  transfers between devices with their start and end apart: 15, of which 5 were waited for; matrix products, arithmetic and copies ran while one was open for 2% of the time, Pallas kernels for 21%

profile of v5, /device:TPU:0, one launch (start us, length us, event | category | flops | bytes accessed | tf_op | source)
XLA Modules:
  0.0 96.7 jit_solution(9989629831763670249)
XLA Ops:
  0.0 1.1 %with_gain.1 = bf16[512,256]{1,0:T(8,128)(2,1)S(1)} custom-call(f32[1,8192]{1,0:T(1,128)} %bitcast.22, bf16[512,256]{1,0:T(8,128)(2,1)} %kvw_ref.3), custom_call_target="tpu_custom_call" | custom-call | tf_op jit(solution)/shard_map/with_gain/pallas_call | solution.py:250
  1.1 1.6 %collective-permute-start = (bf16[512,256]{1,0:T(8,128)(2,1)S(1)}, bf16[512,256]{1,0:T(8,128)(2,1)S(1)}, u32[]{:S(2)}, u32[]{:S(2)}) collective-permute-start(bf16[512,256]{1,0:T(8,128)(2,1)S(1)} %with_gain.1), channel_id=1, source_target_pairs={{0,8},{1,33},{2,10},{3,35},{4,12},{5,37},{6,14},{7,39},{8,16},{9,4... | collective-permute-start | bytes 786440 | tf_op jit(solution)/shard_map/ppermute | solution.py:61
  2.8 2.7 %collective-permute-start.2 = (bf16[512,256]{1,0:T(8,128)(2,1)S(1)}, bf16[512,256]{1,0:T(8,128)(2,1)S(1)}, u32[]{:S(2)}, u32[]{:S(2)}) collective-permute-start(bf16[512,256]{1,0:T(8,128)(2,1)S(1)} %with_gain.1), channel_id=1, source_target_pairs={{0,16},{1,65},{2,18},{3,67},{4,20},{5,69},{6,22},{7,71},{8,24},{9,... | collective-permute-start | bytes 786440 | tf_op jit(solution)/shard_map/ppermute | solution.py:61
  5.5 1.4 %collective-permute-start.1 = (bf16[512,256]{1,0:T(8,128)(2,1)S(1)}, bf16[512,256]{1,0:T(8,128)(2,1)S(1)}, u32[]{:S(2)}, u32[]{:S(2)}) collective-permute-start(bf16[512,256]{1,0:T(8,128)(2,1)S(1)} %with_gain.1), channel_id=1, source_target_pairs={{0,24},{1,97},{2,26},{3,99},{4,28},{5,101},{6,30},{7,103},{8,0},{9... | collective-permute-start | bytes 786440 | tf_op jit(solution)/shard_map/ppermute | solution.py:61
  8.5 0.9 copy-done
  10.2 2.9 %project.1 = (bf16[16,16,1408]{2,1,0:T(8,128)(2,1)}, s32[128]{0:T(128)S(1)}, s32[128]{0:T(128)S(1)}, s32[1]{0:T(128)}) custom-call(s32[16,8]{1,0:T(8,128)S(1)} %copy.12.slot_ref, bf16[256,512]{1,0:T(8,128)(2,1)} %bitcast.21, f32[1,8192]{1,0:T(1,128)S(1)} %bitcast.23, bf16[512,1024]{1,0:T(8,128)(2,1)} %qw_ref.1, bf16[512,256]{1,0:T(8,128)(2,1)S(1)} %copy-done, ...), custom_call_target="tpu_custom_call" | custom-call | tf_op jit(solution)/shard_map/project/pallas_call | solution.py:296
  13.2 2.0 %collective-permute-start.3 = (bf16[1024,256]{1,0:T(8,128)(2,1)S(1)}, bf16[1024,256]{1,0:T(8,128)(2,1)S(1)}, u32[]{:S(2)}, u32[]{:S(2)}) collective-permute-start(bf16[1024,256]{1,0:T(8,128)(2,1)S(1)} %pad_maximum_fusion.refs_0_), channel_id=1, source_target_pairs={{0,32},{1,9},{2,34},{3,11},{4,36},{5,13},{6,38},{7,15},{8,40},{9,1... | collective-permute-start | bytes 1572872 | tf_op jit(solution)/shard_map/ppermute | solution.py:61
  15.2 2.2 %collective-permute-start.4 = (bf16[1024,256]{1,0:T(8,128)(2,1)S(1)}, bf16[1024,256]{1,0:T(8,128)(2,1)S(1)}, u32[]{:S(2)}, u32[]{:S(2)}) collective-permute-start(bf16[1024,256]{1,0:T(8,128)(2,1)S(1)} %pad_maximum_fusion.1.refs_1_), channel_id=1, source_target_pairs={{0,96},{1,25},{2,98},{3,27},{4,100},{5,29},{6,102},{7,31},{8,104},... | collective-permute-start | bytes 1572872 | tf_op jit(solution)/shard_map/ppermute | solution.py:61
  17.4 5.2 %all-to-all-start.1 = ((bf16[16,16,1408]{2,1,0:T(8,128)(2,1)}), bf16[16,16,1408]{2,1,0:T(8,128)(2,1)S(1)}, u32[]{:S(2)}, u32[]{:S(2)}) async-start(bf16[16,16,1408]{2,1,0:T(8,128)(2,1)} %get-tuple-element.42), calls=%async_computation.1 | async-start | bytes 1441792 | tf_op jit(solution)/shard_map/all_to_all | solution.py:526
  22.9 3.0 %collective-permute-start.5 = (bf16[1024,256]{1,0:T(8,128)(2,1)S(1)}, bf16[1024,256]{1,0:T(8,128)(2,1)S(1)}, u32[]{:S(2)}, u32[]{:S(2)}) collective-permute-start(bf16[1024,256]{1,0:T(8,128)(2,1)S(1)} %pad_maximum_fusion.refs_0_), channel_id=1, source_target_pairs={{0,96},{1,25},{2,98},{3,27},{4,100},{5,29},{6,102},{7,31},{8,104},... | collective-permute-start | bytes 1572872 | tf_op jit(solution)/shard_map/ppermute | solution.py:61
  26.7 2.7 %collective-permute-done.4.refs_3_ = bf16[1024,256]{1,0:T(8,128)(2,1)S(1)} collective-permute-done((bf16[1024,256]{1,0:T(8,128)(2,1)S(1)}, bf16[1024,256]{1,0:T(8,128)(2,1)S(1)}, u32[]{:S(2)}, u32[]{:S(2)}) %collective-permute-start.4) | collective-permute-done | bytes 524320 | tf_op jit(solution)/shard_map/ppermute | solution.py:61
  29.4 3.7 %collective-permute-start.8 = (bf16[1024,256]{1,0:T(8,128)(2,1)S(1)}, bf16[1024,256]{1,0:T(8,128)(2,1)S(1)}, u32[]{:S(2)}, u32[]{:S(2)}) collective-permute-start(bf16[1024,256]{1,0:T(8,128)(2,1)S(1)} %collective-permute-done.4.refs_3_), channel_id=1, source_target_pairs={{0,96},{1,25},{2,98},{3,27},{4,100},{5,29},{6,102},{7,31},{8,104},... | collective-permute-start | bytes 1572872 | tf_op jit(solution)/shard_map/ppermute | solution.py:61
  33.6 8.6 %prompt_early.1 = (f32[2048,256]{1,0:T(8,128)S(1)}, bf16[2048,2048]{1,0:T(8,128)(2,1)S(1)}, bf16[2048,2048]{1,0:T(8,128)(2,1)S(1)}, f32[2048,128]{1,0:T(8,128)S(1)}) custom-call(s32[16]{0:T(128)S(1)} %stack.67.blocks_ref, s32[128]{0:T(128)S(1)} %get-tuple-element.30.order_ref, s32[1]{0:T(128)} %get-tuple-element.32.count_ref, bf16[2048,8192]{1,0:T(8,128)(2,1)} %x_ref.1, ...), custom_call_target="tpu_custom_call" | custom-call | tf_op jit(solution)/shard_map/prompt_early/pallas_call | solution.py:151
  42.2 2.9 %prompt_middle.1.acc_ref = f32[2048,256]{1,0:T(8,128)S(1)} custom-call(s32[1]{0:T(128)} %get-tuple-element.32.count_ref, f32[2048,256]{1,0:T(8,128)S(1)} %get-tuple-element.36.acc_ref, bf16[2048,2048]{1,0:T(8,128)(2,1)S(1)} %get-tuple-element.37.x_ref, bf16[1024,256]{1,0:T(8,128)(2,1)S(1)} %collective-permute-done.5.refs_0_, ...), custom_call_target="tpu_custom_call" | custom-call | tf_op jit(solution)/shard_map/prompt_middle/pallas_call | solution.py:188
  45.1 5.0 %prompt_late.1 = bf16[16,128,256]{2,1,0:T(8,128)(2,1)} custom-call(s32[128]{0:T(128)S(1)} %get-tuple-element.30.order_ref, s32[128]{0:T(128)S(1)} %get-tuple-element.31.turn_ref, s32[1]{0:T(128)} %get-tuple-element.32.count_ref, f32[136,128]{1,0:T(8,128)S(1)} %get-tuple-element.58.cos_ref, f32[136,128]{1,0:T(8,128)S(1)} %get-tuple-element.59.sin_ref, ...), custom_call_target="tpu_custom_call" | custom-call | tf_op jit(solution)/shard_map/prompt_late/pallas_call | solution.py:229
  50.1 4.9 %all-to-all-start = ((bf16[16,128,256]{2,1,0:T(8,128)(2,1)}), bf16[16,128,256]{2,1,0:T(8,128)(2,1)S(1)}, u32[]{:S(2)}, u32[]{:S(2)}) async-start(bf16[16,128,256]{2,1,0:T(8,128)(2,1)} %prompt_late.1), calls=%async_computation | async-start | bytes 2097152 | tf_op jit(solution)/shard_map/all_to_all | solution.py:558
  55.8 15.3 %all-to-all-done.pages_ref = bf16[16,128,256]{2,1,0:T(8,128)(2,1)S(1)} async-done(((bf16[16,128,256]{2,1,0:T(8,128)(2,1)}), bf16[16,128,256]{2,1,0:T(8,128)(2,1)S(1)}, u32[]{:S(2)}, u32[]{:S(2)}) %all-to-all-start) | async-done | bytes 1048608 | tf_op jit(solution)/shard_map/all_to_all | solution.py:558
  71.0 1.4 %attend.1 = (bf16[16,16,1024]{2,1,0:T(8,128)(2,1)S(1)}, bf16[1024,512]{1,0:T(8,128)(2,1)S(1)}) custom-call(bf16[16,128,256]{2,1,0:T(8,128)(2,1)S(1)} %all-to-all-done.pages_ref, bf16[128,128]{1,0:T(8,128)(2,1)S(1)} %get-tuple-element.43.q_ref, bf16[16,128]{1,0:T(8,128)(2,1)S(1)} %get-tuple-element.44.key_ref, ...), custom_call_target="tpu_custom_call" | custom-call | tf_op jit(solution)/shard_map/attend/pallas_call | solution.py:415
  72.4 13.0 %all_to_all.15.attn_ref = bf16[16,16,1024]{2,1,0:T(8,128)(2,1)S(1)} all-to-all(bf16[16,16,1024]{2,1,0:T(8,128)(2,1)S(1)} %get-tuple-element.47), channel_id=1, replica_groups=mesh['section'=16,'tensor'=8] {'section'}, dimensions={0} | all-to-all | bytes 1048576 | tf_op jit(solution)/shard_map/all_to_all | solution.py:560
  86.0 1.3 %collective-permute-done.9.got_ref = bf16[4,32,512]{2,1,0:T(8,128)(2,1)S(1)} collective-permute-done((bf16[4,32,512]{2,1,0:T(8,128)(2,1)S(1)}, bf16[4,32,512]{2,1,0:T(8,128)(2,1)S(1)}, u32[]{:S(2)}, u32[]{:S(2)}) %collective-permute-start.9) | collective-permute-done | bytes 131104 | tf_op jit(solution)/shard_map/ppermute | solution.py:562
  87.4 1.6 %collective-permute-start.10 = (bf16[32,512]{1,0:T(8,128)(2,1)S(1)}, bf16[32,512]{1,0:T(8,128)(2,1)S(1)}, u32[]{:S(2)}, u32[]{:S(2)}) collective-permute-start(bf16[32,512]{1,0:T(8,128)(2,1)S(1)} %get-tuple-element.52), channel_id=1, source_target_pairs={{0,2},{1,3},{2,4},{3,5},{4,6},{5,7},{6,0},{7,1},{8,10},{9,11},{10,... | collective-permute-start | bytes 98312 | tf_op jit(solution)/shard_map/ppermute | solution.py:565
  89.0 1.7 %collective-permute-start.11 = (bf16[32,512]{1,0:T(8,128)(2,1)S(1)}, bf16[32,512]{1,0:T(8,128)(2,1)S(1)}, u32[]{:S(2)}, u32[]{:S(2)}) collective-permute-start(bf16[32,512]{1,0:T(8,128)(2,1)S(1)} %get-tuple-element.53), channel_id=1, source_target_pairs={{0,6},{1,7},{2,0},{3,1},{4,2},{5,3},{6,4},{7,5},{8,14},{9,15},{10,... | collective-permute-start | bytes 98312 | tf_op jit(solution)/shard_map/ppermute | solution.py:565
  90.7 2.0 %collective-permute-start.12 = (bf16[32,512]{1,0:T(8,128)(2,1)S(1)}, bf16[32,512]{1,0:T(8,128)(2,1)S(1)}, u32[]{:S(2)}, u32[]{:S(2)}) collective-permute-start(bf16[32,512]{1,0:T(8,128)(2,1)S(1)} %get-tuple-element.54), channel_id=1, source_target_pairs={{0,4},{1,5},{2,6},{3,7},{4,0},{5,1},{6,2},{7,3},{8,12},{9,13},{10,... | collective-permute-start | bytes 98312 | tf_op jit(solution)/shard_map/ppermute | solution.py:565
  92.9 3.2 %collective-permute-done.12.c_ref = bf16[32,512]{1,0:T(8,128)(2,1)S(1)} collective-permute-done((bf16[32,512]{1,0:T(8,128)(2,1)S(1)}, bf16[32,512]{1,0:T(8,128)(2,1)S(1)}, u32[]{:S(2)}, u32[]{:S(2)}) %collective-permute-start.12) | collective-permute-done | bytes 32800 | tf_op jit(solution)/shard_map/ppermute | solution.py:565
  (36 shorter events, 6.1 us)
Async XLA Ops:
  1.1 12.0 %collective-permute-start = (bf16[512,256]{1,0:T(8,128)(2,1)S(1)}, bf16[512,256]{1,0:T(8,128)(2,1)S(1)}, u32[]{:S(2)}, u32[]{:S(2)}) collective-permute-start(bf16[512,256]{1,0:T(8,128)(2,1)S(1)} %with_gain.1), channel_id=1, source_target_pairs={{0,8},{1,33},{2,10},{3,35},{4,12},{5,37},{6,14},{7,39},{8,16},{9,4... | collective-permute-start | bytes 786440 | tf_op jit(solution)/shard_map/ppermute | solution.py:61
  2.8 10.4 %collective-permute-start.2 = (bf16[512,256]{1,0:T(8,128)(2,1)S(1)}, bf16[512,256]{1,0:T(8,128)(2,1)S(1)}, u32[]{:S(2)}, u32[]{:S(2)}) collective-permute-start(bf16[512,256]{1,0:T(8,128)(2,1)S(1)} %with_gain.1), channel_id=1, source_target_pairs={{0,16},{1,65},{2,18},{3,67},{4,20},{5,69},{6,22},{7,71},{8,24},{9,... | collective-permute-start | bytes 786440 | tf_op jit(solution)/shard_map/ppermute | solution.py:61
  5.5 7.7 %collective-permute-start.1 = (bf16[512,256]{1,0:T(8,128)(2,1)S(1)}, bf16[512,256]{1,0:T(8,128)(2,1)S(1)}, u32[]{:S(2)}, u32[]{:S(2)}) collective-permute-start(bf16[512,256]{1,0:T(8,128)(2,1)S(1)} %with_gain.1), channel_id=1, source_target_pairs={{0,24},{1,97},{2,26},{3,99},{4,28},{5,101},{6,30},{7,103},{8,0},{9... | collective-permute-start | bytes 786440 | tf_op jit(solution)/shard_map/ppermute | solution.py:61
  8.5 1.0 copy-start
  9.5 0.8 copy-start.2
  13.2 12.7 %collective-permute-start.3 = (bf16[1024,256]{1,0:T(8,128)(2,1)S(1)}, bf16[1024,256]{1,0:T(8,128)(2,1)S(1)}, u32[]{:S(2)}, u32[]{:S(2)}) collective-permute-start(bf16[1024,256]{1,0:T(8,128)(2,1)S(1)} %pad_maximum_fusion.refs_0_), channel_id=1, source_target_pairs={{0,32},{1,9},{2,34},{3,11},{4,36},{5,13},{6,38},{7,15},{8,40},{9,1... | collective-permute-start | bytes 1572872 | tf_op jit(solution)/shard_map/ppermute | solution.py:61
  15.2 14.2 %collective-permute-start.4 = (bf16[1024,256]{1,0:T(8,128)(2,1)S(1)}, bf16[1024,256]{1,0:T(8,128)(2,1)S(1)}, u32[]{:S(2)}, u32[]{:S(2)}) collective-permute-start(bf16[1024,256]{1,0:T(8,128)(2,1)S(1)} %pad_maximum_fusion.1.refs_1_), channel_id=1, source_target_pairs={{0,96},{1,25},{2,98},{3,27},{4,100},{5,29},{6,102},{7,31},{8,104},... | collective-permute-start | bytes 1572872 | tf_op jit(solution)/shard_map/ppermute | solution.py:61
  17.4 32.6 %all-to-all-start.1 = ((bf16[16,16,1408]{2,1,0:T(8,128)(2,1)}), bf16[16,16,1408]{2,1,0:T(8,128)(2,1)S(1)}, u32[]{:S(2)}, u32[]{:S(2)}) async-start(bf16[16,16,1408]{2,1,0:T(8,128)(2,1)} %get-tuple-element.42), calls=%async_computation.1 | async-start | bytes 1441792 | tf_op jit(solution)/shard_map/all_to_all | solution.py:526
  22.9 19.3 %collective-permute-start.5 = (bf16[1024,256]{1,0:T(8,128)(2,1)S(1)}, bf16[1024,256]{1,0:T(8,128)(2,1)S(1)}, u32[]{:S(2)}, u32[]{:S(2)}) collective-permute-start(bf16[1024,256]{1,0:T(8,128)(2,1)S(1)} %pad_maximum_fusion.refs_0_), channel_id=1, source_target_pairs={{0,96},{1,25},{2,98},{3,27},{4,100},{5,29},{6,102},{7,31},{8,104},... | collective-permute-start | bytes 1572872 | tf_op jit(solution)/shard_map/ppermute | solution.py:61
  25.9 16.3 %collective-permute-start.6 = (bf16[1024,256]{1,0:T(8,128)(2,1)S(1)}, bf16[1024,256]{1,0:T(8,128)(2,1)S(1)}, u32[]{:S(2)}, u32[]{:S(2)}) collective-permute-start(bf16[1024,256]{1,0:T(8,128)(2,1)S(1)} %pad_maximum_fusion.1.refs_1_), channel_id=1, source_target_pairs={{0,32},{1,9},{2,34},{3,11},{4,36},{5,13},{6,38},{7,15},{8,40},{9,1... | collective-permute-start | bytes 1572872 | tf_op jit(solution)/shard_map/ppermute | solution.py:61
  25.9 19.2 %collective-permute-start.7 = (bf16[1024,256]{1,0:T(8,128)(2,1)S(1)}, bf16[1024,256]{1,0:T(8,128)(2,1)S(1)}, u32[]{:S(2)}, u32[]{:S(2)}) collective-permute-start(bf16[1024,256]{1,0:T(8,128)(2,1)S(1)} %collective-permute-done.3.refs_2_), channel_id=1, source_target_pairs={{0,32},{1,9},{2,34},{3,11},{4,36},{5,13},{6,38},{7,15},{8,40},{9,1... | collective-permute-start | bytes 1572872 | tf_op jit(solution)/shard_map/ppermute | solution.py:61
  29.4 15.6 %collective-permute-start.8 = (bf16[1024,256]{1,0:T(8,128)(2,1)S(1)}, bf16[1024,256]{1,0:T(8,128)(2,1)S(1)}, u32[]{:S(2)}, u32[]{:S(2)}) collective-permute-start(bf16[1024,256]{1,0:T(8,128)(2,1)S(1)} %collective-permute-done.4.refs_3_), channel_id=1, source_target_pairs={{0,96},{1,25},{2,98},{3,27},{4,100},{5,29},{6,102},{7,31},{8,104},... | collective-permute-start | bytes 1572872 | tf_op jit(solution)/shard_map/ppermute | solution.py:61
  45.0 9.9 %copy-start.3 = (s32[8]{0:T(128)S(1)}, s32[8]{0:T(128)}, u32[]{:S(2)}) copy-start(s32[8]{0:T(128)} %ctx_ref.1) | copy-start | bytes 100
  45.1 51.0 %copy-start.1 = (bf16[2,128,512]{2,1,0:T(8,128)(2,1)S(1)}, bf16[2,128,512]{2,1,0:T(8,128)(2,1)}, u32[]{:S(2)}) copy-start(bf16[2,128,512]{2,1,0:T(8,128)(2,1)} %tok_ref.1) | copy-start | bytes 786436
  50.1 21.0 %all-to-all-start = ((bf16[16,128,256]{2,1,0:T(8,128)(2,1)}), bf16[16,128,256]{2,1,0:T(8,128)(2,1)S(1)}, u32[]{:S(2)}, u32[]{:S(2)}) async-start(bf16[16,128,256]{2,1,0:T(8,128)(2,1)} %prompt_late.1), calls=%async_computation | async-start | bytes 2097152 | tf_op jit(solution)/shard_map/all_to_all | solution.py:558
  85.9 1.4 %collective-permute-start.9 = (bf16[4,32,512]{2,1,0:T(8,128)(2,1)S(1)}, bf16[4,32,512]{2,1,0:T(8,128)(2,1)S(1)}, u32[]{:S(2)}, u32[]{:S(2)}) collective-permute-start(bf16[4,32,512]{2,1,0:T(8,128)(2,1)S(1)} %get-tuple-element.50), channel_id=1, source_target_pairs={{0,1},{1,0},{2,3},{3,2},{4,5},{5,4},{6,7},{7,6},{8,9},{9,8},{10,11... | collective-permute-start | bytes 393224 | tf_op jit(solution)/shard_map/ppermute | solution.py:562
  87.4 5.3 %collective-permute-start.10 = (bf16[32,512]{1,0:T(8,128)(2,1)S(1)}, bf16[32,512]{1,0:T(8,128)(2,1)S(1)}, u32[]{:S(2)}, u32[]{:S(2)}) collective-permute-start(bf16[32,512]{1,0:T(8,128)(2,1)S(1)} %get-tuple-element.52), channel_id=1, source_target_pairs={{0,2},{1,3},{2,4},{3,5},{4,6},{5,7},{6,0},{7,1},{8,10},{9,11},{10,... | collective-permute-start | bytes 98312 | tf_op jit(solution)/shard_map/ppermute | solution.py:565
  89.0 3.9 %collective-permute-start.11 = (bf16[32,512]{1,0:T(8,128)(2,1)S(1)}, bf16[32,512]{1,0:T(8,128)(2,1)S(1)}, u32[]{:S(2)}, u32[]{:S(2)}) collective-permute-start(bf16[32,512]{1,0:T(8,128)(2,1)S(1)} %get-tuple-element.53), channel_id=1, source_target_pairs={{0,6},{1,7},{2,0},{3,1},{4,2},{5,3},{6,4},{7,5},{8,14},{9,15},{10,... | collective-permute-start | bytes 98312 | tf_op jit(solution)/shard_map/ppermute | solution.py:565
  90.7 5.4 %collective-permute-start.12 = (bf16[32,512]{1,0:T(8,128)(2,1)S(1)}, bf16[32,512]{1,0:T(8,128)(2,1)S(1)}, u32[]{:S(2)}, u32[]{:S(2)}) collective-permute-start(bf16[32,512]{1,0:T(8,128)(2,1)S(1)} %get-tuple-element.54), channel_id=1, source_target_pairs={{0,4},{1,5},{2,6},{3,7},{4,0},{5,1},{6,2},{7,3},{8,12},{9,13},{10,... | collective-permute-start | bytes 98312 | tf_op jit(solution)/shard_map/ppermute | solution.py:565

commit v6 on v5

--- a/solution.py
+++ b/solution.py
@@ -448,7 +448,7 @@
     )(attn, kept(o_weight))
 
 
-CHIP_STEPS = (1, 3, 2)
+CHIP_STEPS = (2, 1, 3)
 
 
 def pair_kernel(mine_ref, got_ref, own_ref, *out_refs):
@@ -526,9 +526,8 @@
     got = lax.all_to_all(payload, "section", split_axis=0, concat_axis=0, tiled=True)
     near_p = shifted(near, 1, 1)
     far_m = shifted(far, 1, -1)
-    near_2, far_2 = lax.optimization_barrier((near, far))
-    far_p = shifted(far_2, 1, 1)
-    near_m = shifted(near_2, 1, -1)
+    far_p = shifted(far, 1, 1)
+    near_m = shifted(near, 1, -1)
     near_o = shifted(near_p, 1, 1)
     far_o = shifted(far_m, 1, -1)
 

time: 97.5 us -> 97.3 us (level)
  starting transfers between devices: 32.9 us -> 35.1 us
  Pallas kernels: 23.7 us -> 22.1 us
    ppermute x3, waiting for transfers between devices: 3.44 us -> 1.89 us  [on_device(): lax.ppermute(piece, 'tensor', [(t, (t + 2 * step) % 8) for t in range(8)])]
    ppermute x3, starting transfers between devices: 5.28 us -> 6.51 us  [on_device(): lax.ppermute(piece, 'tensor', [(t, (t + 2 * step) % 8) for t in range(8)])]
  transfers between devices with their start and end apart: 15 -> 15, of which waited for: 5 -> 5; matrix products, arithmetic and copies ran while one was open for 2% -> 2% of each run, Pallas kernels for 21% -> 19%
where the time goes in v6:
time: 97.3 us; the launch traced here: 96.8 us
  starting transfers between devices  35.1 us (36%)
  waiting for transfers between devices  22.2 us (23%)
  Pallas kernels  22.1 us (23%)
  blocking collectives  13.1 us (13%)
  local copies, waits for them, and re-layouts  2.73 us (3%)
  other arithmetic  1.21 us (1%)
    ppermute x9, starting transfers between devices, shifted(): return lax.ppermute(array, ('section', 'tensor'), pairs)  17.5 us
    all_to_all x1, waiting for transfers between devices, on_device(): lax.all_to_all(pages, 'section', split_axis=0, concat_axis=0, tiled=True)  15.4 us
    all_to_all x1, blocking collectives, on_device(): lax.all_to_all(attn, 'section', split_axis=0, concat_axis=0, tiled=True)  13.1 us
    pallas_call x1, Pallas kernels, prompt_early(): pl.pallas_call(functools.partial(early_kernel, n_early), in_specs=[SMEM_S...  8.03 us
    ppermute x3, starting transfers between devices, on_device(): lax.ppermute(piece, 'tensor', [(t, (t + 2 * step) % 8) for t in range(8)])  6.51 us
    all_to_all x1, starting transfers between devices, on_device(): lax.all_to_all(pages, 'section', split_axis=0, concat_axis=0, tiled=True)  5.86 us
    all_to_all x1, starting transfers between devices, on_device(): lax.all_to_all(payload, 'section', split_axis=0, concat_axis=0, tiled=True)  5.17 us
    pallas_call x1, Pallas kernels, prompt_late(): pl.pallas_call(late_kernel, in_specs=[SMEM_SPEC] * 3 + [VMEM_SPEC] * (5 +...  4.43 us
  transfers between devices with their start and end apart: 15, of which 5 were waited for; matrix products, arithmetic and copies ran while one was open for 2% of the time, Pallas kernels for 19%

profile of v6, /device:TPU:0, one launch (start us, length us, event | category | flops | bytes accessed | tf_op | source)
XLA Modules:
  0.0 96.8 jit_solution(661955697101769690)
XLA Ops:
  0.0 1.1 %with_gain.1 = bf16[512,256]{1,0:T(8,128)(2,1)S(1)} custom-call(f32[1,8192]{1,0:T(1,128)} %bitcast.22, bf16[512,256]{1,0:T(8,128)(2,1)} %kvw_ref.3), custom_call_target="tpu_custom_call" | custom-call | tf_op jit(solution)/shard_map/with_gain/pallas_call | solution.py:250
  1.1 1.6 %collective-permute-start = (bf16[512,256]{1,0:T(8,128)(2,1)S(1)}, bf16[512,256]{1,0:T(8,128)(2,1)S(1)}, u32[]{:S(2)}, u32[]{:S(2)}) collective-permute-start(bf16[512,256]{1,0:T(8,128)(2,1)S(1)} %with_gain.1), channel_id=1, source_target_pairs={{0,8},{1,33},{2,10},{3,35},{4,12},{5,37},{6,14},{7,39},{8,16},{9,4... | collective-permute-start | bytes 786440 | tf_op jit(solution)/shard_map/ppermute | solution.py:61
  2.8 2.7 %collective-permute-start.2 = (bf16[512,256]{1,0:T(8,128)(2,1)S(1)}, bf16[512,256]{1,0:T(8,128)(2,1)S(1)}, u32[]{:S(2)}, u32[]{:S(2)}) collective-permute-start(bf16[512,256]{1,0:T(8,128)(2,1)S(1)} %with_gain.1), channel_id=1, source_target_pairs={{0,16},{1,65},{2,18},{3,67},{4,20},{5,69},{6,22},{7,71},{8,24},{9,... | collective-permute-start | bytes 786440 | tf_op jit(solution)/shard_map/ppermute | solution.py:61
  5.5 1.4 %collective-permute-start.1 = (bf16[512,256]{1,0:T(8,128)(2,1)S(1)}, bf16[512,256]{1,0:T(8,128)(2,1)S(1)}, u32[]{:S(2)}, u32[]{:S(2)}) collective-permute-start(bf16[512,256]{1,0:T(8,128)(2,1)S(1)} %with_gain.1), channel_id=1, source_target_pairs={{0,24},{1,97},{2,26},{3,99},{4,28},{5,101},{6,30},{7,103},{8,0},{9... | collective-permute-start | bytes 786440 | tf_op jit(solution)/shard_map/ppermute | solution.py:61
  8.5 0.9 copy-done
  10.2 2.9 %project.1 = (bf16[16,16,1408]{2,1,0:T(8,128)(2,1)}, s32[128]{0:T(128)S(1)}, s32[128]{0:T(128)S(1)}, s32[1]{0:T(128)}) custom-call(s32[16,8]{1,0:T(8,128)S(1)} %copy.12.slot_ref, bf16[256,512]{1,0:T(8,128)(2,1)} %bitcast.21, f32[1,8192]{1,0:T(1,128)S(1)} %bitcast.23, bf16[512,1024]{1,0:T(8,128)(2,1)} %qw_ref.1, bf16[512,256]{1,0:T(8,128)(2,1)S(1)} %copy-done, ...), custom_call_target="tpu_custom_call" | custom-call | tf_op jit(solution)/shard_map/project/pallas_call | solution.py:296
  13.2 2.0 %collective-permute-start.3 = (bf16[1024,256]{1,0:T(8,128)(2,1)S(1)}, bf16[1024,256]{1,0:T(8,128)(2,1)S(1)}, u32[]{:S(2)}, u32[]{:S(2)}) collective-permute-start(bf16[1024,256]{1,0:T(8,128)(2,1)S(1)} %pad_maximum_fusion.refs_0_), channel_id=1, source_target_pairs={{0,32},{1,9},{2,34},{3,11},{4,36},{5,13},{6,38},{7,15},{8,40},{9,1... | collective-permute-start | bytes 1572872 | tf_op jit(solution)/shard_map/ppermute | solution.py:61
  15.2 2.2 %collective-permute-start.4 = (bf16[1024,256]{1,0:T(8,128)(2,1)S(1)}, bf16[1024,256]{1,0:T(8,128)(2,1)S(1)}, u32[]{:S(2)}, u32[]{:S(2)}) collective-permute-start(bf16[1024,256]{1,0:T(8,128)(2,1)S(1)} %pad_maximum_fusion.1.refs_1_), channel_id=1, source_target_pairs={{0,96},{1,25},{2,98},{3,27},{4,100},{5,29},{6,102},{7,31},{8,104},... | collective-permute-start | bytes 1572872 | tf_op jit(solution)/shard_map/ppermute | solution.py:61
  17.4 5.2 %all-to-all-start.1 = ((bf16[16,16,1408]{2,1,0:T(8,128)(2,1)}), bf16[16,16,1408]{2,1,0:T(8,128)(2,1)S(1)}, u32[]{:S(2)}, u32[]{:S(2)}) async-start(bf16[16,16,1408]{2,1,0:T(8,128)(2,1)} %get-tuple-element.38), calls=%async_computation.1 | async-start | bytes 1441792 | tf_op jit(solution)/shard_map/all_to_all | solution.py:526
  22.9 3.0 %collective-permute-start.5 = (bf16[1024,256]{1,0:T(8,128)(2,1)S(1)}, bf16[1024,256]{1,0:T(8,128)(2,1)S(1)}, u32[]{:S(2)}, u32[]{:S(2)}) collective-permute-start(bf16[1024,256]{1,0:T(8,128)(2,1)S(1)} %pad_maximum_fusion.refs_0_), channel_id=1, source_target_pairs={{0,96},{1,25},{2,98},{3,27},{4,100},{5,29},{6,102},{7,31},{8,104},... | collective-permute-start | bytes 1572872 | tf_op jit(solution)/shard_map/ppermute | solution.py:61
  25.9 0.8 collective-permute-start.7
  26.7 2.7 %collective-permute-done.4.refs_3_ = bf16[1024,256]{1,0:T(8,128)(2,1)S(1)} collective-permute-done((bf16[1024,256]{1,0:T(8,128)(2,1)S(1)}, bf16[1024,256]{1,0:T(8,128)(2,1)S(1)}, u32[]{:S(2)}, u32[]{:S(2)}) %collective-permute-start.4) | collective-permute-done | bytes 524320 | tf_op jit(solution)/shard_map/ppermute | solution.py:61
  29.4 3.7 %collective-permute-start.8 = (bf16[1024,256]{1,0:T(8,128)(2,1)S(1)}, bf16[1024,256]{1,0:T(8,128)(2,1)S(1)}, u32[]{:S(2)}, u32[]{:S(2)}) collective-permute-start(bf16[1024,256]{1,0:T(8,128)(2,1)S(1)} %collective-permute-done.4.refs_3_), channel_id=1, source_target_pairs={{0,96},{1,25},{2,98},{3,27},{4,100},{5,29},{6,102},{7,31},{8,104},... | collective-permute-start | bytes 1572872 | tf_op jit(solution)/shard_map/ppermute | solution.py:61
  33.6 8.0 %prompt_early.1 = (f32[2048,256]{1,0:T(8,128)S(1)}, bf16[2048,2048]{1,0:T(8,128)(2,1)S(1)}, bf16[2048,2048]{1,0:T(8,128)(2,1)S(1)}, f32[2048,128]{1,0:T(8,128)S(1)}) custom-call(s32[16]{0:T(128)S(1)} %stack.67.blocks_ref, s32[128]{0:T(128)S(1)} %get-tuple-element.28.order_ref, s32[1]{0:T(128)} %get-tuple-element.30.count_ref, bf16[2048,8192]{1,0:T(8,128)(2,1)} %x_ref.1, ...), custom_call_target="tpu_custom_call" | custom-call | tf_op jit(solution)/shard_map/prompt_early/pallas_call | solution.py:151
  41.6 2.4 %prompt_middle.1.acc_ref = f32[2048,256]{1,0:T(8,128)S(1)} custom-call(s32[1]{0:T(128)} %get-tuple-element.30.count_ref, f32[2048,256]{1,0:T(8,128)S(1)} %get-tuple-element.34.acc_ref, bf16[2048,2048]{1,0:T(8,128)(2,1)S(1)} %get-tuple-element.35.x_ref, bf16[1024,256]{1,0:T(8,128)(2,1)S(1)} %collective-permute-done.5.refs_0_, ...), custom_call_target="tpu_custom_call" | custom-call | tf_op jit(solution)/shard_map/prompt_middle/pallas_call | solution.py:188
  44.8 4.4 %prompt_late.1 = bf16[16,128,256]{2,1,0:T(8,128)(2,1)} custom-call(s32[128]{0:T(128)S(1)} %get-tuple-element.28.order_ref, s32[128]{0:T(128)S(1)} %get-tuple-element.29.turn_ref, s32[1]{0:T(128)} %get-tuple-element.30.count_ref, f32[136,128]{1,0:T(8,128)S(1)} %get-tuple-element.54.cos_ref, f32[136,128]{1,0:T(8,128)S(1)} %get-tuple-element.55.sin_ref, ...), custom_call_target="tpu_custom_call" | custom-call | tf_op jit(solution)/shard_map/prompt_late/pallas_call | solution.py:229
  49.3 5.9 %all-to-all-start = ((bf16[16,128,256]{2,1,0:T(8,128)(2,1)}), bf16[16,128,256]{2,1,0:T(8,128)(2,1)S(1)}, u32[]{:S(2)}, u32[]{:S(2)}) async-start(bf16[16,128,256]{2,1,0:T(8,128)(2,1)} %prompt_late.1), calls=%async_computation | async-start | bytes 2097152 | tf_op jit(solution)/shard_map/all_to_all | solution.py:557
  55.9 15.4 %all-to-all-done.pages_ref = bf16[16,128,256]{2,1,0:T(8,128)(2,1)S(1)} async-done(((bf16[16,128,256]{2,1,0:T(8,128)(2,1)}), bf16[16,128,256]{2,1,0:T(8,128)(2,1)S(1)}, u32[]{:S(2)}, u32[]{:S(2)}) %all-to-all-start) | async-done | bytes 1048608 | tf_op jit(solution)/shard_map/all_to_all | solution.py:557
  71.3 1.4 %attend.1 = (bf16[16,16,1024]{2,1,0:T(8,128)(2,1)S(1)}, bf16[1024,512]{1,0:T(8,128)(2,1)S(1)}) custom-call(bf16[16,128,256]{2,1,0:T(8,128)(2,1)S(1)} %all-to-all-done.pages_ref, bf16[128,128]{1,0:T(8,128)(2,1)S(1)} %get-tuple-element.39.q_ref, bf16[16,128]{1,0:T(8,128)(2,1)S(1)} %get-tuple-element.40.key_ref, ...), custom_call_target="tpu_custom_call" | custom-call | tf_op jit(solution)/shard_map/attend/pallas_call | solution.py:415
  72.7 13.1 %all_to_all.15.attn_ref = bf16[16,16,1024]{2,1,0:T(8,128)(2,1)S(1)} all-to-all(bf16[16,16,1024]{2,1,0:T(8,128)(2,1)S(1)} %get-tuple-element.43), channel_id=1, replica_groups=mesh['section'=16,'tensor'=8] {'section'}, dimensions={0} | all-to-all | bytes 1048576 | tf_op jit(solution)/shard_map/all_to_all | solution.py:559
  86.4 1.3 %collective-permute-done.9.got_ref = bf16[4,32,512]{2,1,0:T(8,128)(2,1)S(1)} collective-permute-done((bf16[4,32,512]{2,1,0:T(8,128)(2,1)S(1)}, bf16[4,32,512]{2,1,0:T(8,128)(2,1)S(1)}, u32[]{:S(2)}, u32[]{:S(2)}) %collective-permute-start.9) | collective-permute-done | bytes 131104 | tf_op jit(solution)/shard_map/ppermute | solution.py:561
  87.7 3.3 %collective-permute-start.10 = (bf16[32,512]{1,0:T(8,128)(2,1)S(1)}, bf16[32,512]{1,0:T(8,128)(2,1)S(1)}, u32[]{:S(2)}, u32[]{:S(2)}) collective-permute-start(bf16[32,512]{1,0:T(8,128)(2,1)S(1)} %get-tuple-element.48), channel_id=1, source_target_pairs={{0,4},{1,5},{2,6},{3,7},{4,0},{5,1},{6,2},{7,3},{8,12},{9,13},{10,... | collective-permute-start | bytes 98312 | tf_op jit(solution)/shard_map/ppermute | solution.py:564
  91.7 2.6 %collective-permute-start.12 = (bf16[32,512]{1,0:T(8,128)(2,1)S(1)}, bf16[32,512]{1,0:T(8,128)(2,1)S(1)}, u32[]{:S(2)}, u32[]{:S(2)}) collective-permute-start(bf16[32,512]{1,0:T(8,128)(2,1)S(1)} %get-tuple-element.50), channel_id=1, source_target_pairs={{0,6},{1,7},{2,0},{3,1},{4,2},{5,3},{6,4},{7,5},{8,14},{9,15},{10,... | collective-permute-start | bytes 98312 | tf_op jit(solution)/shard_map/ppermute | solution.py:564
  94.2 1.9 %collective-permute-done.11.b_ref = bf16[32,512]{1,0:T(8,128)(2,1)S(1)} collective-permute-done((bf16[32,512]{1,0:T(8,128)(2,1)S(1)}, bf16[32,512]{1,0:T(8,128)(2,1)S(1)}, u32[]{:S(2)}, u32[]{:S(2)}) %collective-permute-start.11) | collective-permute-done | bytes 32800 | tf_op jit(solution)/shard_map/ppermute | solution.py:564
  (36 shorter events, 6.5 us)
Async XLA Ops:
  1.1 12.0 %collective-permute-start = (bf16[512,256]{1,0:T(8,128)(2,1)S(1)}, bf16[512,256]{1,0:T(8,128)(2,1)S(1)}, u32[]{:S(2)}, u32[]{:S(2)}) collective-permute-start(bf16[512,256]{1,0:T(8,128)(2,1)S(1)} %with_gain.1), channel_id=1, source_target_pairs={{0,8},{1,33},{2,10},{3,35},{4,12},{5,37},{6,14},{7,39},{8,16},{9,4... | collective-permute-start | bytes 786440 | tf_op jit(solution)/shard_map/ppermute | solution.py:61
  2.8 10.4 %collective-permute-start.2 = (bf16[512,256]{1,0:T(8,128)(2,1)S(1)}, bf16[512,256]{1,0:T(8,128)(2,1)S(1)}, u32[]{:S(2)}, u32[]{:S(2)}) collective-permute-start(bf16[512,256]{1,0:T(8,128)(2,1)S(1)} %with_gain.1), channel_id=1, source_target_pairs={{0,16},{1,65},{2,18},{3,67},{4,20},{5,69},{6,22},{7,71},{8,24},{9,... | collective-permute-start | bytes 786440 | tf_op jit(solution)/shard_map/ppermute | solution.py:61
  5.5 7.7 %collective-permute-start.1 = (bf16[512,256]{1,0:T(8,128)(2,1)S(1)}, bf16[512,256]{1,0:T(8,128)(2,1)S(1)}, u32[]{:S(2)}, u32[]{:S(2)}) collective-permute-start(bf16[512,256]{1,0:T(8,128)(2,1)S(1)} %with_gain.1), channel_id=1, source_target_pairs={{0,24},{1,97},{2,26},{3,99},{4,28},{5,101},{6,30},{7,103},{8,0},{9... | collective-permute-start | bytes 786440 | tf_op jit(solution)/shard_map/ppermute | solution.py:61
  8.5 1.0 copy-start
  9.5 0.8 copy-start.2
  13.2 12.7 %collective-permute-start.3 = (bf16[1024,256]{1,0:T(8,128)(2,1)S(1)}, bf16[1024,256]{1,0:T(8,128)(2,1)S(1)}, u32[]{:S(2)}, u32[]{:S(2)}) collective-permute-start(bf16[1024,256]{1,0:T(8,128)(2,1)S(1)} %pad_maximum_fusion.refs_0_), channel_id=1, source_target_pairs={{0,32},{1,9},{2,34},{3,11},{4,36},{5,13},{6,38},{7,15},{8,40},{9,1... | collective-permute-start | bytes 1572872 | tf_op jit(solution)/shard_map/ppermute | solution.py:61
  15.2 14.2 %collective-permute-start.4 = (bf16[1024,256]{1,0:T(8,128)(2,1)S(1)}, bf16[1024,256]{1,0:T(8,128)(2,1)S(1)}, u32[]{:S(2)}, u32[]{:S(2)}) collective-permute-start(bf16[1024,256]{1,0:T(8,128)(2,1)S(1)} %pad_maximum_fusion.1.refs_1_), channel_id=1, source_target_pairs={{0,96},{1,25},{2,98},{3,27},{4,100},{5,29},{6,102},{7,31},{8,104},... | collective-permute-start | bytes 1572872 | tf_op jit(solution)/shard_map/ppermute | solution.py:61
  17.4 31.9 %all-to-all-start.1 = ((bf16[16,16,1408]{2,1,0:T(8,128)(2,1)}), bf16[16,16,1408]{2,1,0:T(8,128)(2,1)S(1)}, u32[]{:S(2)}, u32[]{:S(2)}) async-start(bf16[16,16,1408]{2,1,0:T(8,128)(2,1)} %get-tuple-element.38), calls=%async_computation.1 | async-start | bytes 1441792 | tf_op jit(solution)/shard_map/all_to_all | solution.py:526
  22.9 18.8 %collective-permute-start.5 = (bf16[1024,256]{1,0:T(8,128)(2,1)S(1)}, bf16[1024,256]{1,0:T(8,128)(2,1)S(1)}, u32[]{:S(2)}, u32[]{:S(2)}) collective-permute-start(bf16[1024,256]{1,0:T(8,128)(2,1)S(1)} %pad_maximum_fusion.refs_0_), channel_id=1, source_target_pairs={{0,96},{1,25},{2,98},{3,27},{4,100},{5,29},{6,102},{7,31},{8,104},... | collective-permute-start | bytes 1572872 | tf_op jit(solution)/shard_map/ppermute | solution.py:61
  25.9 15.7 %collective-permute-start.6 = (bf16[1024,256]{1,0:T(8,128)(2,1)S(1)}, bf16[1024,256]{1,0:T(8,128)(2,1)S(1)}, u32[]{:S(2)}, u32[]{:S(2)}) collective-permute-start(bf16[1024,256]{1,0:T(8,128)(2,1)S(1)} %pad_maximum_fusion.1.refs_1_), channel_id=1, source_target_pairs={{0,32},{1,9},{2,34},{3,11},{4,36},{5,13},{6,38},{7,15},{8,40},{9,1... | collective-permute-start | bytes 1572872 | tf_op jit(solution)/shard_map/ppermute | solution.py:61
  25.9 18.9 %collective-permute-start.7 = (bf16[1024,256]{1,0:T(8,128)(2,1)S(1)}, bf16[1024,256]{1,0:T(8,128)(2,1)S(1)}, u32[]{:S(2)}, u32[]{:S(2)}) collective-permute-start(bf16[1024,256]{1,0:T(8,128)(2,1)S(1)} %collective-permute-done.3.refs_2_), channel_id=1, source_target_pairs={{0,32},{1,9},{2,34},{3,11},{4,36},{5,13},{6,38},{7,15},{8,40},{9,1... | collective-permute-start | bytes 1572872 | tf_op jit(solution)/shard_map/ppermute | solution.py:61
  29.4 15.4 %collective-permute-start.8 = (bf16[1024,256]{1,0:T(8,128)(2,1)S(1)}, bf16[1024,256]{1,0:T(8,128)(2,1)S(1)}, u32[]{:S(2)}, u32[]{:S(2)}) collective-permute-start(bf16[1024,256]{1,0:T(8,128)(2,1)S(1)} %collective-permute-done.4.refs_3_), channel_id=1, source_target_pairs={{0,96},{1,25},{2,98},{3,27},{4,100},{5,29},{6,102},{7,31},{8,104},... | collective-permute-start | bytes 1572872 | tf_op jit(solution)/shard_map/ppermute | solution.py:61
  44.1 11.1 %copy-start.3 = (s32[8]{0:T(128)S(1)}, s32[8]{0:T(128)}, u32[]{:S(2)}) copy-start(s32[8]{0:T(128)} %ctx_ref.1) | copy-start | bytes 100
  44.8 51.3 %copy-start.1 = (bf16[2,128,512]{2,1,0:T(8,128)(2,1)S(1)}, bf16[2,128,512]{2,1,0:T(8,128)(2,1)}, u32[]{:S(2)}) copy-start(bf16[2,128,512]{2,1,0:T(8,128)(2,1)} %tok_ref.1) | copy-start | bytes 786436
  49.3 22.1 %all-to-all-start = ((bf16[16,128,256]{2,1,0:T(8,128)(2,1)}), bf16[16,128,256]{2,1,0:T(8,128)(2,1)S(1)}, u32[]{:S(2)}, u32[]{:S(2)}) async-start(bf16[16,128,256]{2,1,0:T(8,128)(2,1)} %prompt_late.1), calls=%async_computation | async-start | bytes 2097152 | tf_op jit(solution)/shard_map/all_to_all | solution.py:557
  86.3 1.4 %collective-permute-start.9 = (bf16[4,32,512]{2,1,0:T(8,128)(2,1)S(1)}, bf16[4,32,512]{2,1,0:T(8,128)(2,1)S(1)}, u32[]{:S(2)}, u32[]{:S(2)}) collective-permute-start(bf16[4,32,512]{2,1,0:T(8,128)(2,1)S(1)} %get-tuple-element.46), channel_id=1, source_target_pairs={{0,1},{1,0},{2,3},{3,2},{4,5},{5,4},{6,7},{7,6},{8,9},{9,8},{10,11... | collective-permute-start | bytes 393224 | tf_op jit(solution)/shard_map/ppermute | solution.py:561
  87.7 6.5 %collective-permute-start.10 = (bf16[32,512]{1,0:T(8,128)(2,1)S(1)}, bf16[32,512]{1,0:T(8,128)(2,1)S(1)}, u32[]{:S(2)}, u32[]{:S(2)}) collective-permute-start(bf16[32,512]{1,0:T(8,128)(2,1)S(1)} %get-tuple-element.48), channel_id=1, source_target_pairs={{0,4},{1,5},{2,6},{3,7},{4,0},{5,1},{6,2},{7,3},{8,12},{9,13},{10,... | collective-permute-start | bytes 98312 | tf_op jit(solution)/shard_map/ppermute | solution.py:564
  91.0 5.1 %collective-permute-start.11 = (bf16[32,512]{1,0:T(8,128)(2,1)S(1)}, bf16[32,512]{1,0:T(8,128)(2,1)S(1)}, u32[]{:S(2)}, u32[]{:S(2)}) collective-permute-start(bf16[32,512]{1,0:T(8,128)(2,1)S(1)} %get-tuple-element.49), channel_id=1, source_target_pairs={{0,2},{1,3},{2,4},{3,5},{4,6},{5,7},{6,0},{7,1},{8,10},{9,11},{10,... | collective-permute-start | bytes 98312 | tf_op jit(solution)/shard_map/ppermute | solution.py:564
  91.7 4.5 %collective-permute-start.12 = (bf16[32,512]{1,0:T(8,128)(2,1)S(1)}, bf16[32,512]{1,0:T(8,128)(2,1)S(1)}, u32[]{:S(2)}, u32[]{:S(2)}) collective-permute-start(bf16[32,512]{1,0:T(8,128)(2,1)S(1)} %get-tuple-element.50), channel_id=1, source_target_pairs={{0,6},{1,7},{2,0},{3,1},{4,2},{5,3},{6,4},{7,5},{8,14},{9,15},{10,... | collective-permute-start | bytes 98312 | tf_op jit(solution)/shard_map/ppermute | solution.py:564
